TPU v7x, 32 devices: a whole 2x2x4 slice. The times are simulated.
32 devices in a mesh: dp: 16 (over z, x, core), mem: 2 (over y).
Axes of the slice: x: 2, y: 2, z: 4, core: 2. Of those that a mesh axis runs over, the one named last changes fastest.
Arguments:
- target: bfloat16 [16384, 512], P(('dp', 'mem')), may hold values from -6 to 6
- memory: bfloat16 [128, 512, 512], P('dp', 'mem'), may hold values from -6 to 6
- grad_out: bfloat16 [16384, 512], P(('dp', 'mem')), may hold values from -6 to 6
- tgt_len: int32 [32, 4], P('dp'), may hold values from 1 to 256, 512 in all within a row
- src_len: int32 [32, 4], P('dp'), may hold values from 1 to 512, as said below
- w_qkv: bfloat16 [512, 1536], replicated, may hold values from -0.375 to 0.375
- w_out: bfloat16 [512, 512], replicated, may hold values from -0.75 to 0.75
- wq_cross: bfloat16 [512, 512], replicated, may hold values from -0.375 to 0.375
- wkv_cross: bfloat16 [512, 1024], replicated, may hold values from -0.375 to 0.375
- wo_cross: bfloat16 [512, 512], replicated, may hold values from -0.75 to 0.75
- w_up: bfloat16 [512, 2048], replicated, may hold values from -0.25 to 0.25
- w_down: bfloat16 [2048, 512], replicated, may hold values from -0.125 to 0.125
- ln_gain: float32 [3, 512], replicated, may hold values from 0.5 to 1.5
- ln_bias: float32 [3, 512], replicated, may hold values from -2 to 2
Outputs:
- out: bfloat16 [16384, 512], P(('dp', 'mem'))
- grad_target: bfloat16 [16384, 512], P(('dp', 'mem'))
- grad_memory: bfloat16 [128, 512, 512], P('dp', 'mem')
- grad_w_qkv: float32 [512, 1536], replicated
- grad_w_out: float32 [512, 512], replicated
- grad_wq_cross: float32 [512, 512], replicated
- grad_wkv_cross: float32 [512, 1024], replicated
- grad_wo_cross: float32 [512, 512], replicated
- grad_w_up: float32 [512, 2048], replicated
- grad_w_down: float32 [2048, 512], replicated
- grad_ln_gain: float32 [3, 512], replicated
- grad_ln_bias: float32 [3, 512], replicated
Inputs may be any that keep to these rules, and one draw needn't show every extreme that they name: `tgt_len`: each row of 4 lengths sums to 512, and its longest is exactly 256. `src_len`: in each group of 2 rows along dp, some sentence has exactly 512 source positions.
All inputs are finite; a program needn't handle non-finite values.
Results may differ from a plain program's by a relative error of at most 0.025.
The roundings to bfloat16 on the way count: a program that leaves them out, or rounds other values in their place, can miss the bound.
Values may be sent and summed in bfloat16 or wider, within the bound.
No kernel may reach another device: no remote copies, remote signals or barrier semaphores. Data moves between devices by JAX's collectives and lax.ppermute only.
A program may use at most 128 MiB of HBM per device.

v0:
```python
import functools
import math

import jax
import jax.numpy as jnp
from jax import lax
from jax.experimental import pallas as pl
from jax.experimental.pallas import tpu as pltpu
from jax.sharding import PartitionSpec as P

HEADS = 8
PAIRS = HEADS // 2
SLAB = 128
SIDE = SLAB // 2
TILE = 128
MASKED = -1e30
EPSILON = 1e-05
F32 = jnp.float32
BF16 = jnp.bfloat16
MIB = 1024 * 1024
LN_ROWS = 16
LAST_PARTS = 2


def dot(left, right):
    return jnp.dot(left, right, preferred_element_type=F32)


def dot_nt(left, right):
    return lax.dot_general(left, right, (((1,), (1,)), ((), ())), preferred_element_type=F32)


def dot_tn(left, right):
    return lax.dot_general(left, right, (((0,), (0,)), ((), ())), preferred_element_type=F32)


def iota(shape, axis):
    return lax.broadcasted_iota(jnp.int32, shape, axis)


def norm_parts(hidden):
    centre = hidden - jnp.mean(hidden, axis=-1, keepdims=True)
    inverse = lax.rsqrt(jnp.mean(centre * centre, axis=-1, keepdims=True) + EPSILON)
    return centre * inverse, inverse


def norm_backward(upstream, unit, inverse, gain_row):
    scaled = upstream * gain_row
    shifted = (
        scaled
        - jnp.mean(scaled, axis=-1, keepdims=True)
        - unit * jnp.mean(scaled * unit, axis=-1, keepdims=True)
    )
    gain_grad = jnp.sum(upstream * unit, axis=0, keepdims=True)
    return inverse * shifted, gain_grad, jnp.sum(upstream, axis=0, keepdims=True)


def sentence_order(me, len_ref):
    count = len_ref.shape[1]
    lengths = [len_ref[me, k] for k in range(count)]
    longest, best, start, running = jnp.int32(0), lengths[0], jnp.int32(0), jnp.int32(0)
    for k in range(1, count):
        running = running + lengths[k - 1]
        more = lengths[k] > best
        longest = jnp.where(more, k, longest)
        start = jnp.where(more, running, start)
        best = jnp.where(more, lengths[k], best)
    order = [longest] + [jnp.where(k < longest, k, k + 1) for k in range(count - 1)]
    bounds = [jnp.int32(0)]
    for k in range(1, count):
        bounds.append(bounds[-1] + len_ref[me, order[k]])
    return order, start, bounds


def moved_rows(index, start, half):
    return jnp.where(index < start, index + half, jnp.where(index < start + half, index - start, index))


def sort_matrix(rows, start):
    spot = moved_rows(iota((rows, rows), 1), start, rows // 2)
    return jnp.where(spot == iota((rows, rows), 0), 1.0, 0.0).astype(BF16)


def unsort_matrix(rows, start):
    spot = moved_rows(iota((rows, rows), 0), start, rows // 2)
    return jnp.where(spot == iota((rows, rows), 1), 1.0, 0.0).astype(BF16)


def side_masks(width):
    side = iota((1, width), 1) % SLAB
    first = jnp.where(side < SLAB // 2, 1.0, 0.0)
    return first.astype(BF16), (1.0 - first).astype(BF16)


def each_pair(step):
    def advance(pair, carry):
        step(pair)
        return carry

    lax.fori_loop(0, PAIRS, advance, 0)


def slab_of(pair, first=0):
    if isinstance(pair, int):
        return pl.ds(first + pair * SLAB, SLAB)
    return pl.ds(pl.multiple_of(first + pair * SLAB, SLAB), SLAB)


def pack_heads(out_ref, rows, width):
    even, odd = side_masks(width)
    for t in range(out_ref.shape[0]):
        tile = rows(t * TILE, TILE)
        out_ref[t, :TILE, :] = tile * even
        out_ref[t, TILE:, :] = tile * odd


def fill_self_bias(bias_ref, bounds, half):
    for t in range(bias_ref.shape[0]):
        block, inner = t // (half // TILE), t % (half // TILE)
        key = iota((half, 2 * TILE), 0)
        query = iota((half, 2 * TILE), 1) % TILE + inner * TILE
        allowed = key <= query
        if block == 1:
            first = jnp.zeros((half, 2 * TILE), jnp.int32)
            for bound in bounds[1:-1]:
                first = jnp.where(query >= bound, bound, first)
            allowed = allowed & (key >= first)
        bias_ref[t] = jnp.where(allowed, 0.0, MASKED)


def self_keys(t, half):
    per = half // TILE
    return (t // per) * half, (t % per + 1) * TILE


def fill_live_bias(bias_ref, me, groups, parts, span, src_ref, sentences):
    key = iota((span, bias_ref.shape[2]), 0)
    for j, sentence in enumerate(sentences):
        for i, part in enumerate(parts):
            place = lax.rem(me - part + groups, groups) * span + key
            live = place < src_ref[me, sentence]
            bias_ref[j, pl.ds(i * span, span), :] = jnp.where(live, 0.0, MASKED)


def cross_units(bounds, half):
    units = [(t, 0, None) for t in range(half // TILE)]
    middle = half // 2
    last = jnp.int32(1)
    for bound in bounds[1:-1]:
        last = last + jnp.where(bound < middle, 1, 0)
    ends = bounds[1:]
    column = iota((1, 2 * TILE), 1) % TILE
    for u in range(len(ends) + 1):
        early = u < last
        sentence = jnp.where(early, u + 1, u)
        tile = jnp.where(early, 0, 1)
        low, high = jnp.int32(0), ends[0]
        for k in range(1, len(ends)):
            low = jnp.where(sentence == k + 1, ends[k - 1], low)
            high = jnp.where(sentence == k + 1, ends[k], high)
        row = column + tile * TILE
        units.append((tile + half // TILE, sentence, (row >= low) & (row < high)))
    return units


def own_sides(both):
    return jnp.concatenate([both[:SIDE, :TILE], both[SIDE:, TILE:]], axis=0)


def side_rows(row):
    even = jnp.broadcast_to(row[:, :TILE], (SIDE, TILE))
    return jnp.concatenate([even, jnp.broadcast_to(row[:, TILE:], (SIDE, TILE))], axis=0)


def tile_columns(tile):
    if isinstance(tile, int):
        return pl.ds(tile * TILE, TILE)
    return pl.ds(pl.multiple_of(tile * TILE, TILE), TILE)


def self_forward_kernel(
    groups,
    me_ref,
    len_ref,
    src_ref,
    target_ref,
    w_qkv_ref,
    w_out_ref,
    wq_ref,
    gain_ref,
    bias_row_ref,
    memory_ref,
    wkv_ref,
    sorted_ref,
    qkv_ref,
    norm_ref,
    attn_t_ref,
    hidden_ref,
    query_ref,
    part_ref,
    top_ref,
    sum_ref,
    pair_out_ref,
    bias_ref,
    live_ref,
    q_pack_ref,
    value_t_ref,
    cross_value_t_ref,
    pair_ref,
    copy_sem,
):
    rows, width = target_ref.shape
    half = rows // 2
    me = me_ref[0]
    order, start, bounds = sentence_order(me, len_ref)
    count, span = pair_ref.shape[0], pair_ref.shape[1]
    copies = []
    for j in range(count):
        block = memory_ref[me * count + order[j]]
        pair_ref[j] = dot(block, wkv_ref[...]).astype(BF16)
        copy = pltpu.make_async_copy(
            pair_ref.at[j], pair_out_ref.at[j, pl.ds(0, span), :], copy_sem.at[j]
        )
        copy.start()
        copies.append(copy)
    sorted_rows = dot(sort_matrix(rows, start), target_ref[...]).astype(BF16)
    sorted_ref[...] = sorted_rows
    fill_self_bias(bias_ref, bounds, half)
    queries = (dot(sorted_rows, w_qkv_ref[:, :width]).astype(BF16) * 0.125).astype(BF16)
    qkv_ref[:, :width] = queries
    pack_heads(q_pack_ref, lambda first, size: queries[first : first + size], width)
    qkv_ref[:, width : 2 * width] = dot(sorted_rows, w_qkv_ref[:, width : 2 * width]).astype(BF16)
    values = dot(sorted_rows, w_qkv_ref[:, 2 * width :]).astype(BF16)
    qkv_ref[:, 2 * width :] = values
    value_t_ref[...] = values.T
    tiles = rows // TILE

    def self_step(pair):
        slab = slab_of(pair)
        for t in range(tiles):
            first, size = self_keys(t, half)
            keys = qkv_ref[pl.ds(first, size), slab_of(pair, width)]
            scores = dot_nt(keys, q_pack_ref[t, :, slab]) + bias_ref[t, :size, :]
            top = jnp.max(scores, axis=0, keepdims=True)
            weights = jnp.exp(scores - top)
            total = jnp.sum(weights, axis=0, keepdims=True)
            probs = (weights * (1.0 / total)).astype(BF16)
            both = dot(value_t_ref[slab, pl.ds(first, size)], probs)
            attn_t_ref[slab, tile_columns(t)] = own_sides(both).astype(BF16)
            norm_ref[pl.ds(pair * tiles + t, 1), :] = top + jnp.log(total)

    each_pair(self_step)
    hidden = sorted_rows.astype(F32) + dot(attn_t_ref[...].T, w_out_ref[...])
    hidden_ref[...] = hidden
    unit, _ = norm_parts(hidden)
    normed = (unit * gain_ref[0:1] + bias_row_ref[0:1]).astype(BF16)
    query_ref[...] = (dot(normed, wq_ref[...]).astype(BF16) * 0.125).astype(BF16)

    pack_heads(q_pack_ref, lambda first, size: query_ref[first : first + size, :], width)
    fill_live_bias(live_ref, me, groups, [0], span, src_ref, order)
    for j in range(count):
        cross_value_t_ref[j] = pair_ref[j, :, width:].T
    units = cross_units(bounds, half)

    def cross_step(pair):
        slab = slab_of(pair)
        for tile, sentence, columns in units:
            scores = dot_nt(pair_ref[sentence, :, slab], q_pack_ref[tile, :, slab]) + live_ref[sentence]
            top = jnp.max(scores, axis=0, keepdims=True)
            weights = jnp.exp(scores - top)
            total = jnp.sum(weights, axis=0, keepdims=True)
            result = own_sides(dot(cross_value_t_ref[sentence, slab, :], weights.astype(BF16)))
            here = tile_columns(tile)
            row = pl.ds(pair * tiles + tile, 1)
            if columns is not None:
                result = jnp.where(columns[:, :TILE], result, part_ref[slab, here])
                top = jnp.where(columns, top, top_ref[row, :])
                total = jnp.where(columns, total, sum_ref[row, :])
            part_ref[slab, here] = result
            top_ref[row, :] = top
            sum_ref[row, :] = total

    part_ref[...] = jnp.zeros_like(part_ref)
    top_ref[...] = jnp.zeros_like(top_ref)
    sum_ref[...] = jnp.ones_like(sum_ref)
    each_pair(cross_step)
    for copy in copies:
        copy.wait()


def middle_kernel(
    groups,
    me_ref,
    len_ref,
    src_ref,
    hidden_one_ref,
    query_ref,
    part_ref,
    top_ref,
    sum_ref,
    wkv_ref,
    gain_ref,
    bias_row_ref,
    wo_hbm,
    w_up_hbm,
    w_down_hbm,
    grad_out_hbm,
    pair_in_hbm,
    *refs,
):
    came_refs = refs[: groups - 1]
    (
        out_ref,
        norm_ref,
        along_ref,
        keep_hbm,
        send_hbm,
        grad_hidden_ref,
        grad_attn_ref,
        ln_ref,
        pair_hbm,
        wo_ref,
        w_up_ref,
        w_down_ref,
        grad_out_ref,
        pair_ref,
        halves_ref,
        live_ref,
        q_pack_ref,
        value_t_ref,
        attn_t_ref,
        active_ref,
        slope_ref,
        grad_upper_ref,
        load_sem,
        pair_sem,
        store_sem,
    ) = refs[groups - 1 :]
    rows, width = hidden_one_ref.shape
    half = rows // 2
    me = me_ref[0]
    count, away = pair_ref.shape[0], pair_ref.shape[1]
    span = away // (groups - 1)
    loads = [
        pltpu.make_async_copy(source, there, load_sem.at[i])
        for i, (source, there) in enumerate(
            [(wo_hbm, wo_ref), (w_up_hbm, w_up_ref), (w_down_hbm, w_down_ref), (grad_out_hbm, grad_out_ref)]
        )
    ]
    for copy in loads:
        copy.start()
    order, start, bounds = sentence_order(me, len_ref)
    fill_live_bias(live_ref, me, groups, list(range(1, groups)), span, src_ref, order)
    pack_heads(q_pack_ref, lambda first, size: query_ref[first : first + size, :], width)
    pair_copies = []
    for j in range(count):
        for part in range(1, groups):
            block = came_refs[part - 1][order[j]]
            pair_ref[j, pl.ds((part - 1) * span, span), :] = dot(block, wkv_ref[...]).astype(BF16)
        value_t_ref[j] = pair_ref[j, :, width:].T
        copy = pltpu.make_async_copy(pair_ref.at[j], pair_hbm.at[j, pl.ds(span, away), :], pair_sem.at[j])
        copy.start()
        pair_copies.append(copy)
    units = cross_units(bounds, half)
    tiles = rows // TILE

    def cross_step(pair):
        slab = slab_of(pair)
        for tile, sentence, columns in units:
            here = tile_columns(tile)
            row = pl.ds(pair * tiles + tile, 1)
            scores = dot_nt(pair_ref[sentence, :, slab], q_pack_ref[tile, :, slab]) + live_ref[sentence]
            before = top_ref[row, :]
            top = jnp.maximum(jnp.max(scores, axis=0, keepdims=True), before)
            weights = jnp.exp(scores - top)
            scale = jnp.exp(before - top)
            total = jnp.sum(weights, axis=0, keepdims=True) + sum_ref[row, :] * scale
            result = own_sides(dot(value_t_ref[sentence, slab, :], weights.astype(BF16)))
            result = (result + part_ref[slab, here] * side_rows(scale)) * side_rows(1.0 / total)
            norm = top + jnp.log(total)
            if columns is not None:
                result = jnp.where(columns[:, :TILE], result, attn_t_ref[slab, here])
                norm = jnp.where(columns, norm, norm_ref[row, :])
            attn_t_ref[slab, here] = result
            norm_ref[row, :] = norm

    attn_t_ref[...] = jnp.zeros_like(attn_t_ref)
    norm_ref[...] = jnp.zeros_like(norm_ref)
    each_pair(cross_step)
    attn_t_low = attn_t_ref[...].astype(BF16)
    loads[0].wait()
    unit_one, _ = norm_parts(hidden_one_ref[...])
    normed_one = unit_one * gain_ref[0:1] + bias_row_ref[0:1]
    hidden_two = normed_one + dot(attn_t_low.T, wo_ref[...])
    unit_two, inverse_two = norm_parts(hidden_two)
    normed_two = unit_two * gain_ref[1:2] + bias_row_ref[1:2]
    normed_two_low = normed_two.astype(BF16)
    chunk = width
    chunks = w_down_ref.shape[0] // chunk
    loads[1].wait()
    loads[2].wait()

    def up_step(c, carry):
        cols = pl.ds(pl.multiple_of(c * chunk, chunk), chunk)
        upper = dot(normed_two_low, w_up_ref[:, cols])
        sigma = 0.5 * jnp.tanh(0.5 * upper) + 0.5
        active = (upper * sigma).astype(BF16)
        active_ref[:, cols] = active
        slope_ref[:, cols] = sigma * (1.0 + upper * (1.0 - sigma))
        return carry

    lax.fori_loop(0, chunks, up_step, 0)

    unit_three, inverse_three = norm_parts(normed_two + dot(active_ref[...], w_down_ref[...]))
    result = (unit_three * gain_ref[2:3] + bias_row_ref[2:3]).astype(BF16)
    out_ref[...] = dot(unsort_matrix(rows, start), result).astype(BF16)
    loads[3].wait()
    upstream = dot(sort_matrix(rows, start), grad_out_ref[...])
    grad_three, gain_three, bias_three = norm_backward(upstream, unit_three, inverse_three, gain_ref[2:3])
    grad_down = grad_three.astype(BF16)
    normed_two_t = normed_two_low.T

    def down_step(c, carry):
        cols = pl.ds(pl.multiple_of(c * chunk, chunk), chunk)
        grad_upper = (dot_nt(grad_down, w_down_ref[cols, :]) * slope_ref[:, cols]).astype(BF16)
        down_part = dot_tn(active_ref[:, cols], grad_down).astype(BF16)
        up_part = dot(normed_two_t, grad_upper).astype(BF16)
        half_index, here = c // (chunks // 2), lax.rem(c, chunks // 2)
        down_rows = pl.ds(pl.multiple_of(here * chunk, chunk), chunk)
        up_rows = pl.ds(pl.multiple_of((chunks // 2 + here) * chunk, chunk), chunk)
        halves_ref[half_index, down_rows, :] = down_part
        halves_ref[half_index, up_rows, :] = up_part
        grad_upper_ref[:, cols] = grad_upper
        return carry

    lax.fori_loop(0, chunks, down_step, 0)

    most = chunks * chunk
    core = me_ref[1]
    stores = [
        pltpu.make_async_copy(
            halves_ref.at[half_index, pl.ds(first, size)], there.at[pl.ds(first, size)], store_sem.at[i]
        )
        for i, (half_index, there, first, size) in enumerate(
            [
                (1 - core, send_hbm, 0, most),
                (core, keep_hbm, 0, most),
                (1 - core, send_hbm, most, halves_ref.shape[1] - most),
                (core, keep_hbm, most, halves_ref.shape[1] - most),
            ]
        )
    ]
    stores[0].start()
    stores[1].start()
    upstream_two = grad_three + dot_nt(grad_upper_ref[...], w_up_ref[...])
    grad_two, gain_two, bias_two = norm_backward(upstream_two, unit_two, inverse_two, gain_ref[1:2])
    grad_two_low = grad_two.astype(BF16)
    wo_grad = dot(attn_t_low, grad_two_low).astype(BF16)
    used = most + width // 2
    for half_index in range(2):
        piece = wo_grad[half_index * (width // 2) : (half_index + 1) * (width // 2)]
        halves_ref[half_index, pl.ds(most, width // 2), :] = piece
        if halves_ref.shape[1] > used:
            halves_ref[half_index, used:, :] = jnp.zeros((halves_ref.shape[1] - used, width), BF16)
    stores[2].start()
    stores[3].start()
    grad_hidden_ref[...] = grad_two
    grad_attn = dot_nt(grad_two_low, wo_ref[...]).astype(BF16)
    grad_attn_ref[...] = grad_attn
    product = grad_attn.T.astype(F32) * attn_t_ref[...]
    for pair in range(PAIRS):
        for side in range(2):
            first = pair * SLAB + side * SIDE
            along = jnp.sum(product[first : first + SIDE], axis=0, keepdims=True)
            for t in range(tiles):
                along_ref[pair * tiles + t : pair * tiles + t + 1, side * TILE : (side + 1) * TILE] = along[
                    :, t * TILE : (t + 1) * TILE
                ]
    ln_ref[...] = jnp.concatenate([gain_two, gain_three, bias_two, bias_three], axis=0)
    for copy in pair_copies + stores:
        copy.wait()


def cross_backward_kernel(
    groups,
    block,
    me_ref,
    len_ref,
    src_ref,
    query_ref,
    norm_ref,
    along_ref,
    grad_attn_ref,
    pair_hbm,
    pair_grad_ref,
    query_grad_t_ref,
    pair_ref,
    live_ref,
    q_pack_ref,
    g_pack_ref,
    key_t_ref,
    query_sum_ref,
    sum_ref,
    load_sem,
):
    rows, width = query_ref.shape
    half = rows // 2
    me = me_ref[0]
    sentences, places = pair_ref.shape[0], pair_ref.shape[1]
    first_sentence = 0 if block == 0 else 1
    load = pltpu.make_async_copy(pair_hbm.at[pl.ds(first_sentence, sentences)], pair_ref, load_sem.at[0])
    load.start()
    order, start, bounds = sentence_order(me, len_ref)
    mine = order[:1] if block == 0 else order[1:]
    fill_live_bias(live_ref, me, groups, list(range(groups)), places // groups, src_ref, mine)
    low = block * half
    pack_heads(q_pack_ref, lambda first, size: query_ref[low + first : low + first + size, :], width)
    pack_heads(g_pack_ref, lambda first, size: grad_attn_ref[low + first : low + first + size, :], width)
    tiles, per = rows // TILE, half // TILE
    units = cross_units(bounds, half)
    units = units[:per] if block == 0 else units[per:]
    load.wait()
    for j in range(sentences):
        key_t_ref[j] = pair_ref[j, :, :width].T

    def pair_step(pair):
        slab, value_slab = slab_of(pair), slab_of(pair, width)
        query_sum_ref[...] = jnp.zeros_like(query_sum_ref)
        sum_ref[...] = jnp.zeros_like(sum_ref)
        for tile, sentence, columns in units:
            j = sentence - first_sentence
            t = tile - block * per
            here = tile_columns(t)
            row = pl.ds(pair * tiles + tile, 1)
            q_rows, g_rows = q_pack_ref[t, :, slab], g_pack_ref[t, :, slab]
            norm = norm_ref[row, :]
            if columns is not None:
                norm = jnp.where(columns, norm, -MASKED)
            scores = dot_nt(pair_ref[j, :, slab], q_rows) + live_ref[j]
            probs = jnp.exp(scores - norm)
            grad_probs = dot_nt(pair_ref[j, :, value_slab], g_rows)
            grad_scores = (probs * (grad_probs - along_ref[row, :])).astype(BF16)
            sum_ref[j, :, :SLAB] += dot(grad_scores, q_rows)
            sum_ref[j, :, SLAB:] += dot(probs.astype(BF16), g_rows)
            query_sum_ref[:, here] += own_sides(dot(key_t_ref[j, slab, :], grad_scores))
        query_grad_t_ref[slab, :] = (query_sum_ref[...] * 0.125).astype(BF16)
        pair_grad_ref[:, :, slab] = sum_ref[:, :, :SLAB].astype(BF16)
        pair_grad_ref[:, :, value_slab] = sum_ref[:, :, SLAB:].astype(BF16)

    for pair in range(PAIRS):
        pair_step(pair)


def memory_weight_kernel(groups, me_ref, len_ref, pair_grad_long_ref, pair_grad_rest_ref, memory_ref, *refs):
    came_refs = refs[: groups - 1]
    wkv_grad_ref, total_ref = refs[groups - 1 :]
    width = memory_ref.shape[2]
    me = me_ref[0]
    count = len_ref.shape[1]
    span = pair_grad_long_ref.shape[1] // groups
    order, _, _ = sentence_order(me, len_ref)
    for j in range(count):
        pair_grad_ref, here = (pair_grad_long_ref, 0) if j == 0 else (pair_grad_rest_ref, j - 1)
        blocks = [memory_ref[me * count + order[j]]] + [ref[order[j]] for ref in came_refs]
        term = dot_tn(jnp.concatenate(blocks, axis=0), pair_grad_ref[here])
        if j == 0:
            total_ref[...] = term
        else:
            total_ref[...] += term
    wkv_grad_ref[0] = total_ref[:, :width].astype(BF16)
    wkv_grad_ref[1] = total_ref[:, width:].astype(BF16)


def memory_grad_kernel(pieces, me_ref, len_ref, pair_grad_long_ref, pair_grad_rest_ref, wkv_ref, *outs):
    count = len_ref.shape[1]
    order, _, _ = sentence_order(me_ref[0], len_ref)
    for j in range(count):
        pair_grad_ref, here = (pair_grad_long_ref, 0) if j == 0 else (pair_grad_rest_ref, j - 1)
        for (first, size), out in zip(pieces, outs):
            out[order[j]] = dot_nt(pair_grad_ref[here, pl.ds(first, size), :], wkv_ref[...]).astype(BF16)


def first_norm_backward_kernel(
    me_ref,
    hidden_one_ref,
    query_grad_t_long_ref,
    query_grad_t_rest_ref,
    grad_hidden_two_ref,
    wq_ref,
    w_out_ref,
    self_attn_t_ref,
    gain_ref,
    bias_row_ref,
    ln_in_ref,
    wkv_grad_ref,
    keep_ref,
    send_ref,
    grad_hidden_ref,
    grad_self_ref,
):
    width = wq_ref.shape[0]
    unit_one, inverse_one = norm_parts(hidden_one_ref[...])
    normed_one = (unit_one * gain_ref[0:1] + bias_row_ref[0:1]).astype(BF16)
    query_grad = jnp.concatenate([query_grad_t_long_ref[...].T, query_grad_t_rest_ref[...].T], axis=0)
    upstream = grad_hidden_two_ref[...] + dot_nt(query_grad, wq_ref[...])
    grad_one, gain_one, bias_one = norm_backward(upstream, unit_one, inverse_one, gain_ref[0:1])
    grad_hidden_ref[...] = grad_one
    grad_one_low = grad_one.astype(BF16)
    grad_self_ref[...] = dot_nt(grad_one_low, w_out_ref[...]).astype(BF16)
    wq_grad = dot_tn(normed_one, query_grad).astype(BF16)
    w_out_grad = dot(self_attn_t_ref[...], grad_one_low).astype(BF16)
    norms = jnp.concatenate(
        [gain_one, ln_in_ref[0:2], bias_one, ln_in_ref[2:4], jnp.zeros((LN_ROWS - 6, width), F32)], axis=0
    ).astype(BF16)

    def halves(low_ref, high_ref):
        low_ref[:width, :] = wq_grad
        low_ref[width : 2 * width, :] = wkv_grad_ref[0]
        high_ref[:width, :] = wkv_grad_ref[1]
        high_ref[width : 2 * width, :] = w_out_grad

    @pl.when(me_ref[1] == 0)
    def _():
        halves(keep_ref, send_ref)

    @pl.when(me_ref[1] != 0)
    def _():
        halves(send_ref, keep_ref)

    keep_ref[2 * width :, :] = norms
    send_ref[2 * width :, :] = norms


def self_backward_kernel(
    me_ref,
    len_ref,
    qkv_ref,
    norm_ref,
    grad_attn_ref,
    sorted_ref,
    grad_triple_ref,
    *refs,
):
    keep_refs, send_refs = refs[:LAST_PARTS], refs[LAST_PARTS : 2 * LAST_PARTS]
    self_backward(
        me_ref,
        len_ref,
        qkv_ref,
        norm_ref,
        grad_attn_ref,
        sorted_ref,
        grad_triple_ref,
        keep_refs,
        send_refs,
        *refs[2 * LAST_PARTS :],
    )


def self_backward(
    me_ref,
    len_ref,
    qkv_ref,
    norm_ref,
    grad_attn_ref,
    sorted_ref,
    grad_triple_ref,
    keep_refs,
    send_refs,
    bias_ref,
    q_pack_ref,
    g_pack_ref,
    key_t_ref,
    query_grad_t_ref,
):
    rows, width = sorted_ref.shape
    half = rows // 2
    _, _, bounds = sentence_order(me_ref[0], len_ref)
    fill_self_bias(bias_ref, bounds, half)
    pack_heads(q_pack_ref, lambda first, size: qkv_ref[first : first + size, :width], width)
    pack_heads(g_pack_ref, lambda first, size: grad_attn_ref[first : first + size, :], width)
    key_t_ref[...] = qkv_ref[:, width : 2 * width].T
    tiles, per = rows // TILE, half // TILE

    def pair_step(pair):
        slab, key_slab, value_slab = slab_of(pair), slab_of(pair, width), slab_of(pair, 2 * width)
        sums = [[None, None] for _ in range(tiles)]
        for t in range(tiles):
            first, size = self_keys(t, half)
            span = pl.ds(first, size)
            q_rows, g_rows = q_pack_ref[t, :, slab], g_pack_ref[t, :, slab]
            scores = dot_nt(qkv_ref[span, key_slab], q_rows) + bias_ref[t, :size, :]
            probs = jnp.exp(scores - norm_ref[pl.ds(pair * tiles + t, 1), :])
            grad_probs = dot_nt(qkv_ref[span, value_slab], g_rows)
            along = jnp.sum(probs * grad_probs, axis=0, keepdims=True)
            grad_scores = (probs * (grad_probs - along)).astype(BF16)
            parts = dot(grad_scores, q_rows), dot(probs.astype(BF16), g_rows)
            for i in range(size // TILE):
                spot = sums[first // TILE + i]
                for k in range(2):
                    piece = parts[k][i * TILE : (i + 1) * TILE]
                    spot[k] = piece if spot[k] is None else spot[k] + piece
            query_grad_t_ref[slab, tile_columns(t)] = (
                own_sides(dot(key_t_ref[slab, span], grad_scores)) * 0.125
            ).astype(BF16)
        for t in range(tiles):
            grad_triple_ref[pl.ds(t * TILE, TILE), key_slab] = sums[t][0].astype(BF16)
            grad_triple_ref[pl.ds(t * TILE, TILE), value_slab] = sums[t][1].astype(BF16)

    for pair in range(PAIRS):
        pair_step(pair)
    grad_triple_ref[:, :width] = query_grad_t_ref[...].T
    sorted_t = sorted_ref[...].T
    grads = [
        dot(sorted_t, grad_triple_ref[:, part * width : (part + 1) * width]).astype(BF16)
        for part in range(3)
    ]
    short = width // 2

    low = jnp.concatenate([grads[0], grads[1][:short]], axis=0)
    high = jnp.concatenate([grads[1][short:], grads[2]], axis=0)
    size = keep_refs[0].shape[0]

    def halves(low_refs, high_refs):
        for i in range(LAST_PARTS):
            low_refs[i][...] = low[i * size : (i + 1) * size]
            high_refs[i][...] = high[i * size : (i + 1) * size]

    @pl.when(me_ref[1] == 0)
    def _():
        halves(keep_refs, send_refs)

    @pl.when(me_ref[1] != 0)
    def _():
        halves(send_refs, keep_refs)


def target_kernel(me_ref, len_ref, grad_triple_ref, w_qkv_ref, grad_hidden_ref, grad_target_ref):
    rows = grad_hidden_ref.shape[0]
    _, start, _ = sentence_order(me_ref[0], len_ref)
    result = grad_hidden_ref[...] + dot_nt(grad_triple_ref[...], w_qkv_ref[...])
    grad_target_ref[...] = dot(unsort_matrix(rows, start), result.astype(BF16)).astype(BF16)


def tree_sum(terms):
    while len(terms) > 1:
        terms = [terms[i] + terms[i + 1] for i in range(0, len(terms), 2)]
    return terms[0]


def rows_of(ref, first, count):
    return ref[pl.ds(pl.multiple_of(first, 16), count), :].astype(F32)


def first_split_kernel(segments, ln, peers, spot_ref, *refs):
    ins, outs, sum_ref = refs[: 2 * segments], refs[2 * segments : -1], refs[-1]
    extra = LN_ROWS if ln else 0
    size = outs[0].shape[0] - extra
    used = 0
    for i in range(segments):
        keep_ref, came_ref = ins[2 * i], ins[2 * i + 1]
        count = keep_ref.shape[0] - (extra if i == 0 else 0)
        sum_ref[used : used + count, :] = (rows_of(keep_ref, 0, count) + rows_of(came_ref, 0, count)).astype(BF16)
        if i == 0 and ln:
            tail = (rows_of(keep_ref, count, LN_ROWS) + rows_of(came_ref, count, LN_ROWS)).astype(BF16)
        used += count
    if sum_ref.shape[0] > used:
        sum_ref[used:, :] = jnp.zeros((sum_ref.shape[0] - used, sum_ref.shape[1]), BF16)
    for d, out in enumerate(outs):
        out[:size, :] = sum_ref[pl.ds(pl.multiple_of((spot_ref[2] ^ d) * size, 16), size), :]
        if ln:
            out[size:, :] = tail


def split_kernel(stage, ln, peers, spot_ref, *refs):
    ins, outs = refs[:peers], refs[peers:]
    extra = LN_ROWS if ln else 0
    size = outs[0].shape[0] - extra
    if ln:
        tail = tree_sum([rows_of(ref, size * len(outs), LN_ROWS) for ref in ins]).astype(BF16)
    for d, out in enumerate(outs):
        first = (spot_ref[2 + stage] ^ d) * size
        out[:size, :] = tree_sum([rows_of(ref, first, size) for ref in ins]).astype(BF16)
        if ln:
            out[size:, :] = tail


def total_kernel(ln, count, *refs):
    ins, outs = refs[:count], refs[count:]
    size = outs[0].shape[0]
    outs[0][...] = tree_sum([rows_of(ref, 0, size) for ref in ins]).astype(BF16)
    if ln:
        outs[1][...] = tree_sum([rows_of(ref, size, LN_ROWS) for ref in ins])


def join_kernel(stage, spot_ref, *refs):
    out_ref = refs[-1]
    for d, ref in enumerate(refs[:-1]):
        size = ref.shape[0]
        out_ref[pl.ds(pl.multiple_of((spot_ref[2 + stage] ^ d) * size, 16), size), :] = ref[...]


def finish_kernel(offsets, peers, twisted, pieces, held, spot_ref, *refs):
    arrays, refs = refs[: 2 * len(offsets)], refs[2 * len(offsets) + held :]
    outs, (wide_ref, sem) = refs[:-2], refs[-2:]
    core = spot_ref[1]
    size, width = wide_ref.shape[1:]
    copies = []
    for k, ref in enumerate(arrays):
        wide_ref[k] = ref[...].astype(F32)
        d, other = offsets[k // 2], k % 2
        half = 1 - core if other else core
        place = spot_ref[3 if twisted and other else 2] ^ d
        for i in range(2):
            for j in range(peers):
                cut = []
                for piece_half, first, rows, out, row, col in pieces:
                    low, high = max(first, j * size), min(first + rows, (j + 1) * size)
                    if piece_half == i and low < high:
                        there = outs[out].at[pl.ds(row + low - first, high - low), pl.ds(col, width)]
                        here = wide_ref.at[k, pl.ds(low - j * size, high - low), :]
                        cut.append(pltpu.make_async_copy(here, there, sem.at[k, len(cut)]))
                copies.append(((half == i) & (place == j), cut))
                _start_all(*copies[-1])
    for chosen, cut in copies:
        _wait_all(chosen, cut)


def _start_all(chosen, cut):
    @pl.when(chosen)
    def _():
        for copy in cut:
            copy.start()


def _wait_all(chosen, cut):
    @pl.when(chosen)
    def _():
        for copy in cut:
            copy.wait()


class Summing:
    def __init__(self, rows, width, ln):
        self.width, self.ln = width, ln
        self.dp, self.mem = lax.axis_size("dp"), lax.axis_size("mem")
        z_size = 4
        x_size = self.dp // (2 * z_size)
        self.sizes = (x_size, self.mem, z_size)
        self.twisted = x_size == self.mem
        self.chunk = -(-rows // (16 * math.prod(self.sizes))) * 16
        self.rows = self.chunk * math.prod(self.sizes)

    def after(self, stage):
        return self.rows // math.prod(self.sizes[:stage])

    def axis(self, stage, core):
        return 1 - stage if self.twisted and core == 1 and stage < 2 else stage

    def coords(self, dp, mem):
        return [dp // 2 % self.sizes[0], mem, dp // (2 * self.sizes[0])], dp % 2

    def spot(self, me, dp):
        (x, mem, z), core = self.coords(dp, me)
        if self.twisted:
            x, mem = jnp.where(core == 0, x, mem), jnp.where(core == 0, mem, x)
        return jnp.stack([me, core, x, mem, z]).astype(jnp.int32)

    def permute(self, array, stage, offset):
        pairs = []
        for dp in range(self.dp):
            for mem in range(self.mem):
                spots, core = self.coords(dp, mem)
                if stage is None:
                    core ^= offset
                else:
                    spots[self.axis(stage, core)] ^= offset
                to_dp = (spots[2] * self.sizes[0] + spots[0]) * 2 + core
                pairs.append((dp * self.mem + mem, to_dp * self.mem + spots[1]))
        return lax.ppermute(array, ("dp", "mem"), pairs)

    def core_swap(self, send):
        return self.permute(send, None, 1)

    def swap(self, arrays, stage):
        return [arrays[0]] + [self.permute(array, stage, d) for d, array in enumerate(arrays) if d > 0]

    def spread(self, stage, array):
        return [array] + [self.permute(array, stage, d) for d in range(1, self.sizes[stage])]

    def messages(self, stage):
        size = self.after(stage + 1) + (LN_ROWS if self.ln else 0)
        return [((size, self.width), BF16)] * self.sizes[stage]

    def first_split(self, spot, *arrays):
        kernel = functools.partial(first_split_kernel, len(arrays) // 2, self.ln, self.sizes[0])
        return call(kernel, self.messages(0), [((self.rows, self.width), BF16)], 1, spot, *arrays, work=0.01)

    def split(self, stage, spot, arrays):
        kernel = functools.partial(split_kernel, stage, self.ln, self.sizes[stage - 1])
        return call(kernel, self.messages(stage), [], 1, spot, *arrays, work=0.01)

    def total(self, arrays):
        outs = [((self.chunk, self.width), BF16)]
        if self.ln:
            outs.append(((LN_ROWS, self.width), F32))
        return call(functools.partial(total_kernel, self.ln, self.sizes[2]), outs, [], 0, *arrays, work=0.01)

    def join(self, stage, spot, arrays):
        outs = [((self.after(stage), self.width), BF16)]
        return call(functools.partial(join_kernel, stage), outs, [], 1, spot, *arrays, work=0.01)[0]

    def finish(self, spot, mine, others, offsets, pieces, outs, held=()):
        kernel = functools.partial(finish_kernel, offsets, self.sizes[0], self.twisted, pieces, len(held))
        arrays = [array for d in offsets for array in (mine[d], others[d])]
        size = self.after(1)
        scratch = [((len(arrays), size, self.width), F32), pltpu.SemaphoreType.DMA((len(arrays), len(pieces)))]
        aliases = {1 + len(arrays) + i: i for i in range(len(held))}
        return call(
            kernel,
            outs,
            scratch,
            1,
            spot,
            *arrays,
            *held,
            work=1,
            vmem=40,
            hbm_in=len(held),
            hbm_out=len(outs),
            aliases=aliases,
        )


def call(kernel, outs, scratch, scalars, *arrays, work=0.5, vmem=0, hbm_in=0, hbm_out=0, aliases=None):
    plain = len(arrays) - scalars - hbm_in
    if not vmem:
        blocks = [(array.shape, array.dtype) for array in arrays[scalars:]] + outs
        blocks = blocks + [entry for entry in scratch if isinstance(entry, tuple)]
        vmem = max(16, sum(math.prod(shape) * jnp.dtype(kind).itemsize for shape, kind in blocks) // MIB + 7)
    specs = [pl.BlockSpec(memory_space=pltpu.SMEM)] * scalars
    specs = specs + [pl.BlockSpec(memory_space=pltpu.VMEM)] * plain
    specs = specs + [pl.BlockSpec(memory_space=pl.ANY)] * hbm_in
    out_specs = [pl.BlockSpec(memory_space=pltpu.VMEM)] * (len(outs) - hbm_out)
    out_specs = out_specs + [pl.BlockSpec(memory_space=pl.ANY)] * hbm_out
    return pl.pallas_call(
        kernel,
        out_shape=[jax.ShapeDtypeStruct(shape, kind) for shape, kind in outs],
        in_specs=specs,
        out_specs=out_specs,
        scratch_shapes=[pltpu.VMEM(*entry) if isinstance(entry, tuple) else entry for entry in scratch],
        input_output_aliases=aliases or {},
        compiler_params=pltpu.CompilerParams(vmem_limit_bytes=vmem * MIB),
        cost_estimate=pl.CostEstimate(flops=int(work * 1e9), bytes_accessed=int(work * 3e6), transcendentals=0),
    )(*arrays)


def middle(
    groups, first_sum, stats, spot, tgt_len, src_len, hidden_one, query, part, part_top, part_sum, wkv_cross,
    ln_gain, ln_bias, wo_cross, w_up, w_down, grad_out, pair_mine, came,
):
    rows, width = hidden_one.shape
    half, tiles = rows // 2, rows // TILE
    hidden_width = w_down.shape[0]
    count, places, _ = pair_mine.shape
    away = places // groups * (groups - 1)
    arrays = [spot, tgt_len, src_len, hidden_one, query, part, part_top, part_sum, wkv_cross, ln_gain, ln_bias]
    stay = [wo_cross, w_up, w_down, grad_out, pair_mine]

    def kernel(*refs):
        ins, refs = refs[: len(arrays)], refs[len(arrays) :]
        came_refs, refs = refs[: len(came)], refs[len(came) :]
        stay_refs, refs = refs[: len(stay)], refs[len(stay) :]
        outs, refs = refs[:9], refs[9:]
        middle_kernel(groups, *ins, *stay_refs, *came_refs, *outs[:3], *outs[6:8], *outs[3:6], outs[8], *refs)

    result_out, cross_norm, cross_along, grad_hidden_two, grad_attn, ln_part, keep_one, send_one, pair_all = call(
        kernel,
        [
            ((rows, width), BF16),
            (stats, F32),
            (stats, F32),
            ((rows, width), F32),
            ((rows, width), BF16),
            ((4, width), F32),
            ((first_sum.rows, width), BF16),
            ((first_sum.rows, width), BF16),
            ((count, places, 2 * width), BF16),
        ],
        [
            ((width, width), BF16),
            ((width, hidden_width), BF16),
            ((hidden_width, width), BF16),
            ((rows, width), BF16),
            ((count, away, 2 * width), BF16),
            ((2, first_sum.rows, width), BF16),
            ((count, away, 2 * TILE), F32),
            ((tiles, 2 * TILE, width), BF16),
            ((count, width, away), BF16),
            ((width, rows), F32),
            ((rows, hidden_width), BF16),
            ((rows, hidden_width), F32),
            ((rows, hidden_width), BF16),
            pltpu.SemaphoreType.DMA((4,)),
            pltpu.SemaphoreType.DMA((count,)),
            pltpu.SemaphoreType.DMA((4,)),
        ],
        3,
        *arrays,
        *came,
        *stay,
        vmem=60,
        hbm_in=len(stay),
        hbm_out=3,
        aliases={len(arrays) + len(came) + len(stay) - 1: 8},
    )
    return result_out, cross_norm, cross_along, keep_one, send_one, grad_hidden_two, grad_attn, ln_part, pair_all


def body(
    target,
    memory,
    grad_out,
    tgt_len,
    src_len,
    w_qkv,
    w_out,
    wq_cross,
    wkv_cross,
    wo_cross,
    w_up,
    w_down,
    ln_gain,
    ln_bias,
):
    rows, width = target.shape
    half = rows // 2
    tiles = rows // TILE
    hidden_width = w_down.shape[0]
    groups = lax.axis_size("mem")
    me = lax.axis_index("mem")
    count = tgt_len.shape[1]
    span = memory.shape[1]
    places, away = groups * span, (groups - 1) * span
    dp = lax.axis_index("dp")
    short = width // 2
    first_sum = Summing(hidden_width + short, width, False)
    second_sum = Summing(3 * width + short, width, True)
    spot = first_sum.spot(me, dp)
    stats = (PAIRS * tiles, 2 * TILE)

    came = []
    for shift in range(1, groups):
        pairs = [(i, (i + shift) % groups) for i in range(groups)]
        sent = lax.dynamic_slice_in_dim(memory, ((me + shift) % groups) * count, count, 0)
        came.append(lax.ppermute(sent, "mem", pairs))

    sorted_rows, qkv, self_norm, self_attn_t, hidden_one, query, part, part_top, part_sum, pair_mine = call(
        functools.partial(self_forward_kernel, groups),
        [
            ((rows, width), BF16),
            ((rows, 3 * width), BF16),
            (stats, F32),
            ((width, rows), BF16),
            ((rows, width), F32),
            ((rows, width), BF16),
            ((width, rows), F32),
            (stats, F32),
            (stats, F32),
            ((count, places, 2 * width), BF16),
        ],
        [
            ((tiles, half, 2 * TILE), F32),
            ((count, span, 2 * TILE), F32),
            ((tiles, 2 * TILE, width), BF16),
            ((width, rows), BF16),
            ((count, width, span), BF16),
            ((count, span, 2 * width), BF16),
            pltpu.SemaphoreType.DMA((count,)),
        ],
        3,
        spot,
        tgt_len,
        src_len,
        target,
        w_qkv,
        w_out,
        wq_cross,
        ln_gain,
        ln_bias,
        memory,
        wkv_cross,
        vmem=60,
        hbm_out=1,
    )
    result_out, cross_norm, cross_along, keep_one, send_one, grad_hidden_two, grad_attn, ln_part, pair_all = middle(
        groups, first_sum, stats, spot, tgt_len, src_len, hidden_one, query, part, part_top, part_sum, wkv_cross,
        ln_gain, ln_bias, wo_cross, w_up, w_down, grad_out, pair_mine, came,
    )
    came_one = first_sum.core_swap(send_one)

    def cross_backward(block):
        sentences = 1 if block == 0 else count - 1
        return call(
            functools.partial(cross_backward_kernel, groups, block),
            [((sentences, places, 2 * width), BF16), ((width, half), BF16)],
            [
                ((sentences, places, 2 * width), BF16),
                ((sentences, places, 2 * TILE), F32),
                ((half // TILE, 2 * TILE, width), BF16),
                ((half // TILE, 2 * TILE, width), BF16),
                ((sentences, width, places), BF16),
                ((SLAB, half), F32),
                ((sentences, places, 2 * SLAB), F32),
                pltpu.SemaphoreType.DMA((1,)),
            ],
            3,
            spot,
            tgt_len,
            src_len,
            query,
            cross_norm,
            cross_along,
            grad_attn,
            pair_all,
            work=10,
            vmem=58 if block == 0 else 32,
            hbm_in=1,
        )

    pair_grad_long, query_grad_t_long = cross_backward(0)
    came_one, pair_grad_long = lax.optimization_barrier((came_one, pair_grad_long))
    parts_one = first_sum.first_split(spot, keep_one, came_one)
    parts_one, pair_all = lax.optimization_barrier((parts_one, pair_all))
    parts_one = first_sum.swap(parts_one, 0)
    pair_grad_rest, query_grad_t_rest = cross_backward(1)
    (wkv_grad,) = call(
        functools.partial(memory_weight_kernel, groups),
        [((2, width, width), BF16)],
        [((width, 2 * width), F32)],
        2,
        spot,
        tgt_len,
        pair_grad_long,
        pair_grad_rest,
        memory,
        *came,
        work=1,
        vmem=32,
    )
    keep_mid, send_mid, grad_hidden_one, grad_self = call(
        first_norm_backward_kernel,
        [
            ((2 * width + LN_ROWS, width), BF16),
            ((2 * width + LN_ROWS, width), BF16),
            ((rows, width), F32),
            ((rows, width), BF16),
        ],
        [],
        1,
        spot,
        hidden_one,
        query_grad_t_long,
        query_grad_t_rest,
        grad_hidden_two,
        wq_cross,
        w_out,
        self_attn_t,
        ln_gain,
        ln_bias,
        ln_part,
        wkv_grad,
        work=0.1,
        vmem=24,
    )
    def memory_grad(pieces, pair_grad_long):
        return call(
            functools.partial(memory_grad_kernel, pieces),
            [((count, size, width), BF16) for _, size in pieces],
            [],
            2,
            spot,
            tgt_len,
            pair_grad_long,
            pair_grad_rest,
            wkv_cross,
            work=0.01,
            vmem=32,
        )

    def send_back(grads):
        return [
            lax.ppermute(array, "mem", [(k, (k - 1 - i) % groups) for k in range(groups)])
            for i, array in enumerate(grads)
        ]

    parts_one, grad_self = lax.optimization_barrier((parts_one, grad_self))
    parts_one = first_sum.split(1, spot, parts_one)
    parts_one, grad_self, pair_grad_long = lax.optimization_barrier((parts_one, grad_self, pair_grad_long))
    parts_one = first_sum.swap(parts_one, 1)
    grad_late = memory_grad(
        [(part * span + span // 2, span // 2) for part in range(1, groups)], pair_grad_long
    )
    backs_late = send_back(grad_late)
    grad_late, grad_self = lax.optimization_barrier((grad_late, grad_self))
    grad_triple, *last = call(
        self_backward_kernel,
        [((rows, 3 * width), BF16)] + [(((width + short) // LAST_PARTS, width), BF16)] * (2 * LAST_PARTS),
        [
            ((tiles, half, 2 * TILE), F32),
            ((tiles, 2 * TILE, width), BF16),
            ((tiles, 2 * TILE, width), BF16),
            ((width, rows), BF16),
            ((width, rows), BF16),
        ],
        2,
        spot,
        tgt_len,
        qkv,
        self_norm,
        grad_self,
        sorted_rows,
        work=0.1,
        vmem=28,
    )
    came_mid = second_sum.core_swap(send_mid)
    parts_one, last, came_mid, pair_grad_long = lax.optimization_barrier(
        (parts_one, last, came_mid, pair_grad_long)
    )
    keep_last = last[:LAST_PARTS]
    came_last = [second_sum.core_swap(part) for part in last[LAST_PARTS:]]
    parts_one = first_sum.split(2, spot, parts_one)
    came_mid, parts_one = lax.optimization_barrier((came_mid, parts_one))
    parts_two = second_sum.first_split(
        spot, keep_mid, came_mid, *[part for both in zip(keep_last, came_last) for part in both]
    )
    parts_one = first_sum.swap(parts_one, 2)
    parts_two, pair_grad_long, grad_triple = lax.optimization_barrier((parts_two, pair_grad_long, grad_triple))
    parts_two = second_sum.swap(parts_two, 0)
    grad_mine, *grad_away = memory_grad(
        [(0, span)] + [(part * span, span // 2) for part in range(1, groups)], pair_grad_long
    )
    backs_late, grad_triple = lax.optimization_barrier((backs_late, grad_triple))
    (grad_target,) = call(
        target_kernel,
        [((rows, width), BF16)],
        [],
        2,
        spot,
        tgt_len,
        grad_triple,
        w_qkv,
        grad_hidden_one,
        work=30,
        vmem=16,
    )
    parts_one, parts_two, grad_away, grad_target = lax.optimization_barrier(
        (parts_one, parts_two, grad_away, grad_target)
    )
    backs_early = send_back(grad_away)
    parts_two = second_sum.swap(second_sum.split(1, spot, parts_two), 1)
    spread_one = first_sum.spread(2, first_sum.total(parts_one)[0])
    parts_two, spread_one, backs_early = lax.optimization_barrier((parts_two, spread_one, backs_early))
    spread_one = first_sum.spread(1, first_sum.join(2, spot, spread_one))
    parts_two = second_sum.swap(second_sum.split(2, spot, parts_two), 2)
    parts_two, spread_one = lax.optimization_barrier((parts_two, spread_one))
    spread_one = first_sum.spread(0, first_sum.join(1, spot, spread_one))
    sum_two, norm_sums = second_sum.total(parts_two)
    spread_two = second_sum.spread(2, sum_two)
    spread_two = second_sum.spread(1, second_sum.join(2, spot, spread_two))
    joined_two = second_sum.join(1, spot, spread_two)
    spread_one, joined_two = lax.optimization_barrier((spread_one, joined_two))
    other_one = [first_sum.core_swap(array) for array in spread_one]
    chunks = hidden_width // width
    pieces = []
    for chunk in range(chunks):
        side, here = chunk // (chunks // 2), chunk % (chunks // 2)
        pieces.append((side, here * width, width, 0, chunk * width, 0))
        pieces.append((side, (chunks // 2 + here) * width, width, 1, 0, chunk * width))
    for side in range(2):
        pieces.append((side, chunks * width, short, 2, side * short, 0))
    grad_w_down, grad_w_up, grad_wo = first_sum.finish(
        spot,
        spread_one,
        other_one,
        list(range(len(spread_one))),
        pieces,
        [((hidden_width, width), F32), ((width, hidden_width), F32), ((width, width), F32)],
    )
    spread_two = second_sum.spread(0, joined_two)
    pieces = [
        (0, 0, width, 0, 0, 0),
        (0, width, width, 1, 0, 0),
        (0, 2 * width, width, 2, 0, 0),
        (0, 3 * width, short, 2, 0, width),
        (1, 0, width, 1, 0, width),
        (1, width, width, 3, 0, 0),
        (1, 2 * width, short, 2, short, width),
        (1, 2 * width + short, width, 2, 0, 2 * width),
    ]
    outs = [
        ((width, width), F32),
        ((width, 2 * width), F32),
        ((width, 3 * width), F32),
        ((width, width), F32),
    ]
    other_two = [second_sum.core_swap(spread_two[0])]
    own_two, grad_w_down = lax.optimization_barrier((spread_two[0], grad_w_down))
    held = second_sum.finish(spot, [own_two], other_two, [0], pieces, outs)
    spread_two, held = lax.optimization_barrier((spread_two, held))
    other_two = other_two + [second_sum.core_swap(array) for array in spread_two[1:]]
    grad_wq, grad_wkv, grad_w_qkv, grad_w_out = second_sum.finish(
        spot, spread_two, other_two, list(range(1, len(spread_two))), pieces, outs, held
    )
    grad_memory = jnp.zeros(memory.shape, BF16)
    grad_memory = lax.dynamic_update_slice(grad_memory, grad_mine, (me * count, 0, 0))
    for part, backs in enumerate((backs_early, backs_late)):
        for i, grads in enumerate(backs):
            owner = (me + i + 1) % groups
            grad_memory = lax.dynamic_update_slice(grad_memory, grads, (owner * count, part * (span // 2), 0))
    return (
        result_out,
        grad_target,
        grad_memory,
        grad_w_qkv,
        grad_w_out,
        grad_wq,
        grad_wkv,
        grad_wo,
        grad_w_up,
        grad_w_down,
        norm_sums[:3],
        norm_sums[3:6],
    )


def solution(mesh):
    rows_spec = P(("dp", "mem"), None)
    memory_spec = P("dp", "mem", None)
    return jax.shard_map(
        body,
        mesh=mesh,
        in_specs=(rows_spec, memory_spec, rows_spec, P("dp", None), P("dp", None)) + (P(),) * 9,
        out_specs=(rows_spec, rows_spec, memory_spec) + (P(),) * 9,
        check_vma=False,
    )
```

profile of v0, /device:TPU:0, one launch (start us, length us, event | category | flops | bytes accessed | tf_op | source)
XLA Modules:
  0.0 192.2 jit_solution(7351784525060643097)
XLA Ops:
  0.7 1.3 constant_dynamic-slice_fusion
  2.0 3.0 %collective-permute-start = (bf16[4,256,512]{2,1,0:T(8,128)(2,1)S(1)}, bf16[4,256,512]{2,1,0:T(8,128)(2,1)S(1)}, u32[]{:S(2)}, u32[]{:S(2)}) collective-permute-start(bf16[4,256,512]{2,1,0:T(8,128)(2,1)S(1)} %constant_dynamic-slice_fusion), channel_id=1, source_target_pairs={{0,1},{1,0},{2,3},{3,2},{4,5},{5,4},{6,7},{7,6},{8,9},{9,8},{10,11... | collective-permute-start | bytes 3145736 | tf_op jit(solution)/shard_map/ppermute | solution.py:1055
  5.7 21.0 %shard_map.229 = (bf16[512,512]{1,0:T(8,128)(2,1)}, bf16[512,1536]{1,0:T(8,128)(2,1)}, f32[16,256]{1,0:T(8,128)}, bf16[512,512]{1,0:T(8,128)(2,1)}, f32[512,512]...) custom-call(s32[5]{0:T(128)} %stack.23.me_ref.refs_0_.spot_ref, ...), custom_call_target="tpu_custom_call" | custom-call | flops 500000000 | bytes 1500000 | tf_op jit(solution)/shard_map/pallas_call | solution.py:945
  26.7 1.5 collective-permute-done.refs_11_.refs_0_
  28.2 1.0 copy-done.4
  29.1 26.3 %shard_map.230 = (bf16[512,512]{1,0:T(8,128)(2,1)}, f32[16,256]{1,0:T(8,128)}, f32[16,256]{1,0:T(8,128)}, f32[512,512]{1,0:T(8,128)}, bf16[512,512]{1,0:T(8,128)...) custom-call(s32[5]{0:T(128)} %stack.23.me_ref.refs_0_.spot_ref, ...), custom_call_target="tpu_custom_call", output_to_operand_aliasing={{8}: (16, {})} | custom-call | flops 500000000 | bytes 1500000 | tf_op jit(solution)/shard_map/pallas_call | solution.py:945
  55.6 6.3 %shard_map.231 = (bf16[1,512,1024]{2,1,0:T(8,128)(2,1)}, bf16[512,256]{1,0:T(8,128)(2,1)}) custom-call(s32[5]{0:T(128)} %stack.23.me_ref.refs_0_.spot_ref, s32[2,4]{1,0:T(2,128)} %len_ref.15, s32[2,4]{1,0:T(2,128)} %src_ref.5, bf16[512,512]{1,0:T(8,128)(2,1)} %get-tuple-element.139.refs_4_.query_ref, f32[16,256]{1,0:T(8,128)} %get-tuple-element.147.norm_ref, ...), custom_call_target="tpu_custom_call" | custom-call | flops 10000000000 | bytes 30000000 | tf_op jit(solution)/shard_map/pallas_call | solution.py:945
  62.0 2.0 %shard_map.232 = (bf16[1152,512]{1,0:T(8,128)(2,1)S(1)}, bf16[1152,512]{1,0:T(8,128)(2,1)S(1)}) custom-call(s32[5]{0:T(128)S(1)} %copy-done.17, bf16[2304,512]{1,0:T(8,128)(2,1)S(1)} %copy-done.7, bf16[2304,512]{1,0:T(8,128)(2,1)S(1)} %collective-permute-done.1.refs_1_), custom_call_target="tpu_custom_call" | custom-call | flops 10000000 | bytes 30000 | tf_op jit(solution)/shard_map/pallas_call | solution.py:945
  64.0 1.8 collective-permute-start.2
  65.8 8.0 %shard_map.233 = (bf16[3,512,1024]{2,1,0:T(8,128)(2,1)S(1)}, bf16[512,256]{1,0:T(8,128)(2,1)S(1)}) custom-call(s32[5]{0:T(128)S(1)} %copy-done.17, s32[2,4]{1,0:T(2,128)S(1)} %copy-done.20, s32[2,4]{1,0:T(2,128)S(1)} %copy-done.23, bf16[512,512]{1,0:T(8,128)(2,1)S(1)} %copy-done.15, f32[16,256]{1,0:T(8,128)S(1)} %copy-done.25, f32[16,256]{1,0:T(8,128)S(1)} %copy-done.26, ...), custom_call_target="tpu_custom_call" | custom-call | flops 10000000000 | bytes 30000000 | tf_op jit(solution)/shard_map/pallas_call | solution.py:945
  73.9 2.9 %shard_map.234.wkv_grad_ref = bf16[2,512,512]{2,1,0:T(8,128)(2,1)S(1)} custom-call(s32[5]{0:T(128)S(1)} %copy-done.17, s32[2,4]{1,0:T(2,128)S(1)} %copy-done.20, bf16[1,512,1024]{2,1,0:T(8,128)(2,1)S(1)} %copy-done.2, bf16[3,512,1024]{2,1,0:T(8,128)(2,1)S(1)} %get-tuple-element.164.pair_grad_rest_ref, bf16[8,256,512]{2,1,0:T(8,128)(2,1)S(1)} %copy-done.1, ...), custom_call_target="tpu_custom_call" | custom-call | flops 1000000000 | bytes 3000000 | tf_op jit(solution)/shard_map/pallas_call | solution.py:945
  77.0 3.1 %shard_map.235 = (bf16[1040,512]{1,0:T(8,128)(2,1)S(1)}, bf16[1040,512]{1,0:T(8,128)(2,1)S(1)}, f32[512,512]{1,0:T(8,128)S(1)}, bf16[512,512]{1,0:T(8,128)(2,1)S(1)}) custom-call(s32[5]{0:T(128)S(1)} %copy-done.17, f32[512,512]{1,0:T(8,128)S(1)} %copy-done.6, bf16[512,256]{1,0:T(8,128)(2,1)S(1)} %copy-done.16, ...), custom_call_target="tpu_custom_call" | custom-call | flops 100000000 | bytes 300000 | tf_op jit(solution)/shard_map/pallas_call | solution.py:945
  80.4 0.8 shard_map.236
  81.3 1.6 collective-permute-start.3
  82.9 2.0 %shard_map.237 = bf16[4,128,512]{2,1,0:T(8,128)(2,1)S(1)} custom-call(s32[5]{0:T(128)S(1)} %copy-done.17, s32[2,4]{1,0:T(2,128)S(1)} %copy-done.20, bf16[1,512,1024]{2,1,0:T(8,128)(2,1)S(1)} %copy-done.2, bf16[3,512,1024]{2,1,0:T(8,128)(2,1)S(1)} %get-tuple-element.164.pair_grad_rest_ref, bf16[512,1024]{1,0:T(8,128)(2,1)S(1)} %copy-done), custom_call_target="tpu_custom_call" | custom-call | flops 10000000 | bytes 30000 | tf_op jit(solution)/shard_map/pallas_call | solution.py:945
  85.5 6.5 %shard_map.238 = (bf16[512,1536]{1,0:T(8,128)(2,1)S(1)}, bf16[384,512]{1,0:T(8,128)(2,1)S(1)}, bf16[384,512]{1,0:T(8,128)(2,1)S(1)}, bf16[384,512]{1,0:T(8,128)(2,1)S(1)}, bf16[384,512]{1,0:T(8,128)(2,1)S(1)}) custom-call(s32[5]{0:T(128)S(1)} %copy-done.17, s32[2,4]{1,0:T(2,128)S(1)} %copy-done.20, bf16[512,1536]{1,0:T(8,128)(2,1)S(1)} %copy-done.11, ...), custom_call_target="tpu_custom_call" | custom-call | flops 100000000 | bytes 300000 | tf_op jit(solution)/shard_map/pallas_call | solution.py:945
  92.1 3.0 %collective-permute-done.3.refs_1_ = bf16[576,512]{1,0:T(8,128)(2,1)S(1)} collective-permute-done((bf16[576,512]{1,0:T(8,128)(2,1)S(1)}, bf16[576,512]{1,0:T(8,128)(2,1)S(1)}, u32[]{:S(2)}, u32[]{:S(2)}) %collective-permute-start.3) | collective-permute-done | bytes 589856 | tf_op jit(solution)/shard_map/ppermute | solution.py:879
  96.3 1.7 collective-permute-start.5
  98.0 2.7 %collective-permute-start.6 = (bf16[144,512]{1,0:T(8,128)(2,1)S(1)}, bf16[144,512]{1,0:T(8,128)(2,1)S(1)}, u32[]{:S(2)}, u32[]{:S(2)}) collective-permute-start(bf16[144,512]{1,0:T(8,128)(2,1)S(1)} %get-tuple-element.193), channel_id=1, source_target_pairs={{0,16},{1,17},{2,18},{3,19},{4,20},{5,21},{6,22},{7,23},{8,24},{9,... | collective-permute-start | bytes 442376 | tf_op jit(solution)/shard_map/ppermute | solution.py:879
  100.8 1.6 shard_map.240
  102.5 2.3 %collective-permute-start.10 = (bf16[912,512]{1,0:T(8,128)(2,1)S(1)}, bf16[912,512]{1,0:T(8,128)(2,1)S(1)}, u32[]{:S(2)}, u32[]{:S(2)}) collective-permute-start(bf16[912,512]{1,0:T(8,128)(2,1)S(1)} %get-tuple-element.206), channel_id=1, source_target_pairs={{0,4},{1,5},{2,3},{3,2},{4,0},{5,1},{6,7},{7,6},{8,12},{9,13},{10,... | collective-permute-start | bytes 2801672 | tf_op jit(solution)/shard_map/ppermute | solution.py:879
  104.7 2.7 %shard_map.242 = bf16[512,512]{1,0:T(8,128)(2,1)} custom-call(s32[5]{0:T(128)S(1)} %copy-done.17, s32[2,4]{1,0:T(2,128)S(1)} %copy-done.20, bf16[512,1536]{1,0:T(8,128)(2,1)S(1)} %get-tuple-element.210.grad_triple_ref, bf16[512,1536]{1,0:T(8,128)(2,1)S(1)} %copy-done.10, f32[512,512]{1,0:T(8,128)S(1)} %get-tuple-element.211.grad_hidden_ref), custom_call_target="tpu_custom_call" | custom-call | flops 30000001024 | bytes 90000000 | tf_op jit(solution)/shard_map/pallas_call | solution.py:945
  107.4 3.2 %shard_map.241 = (bf16[4,256,512]{2,1,0:T(8,128)(2,1)S(1)}, bf16[4,128,512]{2,1,0:T(8,128)(2,1)S(1)}) custom-call(s32[5]{0:T(128)S(1)} %copy-done.17, s32[2,4]{1,0:T(2,128)S(1)} %copy-done.20, bf16[1,512,1024]{2,1,0:T(8,128)(2,1)S(1)} %copy-done.2, bf16[3,512,1024]{2,1,0:T(8,128)(2,1)S(1)} %get-tuple-element.164.pair_grad_rest_ref, bf16[512,1024]{1,0:T(8,128)(2,1)S(1)} %copy-done), custom_call_target="tpu_custom_call" | custom-call | flops 10000000 | bytes 30000 | tf_op jit(solution)/shard_map/pallas_call | solution.py:945
  110.6 1.4 collective-permute-done.6.refs_2_
  112.0 4.3 %collective-permute-done.10.refs_1_ = bf16[912,512]{1,0:T(8,128)(2,1)S(1)} collective-permute-done((bf16[912,512]{1,0:T(8,128)(2,1)S(1)}, bf16[912,512]{1,0:T(8,128)(2,1)S(1)}, u32[]{:S(2)}, u32[]{:S(2)}) %collective-permute-start.10) | collective-permute-done | bytes 933920 | tf_op jit(solution)/shard_map/ppermute | solution.py:879
  116.3 1.7 collective-permute-start.16
  118.0 0.8 shard_map.243
  119.2 3.7 %collective-permute-start.15 = (bf16[144,512]{1,0:T(8,128)(2,1)S(1)}, bf16[144,512]{1,0:T(8,128)(2,1)S(1)}, u32[]{:S(2)}, u32[]{:S(2)}) collective-permute-start(bf16[144,512]{1,0:T(8,128)(2,1)S(1)} %shard_map.244.refs_0_), channel_id=1, source_target_pairs={{0,24},{1,25},{2,26},{3,27},{4,28},{5,29},{6,30},{7,31},{8,16},{9,... | collective-permute-start | bytes 442376 | tf_op jit(solution)/shard_map/ppermute | solution.py:879
  122.9 0.8 collective-permute-start.13
  123.7 4.3 %collective-permute-done.15.refs_3_ = bf16[144,512]{1,0:T(8,128)(2,1)S(1)} collective-permute-done((bf16[144,512]{1,0:T(8,128)(2,1)S(1)}, bf16[144,512]{1,0:T(8,128)(2,1)S(1)}, u32[]{:S(2)}, u32[]{:S(2)}) %collective-permute-start.15) | collective-permute-done | bytes 147488 | tf_op jit(solution)/shard_map/ppermute | solution.py:879
  127.9 6.4 %collective-permute-done.14.refs_2_ = bf16[144,512]{1,0:T(8,128)(2,1)S(1)} collective-permute-done((bf16[144,512]{1,0:T(8,128)(2,1)S(1)}, bf16[144,512]{1,0:T(8,128)(2,1)S(1)}, u32[]{:S(2)}, u32[]{:S(2)}) %collective-permute-start.14) | collective-permute-done | bytes 147488 | tf_op jit(solution)/shard_map/ppermute | solution.py:879
  134.9 1.3 collective-permute-start.20
  137.2 3.5 %collective-permute-start.18 = (bf16[128,512]{1,0:T(8,128)(2,1)S(1)}, bf16[128,512]{1,0:T(8,128)(2,1)S(1)}, u32[]{:S(2)}, u32[]{:S(2)}) collective-permute-start(bf16[128,512]{1,0:T(8,128)(2,1)S(1)} %get-tuple-element.229), channel_id=1, source_target_pairs={{0,16},{1,17},{2,18},{3,19},{4,20},{5,21},{6,22},{7,23},{8,24},{9,... | collective-permute-start | bytes 393224 | tf_op jit(solution)/shard_map/ppermute | solution.py:879
  141.3 2.8 %collective-permute-done.17.refs_1_ = bf16[128,512]{1,0:T(8,128)(2,1)S(1)} collective-permute-done((bf16[128,512]{1,0:T(8,128)(2,1)S(1)}, bf16[128,512]{1,0:T(8,128)(2,1)S(1)}, u32[]{:S(2)}, u32[]{:S(2)}) %collective-permute-start.17) | collective-permute-done | bytes 131104 | tf_op jit(solution)/shard_map/ppermute | solution.py:879
  144.1 3.7 %collective-permute-done.18.refs_2_ = bf16[128,512]{1,0:T(8,128)(2,1)S(1)} collective-permute-done((bf16[128,512]{1,0:T(8,128)(2,1)S(1)}, bf16[128,512]{1,0:T(8,128)(2,1)S(1)}, u32[]{:S(2)}, u32[]{:S(2)}) %collective-permute-start.18) | collective-permute-done | bytes 131104 | tf_op jit(solution)/shard_map/ppermute | solution.py:879
  148.5 3.0 %collective-permute-start.21 = (bf16[1152,512]{1,0:T(8,128)(2,1)S(1)}, bf16[1152,512]{1,0:T(8,128)(2,1)S(1)}, u32[]{:S(2)}, u32[]{:S(2)}) collective-permute-start(bf16[1152,512]{1,0:T(8,128)(2,1)S(1)} %shard_map.247.refs_0_), channel_id=1, source_target_pairs={{0,4},{1,5},{2,3},{3,2},{4,0},{5,1},{6,7},{7,6},{8,12},{9,13},{10,... | collective-permute-start | bytes 3538952 | tf_op jit(solution)/shard_map/ppermute | solution.py:879
  151.6 0.9 collective-permute-start.24
  152.4 4.6 %collective-permute-start.23 = (bf16[112,512]{1,0:T(8,128)(2,1)S(1)}, bf16[112,512]{1,0:T(8,128)(2,1)S(1)}, u32[]{:S(2)}, u32[]{:S(2)}) collective-permute-start(bf16[112,512]{1,0:T(8,128)(2,1)S(1)} %get-tuple-element.241.refs_0_), channel_id=1, source_target_pairs={{0,16},{1,17},{2,18},{3,19},{4,20},{5,21},{6,22},{7,23},{8,24},{9,... | collective-permute-start | bytes 344072 | tf_op jit(solution)/shard_map/ppermute | solution.py:879
  157.1 1.2 collective-permute-done.24.refs_3_
  158.2 4.2 %collective-permute-done.23.refs_2_ = bf16[112,512]{1,0:T(8,128)(2,1)S(1)} collective-permute-done((bf16[112,512]{1,0:T(8,128)(2,1)S(1)}, bf16[112,512]{1,0:T(8,128)(2,1)S(1)}, u32[]{:S(2)}, u32[]{:S(2)}) %collective-permute-start.23) | collective-permute-done | bytes 114720 | tf_op jit(solution)/shard_map/ppermute | solution.py:879
  163.8 8.5 %collective-permute-done.25.refs_1_ = bf16[448,512]{1,0:T(8,128)(2,1)S(1)} collective-permute-done((bf16[448,512]{1,0:T(8,128)(2,1)S(1)}, bf16[448,512]{1,0:T(8,128)(2,1)S(1)}, u32[]{:S(2)}, u32[]{:S(2)}) %collective-permute-start.25) | collective-permute-done | bytes 458784 | tf_op jit(solution)/shard_map/ppermute | solution.py:879
  173.5 2.2 %collective-permute-done.27.refs_1_ = bf16[1152,512]{1,0:T(8,128)(2,1)S(1)} collective-permute-done((bf16[1152,512]{1,0:T(8,128)(2,1)S(1)}, bf16[1152,512]{1,0:T(8,128)(2,1)S(1)}, u32[]{:S(2)}, u32[]{:S(2)}) %collective-permute-start.27) | collective-permute-done | bytes 1179680 | tf_op jit(solution)/shard_map/ppermute | solution.py:879
  175.8 1.7 collective-permute-done.28.refs_3_
  177.4 4.7 %shard_map.251 = (f32[2048,512]{1,0:T(8,128)}, f32[512,2048]{1,0:T(8,128)}, f32[512,512]{1,0:T(8,128)}) custom-call(s32[5]{0:T(128)S(1)} %copy-done.17, bf16[1152,512]{1,0:T(8,128)(2,1)S(1)} %shard_map.247.refs_0_, bf16[1152,512]{1,0:T(8,128)(2,1)S(1)} %collective-permute-done.27.refs_1_, bf16[1152,512]{1,0:T(8,128)(2,1)S(1)} %collective-permute-done.21.refs_2_, ...), custom_call_target="tpu_custom_call" | custom-call | flops 1000000000 | bytes 3000000 | tf_op jit(solution)/shard_map/pallas_call | solution.py:945
  182.1 2.6 %shard_map.252 = (f32[512,512]{1,0:T(8,128)}, f32[512,1024]{1,0:T(8,128)}, f32[512,1536]{1,0:T(8,128)}, f32[512,512]{1,0:T(8,128)}) custom-call(s32[5]{0:T(128)S(1)} %copy-done.17, bf16[896,512]{1,0:T(8,128)(2,1)S(1)} %shard_map.250.refs_0_, bf16[896,512]{1,0:T(8,128)(2,1)S(1)} %collective-permute-done.29.refs_1_), custom_call_target="tpu_custom_call" | custom-call | flops 1000000000 | bytes 3000000 | tf_op jit(solution)/shard_map/pallas_call | solution.py:945
  184.8 2.1 %collective-permute-done.26.refs_0_ = bf16[896,512]{1,0:T(8,128)(2,1)S(1)} collective-permute-done((bf16[896,512]{1,0:T(8,128)(2,1)S(1)}, bf16[896,512]{1,0:T(8,128)(2,1)S(1)}, u32[]{:S(2)}, u32[]{:S(2)}) %collective-permute-start.26) | collective-permute-done | bytes 917536 | tf_op jit(solution)/shard_map/ppermute | solution.py:879
  187.2 0.8 copy-done.29
  189.4 2.6 %shard_map.253 = (f32[512,512]{1,0:T(8,128)}, f32[512,1024]{1,0:T(8,128)}, f32[512,1536]{1,0:T(8,128)}, f32[512,512]{1,0:T(8,128)}) custom-call(s32[5]{0:T(128)S(1)} %copy-done.17, bf16[896,512]{1,0:T(8,128)(2,1)S(1)} %collective-permute-done.26.refs_0_, ...), custom_call_target="tpu_custom_call", output_to_operand_aliasing={{0}: (3, {}), {1}: (4, {}), {2}: (5, {}), {3}: (6, {})} | custom-call | flops 1000000000 | bytes 3000000 | tf_op jit(solution)/shard_map/pallas_call | solution.py:945
  (106 shorter events, 10.8 us)
Async XLA Ops:
  2.0 26.2 %collective-permute-start = (bf16[4,256,512]{2,1,0:T(8,128)(2,1)S(1)}, bf16[4,256,512]{2,1,0:T(8,128)(2,1)S(1)}, u32[]{:S(2)}, u32[]{:S(2)}) collective-permute-start(bf16[4,256,512]{2,1,0:T(8,128)(2,1)S(1)} %constant_dynamic-slice_fusion), channel_id=1, source_target_pairs={{0,1},{1,0},{2,3},{3,2},{4,5},{5,4},{6,7},{7,6},{8,9},{9,8},{10,11... | collective-permute-start | bytes 3145736 | tf_op jit(solution)/shard_map/ppermute | solution.py:1055
  55.4 6.5 %collective-permute-start.1 = (bf16[2304,512]{1,0:T(8,128)(2,1)}, bf16[2304,512]{1,0:T(8,128)(2,1)S(1)}, u32[]{:S(2)}, u32[]{:S(2)}) collective-permute-start(bf16[2304,512]{1,0:T(8,128)(2,1)} %get-tuple-element.146), channel_id=1, source_target_pairs={{0,2},{1,3},{2,0},{3,1},{4,6},{5,7},{6,4},{7,5},{8,10},{9,11},{10,... | collective-permute-start | bytes 7077896 | tf_op jit(solution)/shard_map/ppermute | solution.py:879
  55.5 6.4 %copy-start.7 = (bf16[2304,512]{1,0:T(8,128)(2,1)S(1)}, bf16[2304,512]{1,0:T(8,128)(2,1)}, u32[]{:S(2)}) copy-start(bf16[2304,512]{1,0:T(8,128)(2,1)} %get-tuple-element.145.refs_0_) | copy-start | bytes 7077892
  55.5 6.4 %copy-start.17 = (s32[5]{0:T(128)S(1)}, s32[5]{0:T(128)}, u32[]{:S(2)}) copy-start(s32[5]{0:T(128)} %stack.23.me_ref.refs_0_.spot_ref) | copy-start | bytes 64
  55.5 10.2 %copy-start.24 = (bf16[512,512]{1,0:T(8,128)(2,1)S(1)}, bf16[512,512]{1,0:T(8,128)(2,1)}, u32[]{:S(2)}) copy-start(bf16[512,512]{1,0:T(8,128)(2,1)} %get-tuple-element.149.grad_attn_ref) | copy-start | bytes 1572868
  55.6 10.2 %copy-start.25 = (f32[16,256]{1,0:T(8,128)S(1)}, f32[16,256]{1,0:T(8,128)}, u32[]{:S(2)}) copy-start(f32[16,256]{1,0:T(8,128)} %get-tuple-element.147.norm_ref) | copy-start | bytes 49156
  55.6 10.2 %copy-start.26 = (f32[16,256]{1,0:T(8,128)S(1)}, f32[16,256]{1,0:T(8,128)}, u32[]{:S(2)}) copy-start(f32[16,256]{1,0:T(8,128)} %get-tuple-element.148.along_ref) | copy-start | bytes 49156
  61.9 3.8 %copy-start.3 = (bf16[4,512,1024]{2,1,0:T(8,128)(2,1)S(1)}, bf16[4,512,1024]{2,1,0:T(8,128)(2,1)}, u32[]{:S(2)}) copy-start(bf16[4,512,1024]{2,1,0:T(8,128)(2,1)} %get-tuple-element.158.pair_hbm) | copy-start | bytes 12582916
  61.9 3.8 %copy-start.15 = (bf16[512,512]{1,0:T(8,128)(2,1)S(1)}, bf16[512,512]{1,0:T(8,128)(2,1)}, u32[]{:S(2)}) copy-start(bf16[512,512]{1,0:T(8,128)(2,1)} %get-tuple-element.139.refs_4_.query_ref) | copy-start | bytes 1572868
  62.0 3.8 %copy-start.20 = (s32[2,4]{1,0:T(2,128)S(1)}, s32[2,4]{1,0:T(2,128)}, u32[]{:S(2)}) copy-start(s32[2,4]{1,0:T(2,128)} %len_ref.15) | copy-start | bytes 100
  63.9 9.9 %copy-start.1 = (bf16[8,256,512]{2,1,0:T(8,128)(2,1)S(1)}, bf16[8,256,512]{2,1,0:T(8,128)(2,1)}, u32[]{:S(2)}) copy-start(bf16[8,256,512]{2,1,0:T(8,128)(2,1)} %memory_ref.3) | copy-start | bytes 6291460
  63.9 9.9 %copy-start.2 = (bf16[1,512,1024]{2,1,0:T(8,128)(2,1)S(1)}, bf16[1,512,1024]{2,1,0:T(8,128)(2,1)}, u32[]{:S(2)}) copy-start(bf16[1,512,1024]{2,1,0:T(8,128)(2,1)} %get-tuple-element.207.pair_grad_long_ref) | copy-start | bytes 3145732
  64.0 9.9 %copy-start.5 = (bf16[4,256,512]{2,1,0:T(8,128)(2,1)S(1)}, bf16[4,256,512]{2,1,0:T(8,128)(2,1)}, u32[]{:S(2)}) copy-start(bf16[4,256,512]{2,1,0:T(8,128)(2,1)} %copy-done.4) | copy-start | bytes 3145732
  64.0 16.4 %collective-permute-start.2 = (bf16[1152,512]{1,0:T(8,128)(2,1)S(1)}, bf16[1152,512]{1,0:T(8,128)(2,1)S(1)}, u32[]{:S(2)}, u32[]{:S(2)}) collective-permute-start(bf16[1152,512]{1,0:T(8,128)(2,1)S(1)} %get-tuple-element.156), channel_id=1, source_target_pairs={{0,4},{1,5},{2,3},{3,2},{4,0},{5,1},{6,7},{7,6},{8,12},{9,13},{10,... | collective-permute-start | bytes 3538952 | tf_op jit(solution)/shard_map/ppermute | solution.py:879
  80.1 12.0 %collective-permute-start.4 = (bf16[1040,512]{1,0:T(8,128)(2,1)S(1)}, bf16[1040,512]{1,0:T(8,128)(2,1)S(1)}, u32[]{:S(2)}, u32[]{:S(2)}) collective-permute-start(bf16[1040,512]{1,0:T(8,128)(2,1)S(1)} %get-tuple-element.183), channel_id=1, source_target_pairs={{0,2},{1,3},{2,0},{3,1},{4,6},{5,7},{6,4},{7,5},{8,10},{9,11},{10,... | collective-permute-start | bytes 3194888 | tf_op jit(solution)/shard_map/ppermute | solution.py:879
  81.2 4.3 %copy-start.11 = (bf16[512,1536]{1,0:T(8,128)(2,1)S(1)}, bf16[512,1536]{1,0:T(8,128)(2,1)}, u32[]{:S(2)}) copy-start(bf16[512,1536]{1,0:T(8,128)(2,1)} %get-tuple-element.173.qkv_ref) | copy-start | bytes 4718596
  81.3 4.3 %copy-start.13 = (bf16[512,512]{1,0:T(8,128)(2,1)S(1)}, bf16[512,512]{1,0:T(8,128)(2,1)}, u32[]{:S(2)}) copy-start(bf16[512,512]{1,0:T(8,128)(2,1)} %get-tuple-element.178.sorted_ref) | copy-start | bytes 1572868
  81.3 4.2 %copy-start.21 = (f32[16,256]{1,0:T(8,128)S(1)}, f32[16,256]{1,0:T(8,128)}, u32[]{:S(2)}) copy-start(f32[16,256]{1,0:T(8,128)} %get-tuple-element.174.norm_ref) | copy-start | bytes 49156
  81.3 13.8 %collective-permute-start.3 = (bf16[576,512]{1,0:T(8,128)(2,1)S(1)}, bf16[576,512]{1,0:T(8,128)(2,1)S(1)}, u32[]{:S(2)}, u32[]{:S(2)}) collective-permute-start(bf16[576,512]{1,0:T(8,128)(2,1)S(1)} %get-tuple-element.172), channel_id=1, source_target_pairs={{0,1},{1,0},{2,6},{3,7},{4,5},{5,4},{6,2},{7,3},{8,9},{9,8},{10,14... | collective-permute-start | bytes 1769480 | tf_op jit(solution)/shard_map/ppermute | solution.py:879
  85.0 17.5 %collective-permute-start.11 = (bf16[4,128,512]{2,1,0:T(8,128)(2,1)S(1)}, bf16[4,128,512]{2,1,0:T(8,128)(2,1)S(1)}, u32[]{:S(2)}, u32[]{:S(2)}) collective-permute-start(bf16[4,128,512]{2,1,0:T(8,128)(2,1)S(1)} %shard_map.237), channel_id=1, source_target_pairs={{0,1},{1,0},{2,3},{3,2},{4,5},{5,4},{6,7},{7,6},{8,9},{9,8},{10,11... | collective-permute-start | bytes 1572872 | tf_op jit(solution)/shard_map/ppermute | solution.py:1192
  95.1 5.6 %collective-permute-start.8 = (bf16[384,512]{1,0:T(8,128)(2,1)S(1)}, bf16[384,512]{1,0:T(8,128)(2,1)S(1)}, u32[]{:S(2)}, u32[]{:S(2)}) collective-permute-start(bf16[384,512]{1,0:T(8,128)(2,1)S(1)} %get-tuple-element.198), channel_id=1, source_target_pairs={{0,2},{1,3},{2,0},{3,1},{4,6},{5,7},{6,4},{7,5},{8,10},{9,11},{10,... | collective-permute-start | bytes 1179656 | tf_op jit(solution)/shard_map/ppermute | solution.py:879
  95.1 5.7 %collective-permute-start.9 = (bf16[384,512]{1,0:T(8,128)(2,1)S(1)}, bf16[384,512]{1,0:T(8,128)(2,1)S(1)}, u32[]{:S(2)}, u32[]{:S(2)}) collective-permute-start(bf16[384,512]{1,0:T(8,128)(2,1)S(1)} %get-tuple-element.200), channel_id=1, source_target_pairs={{0,2},{1,3},{2,0},{3,1},{4,6},{5,7},{6,4},{7,5},{8,10},{9,11},{10,... | collective-permute-start | bytes 1179656 | tf_op jit(solution)/shard_map/ppermute | solution.py:879
  96.3 8.4 %copy-start.10 = (bf16[512,1536]{1,0:T(8,128)(2,1)S(1)}, bf16[512,1536]{1,0:T(8,128)(2,1)}, u32[]{:S(2)}) copy-start(bf16[512,1536]{1,0:T(8,128)(2,1)} %w_qkv_ref.3) | copy-start | bytes 4718596
  96.3 14.2 %collective-permute-start.5 = (bf16[144,512]{1,0:T(8,128)(2,1)S(1)}, bf16[144,512]{1,0:T(8,128)(2,1)S(1)}, u32[]{:S(2)}, u32[]{:S(2)}) collective-permute-start(bf16[144,512]{1,0:T(8,128)(2,1)S(1)} %get-tuple-element.192), channel_id=1, source_target_pairs={{0,8},{1,9},{2,10},{3,11},{4,12},{5,13},{6,14},{7,15},{8,0},{9,1},... | collective-permute-start | bytes 442376 | tf_op jit(solution)/shard_map/ppermute | solution.py:879
  98.0 14.0 %collective-permute-start.6 = (bf16[144,512]{1,0:T(8,128)(2,1)S(1)}, bf16[144,512]{1,0:T(8,128)(2,1)S(1)}, u32[]{:S(2)}, u32[]{:S(2)}) collective-permute-start(bf16[144,512]{1,0:T(8,128)(2,1)S(1)} %get-tuple-element.193), channel_id=1, source_target_pairs={{0,16},{1,17},{2,18},{3,19},{4,20},{5,21},{6,22},{7,23},{8,24},{9,... | collective-permute-start | bytes 442376 | tf_op jit(solution)/shard_map/ppermute | solution.py:879
  100.7 11.3 %collective-permute-start.7 = (bf16[144,512]{1,0:T(8,128)(2,1)S(1)}, bf16[144,512]{1,0:T(8,128)(2,1)S(1)}, u32[]{:S(2)}, u32[]{:S(2)}) collective-permute-start(bf16[144,512]{1,0:T(8,128)(2,1)S(1)} %get-tuple-element.194), channel_id=1, source_target_pairs={{0,24},{1,25},{2,26},{3,27},{4,28},{5,29},{6,30},{7,31},{8,16},{9,... | collective-permute-start | bytes 442376 | tf_op jit(solution)/shard_map/ppermute | solution.py:879
  102.5 13.8 %collective-permute-start.10 = (bf16[912,512]{1,0:T(8,128)(2,1)S(1)}, bf16[912,512]{1,0:T(8,128)(2,1)S(1)}, u32[]{:S(2)}, u32[]{:S(2)}) collective-permute-start(bf16[912,512]{1,0:T(8,128)(2,1)S(1)} %get-tuple-element.206), channel_id=1, source_target_pairs={{0,4},{1,5},{2,3},{3,2},{4,0},{5,1},{6,7},{7,6},{8,12},{9,13},{10,... | collective-permute-start | bytes 2801672 | tf_op jit(solution)/shard_map/ppermute | solution.py:879
  116.3 18.1 %collective-permute-start.16 = (bf16[4,128,512]{2,1,0:T(8,128)(2,1)S(1)}, bf16[4,128,512]{2,1,0:T(8,128)(2,1)S(1)}, u32[]{:S(2)}, u32[]{:S(2)}) collective-permute-start(bf16[4,128,512]{2,1,0:T(8,128)(2,1)S(1)} %get-tuple-element.222), channel_id=1, source_target_pairs={{0,1},{1,0},{2,3},{3,2},{4,5},{5,4},{6,7},{7,6},{8,9},{9,8},{10,11... | collective-permute-start | bytes 1572872 | tf_op jit(solution)/shard_map/ppermute | solution.py:1192
  118.7 15.6 %collective-permute-start.12 = (bf16[464,512]{1,0:T(8,128)(2,1)S(1)}, bf16[464,512]{1,0:T(8,128)(2,1)S(1)}, u32[]{:S(2)}, u32[]{:S(2)}) collective-permute-start(bf16[464,512]{1,0:T(8,128)(2,1)S(1)} %get-tuple-element.217), channel_id=1, source_target_pairs={{0,1},{1,0},{2,6},{3,7},{4,5},{5,4},{6,2},{7,3},{8,9},{9,8},{10,14... | collective-permute-start | bytes 1425416 | tf_op jit(solution)/shard_map/ppermute | solution.py:879
  119.2 8.7 %collective-permute-start.15 = (bf16[144,512]{1,0:T(8,128)(2,1)S(1)}, bf16[144,512]{1,0:T(8,128)(2,1)S(1)}, u32[]{:S(2)}, u32[]{:S(2)}) collective-permute-start(bf16[144,512]{1,0:T(8,128)(2,1)S(1)} %shard_map.244.refs_0_), channel_id=1, source_target_pairs={{0,24},{1,25},{2,26},{3,27},{4,28},{5,29},{6,30},{7,31},{8,16},{9,... | collective-permute-start | bytes 442376 | tf_op jit(solution)/shard_map/ppermute | solution.py:879
  122.9 11.5 %collective-permute-start.14 = (bf16[144,512]{1,0:T(8,128)(2,1)S(1)}, bf16[144,512]{1,0:T(8,128)(2,1)S(1)}, u32[]{:S(2)}, u32[]{:S(2)}) collective-permute-start(bf16[144,512]{1,0:T(8,128)(2,1)S(1)} %shard_map.244.refs_0_), channel_id=1, source_target_pairs={{0,16},{1,17},{2,18},{3,19},{4,20},{5,21},{6,22},{7,23},{8,24},{9,... | collective-permute-start | bytes 442376 | tf_op jit(solution)/shard_map/ppermute | solution.py:879
  122.9 11.5 %collective-permute-start.13 = (bf16[144,512]{1,0:T(8,128)(2,1)S(1)}, bf16[144,512]{1,0:T(8,128)(2,1)S(1)}, u32[]{:S(2)}, u32[]{:S(2)}) collective-permute-start(bf16[144,512]{1,0:T(8,128)(2,1)S(1)} %shard_map.244.refs_0_), channel_id=1, source_target_pairs={{0,8},{1,9},{2,10},{3,11},{4,12},{5,13},{6,14},{7,15},{8,0},{9,1},... | collective-permute-start | bytes 442376 | tf_op jit(solution)/shard_map/ppermute | solution.py:879
  134.3 14.1 %copy-start.28 = (bf16[4,128,512]{2,1,0:T(8,128)(2,1)}, bf16[4,128,512]{2,1,0:T(8,128)(2,1)S(1)}, u32[]{:S(2)}) copy-start(bf16[4,128,512]{2,1,0:T(8,128)(2,1)S(1)} %collective-permute-done.16) | copy-start | bytes 1572868
  134.9 12.9 %collective-permute-start.20 = (bf16[576,512]{1,0:T(8,128)(2,1)S(1)}, bf16[576,512]{1,0:T(8,128)(2,1)S(1)}, u32[]{:S(2)}, u32[]{:S(2)}) collective-permute-start(bf16[576,512]{1,0:T(8,128)(2,1)S(1)} %shard_map.246.refs_0_), channel_id=1, source_target_pairs={{0,1},{1,0},{2,6},{3,7},{4,5},{5,4},{6,2},{7,3},{8,9},{9,8},{10,14... | collective-permute-start | bytes 1769480 | tf_op jit(solution)/shard_map/ppermute | solution.py:879
  136.9 7.3 %collective-permute-start.17 = (bf16[128,512]{1,0:T(8,128)(2,1)S(1)}, bf16[128,512]{1,0:T(8,128)(2,1)S(1)}, u32[]{:S(2)}, u32[]{:S(2)}) collective-permute-start(bf16[128,512]{1,0:T(8,128)(2,1)S(1)} %get-tuple-element.228), channel_id=1, source_target_pairs={{0,8},{1,9},{2,10},{3,11},{4,12},{5,13},{6,14},{7,15},{8,0},{9,1},... | collective-permute-start | bytes 393224 | tf_op jit(solution)/shard_map/ppermute | solution.py:879
  137.2 10.6 %collective-permute-start.18 = (bf16[128,512]{1,0:T(8,128)(2,1)S(1)}, bf16[128,512]{1,0:T(8,128)(2,1)S(1)}, u32[]{:S(2)}, u32[]{:S(2)}) collective-permute-start(bf16[128,512]{1,0:T(8,128)(2,1)S(1)} %get-tuple-element.229), channel_id=1, source_target_pairs={{0,16},{1,17},{2,18},{3,19},{4,20},{5,21},{6,22},{7,23},{8,24},{9,... | collective-permute-start | bytes 393224 | tf_op jit(solution)/shard_map/ppermute | solution.py:879
  140.7 7.1 %collective-permute-start.19 = (bf16[128,512]{1,0:T(8,128)(2,1)S(1)}, bf16[128,512]{1,0:T(8,128)(2,1)S(1)}, u32[]{:S(2)}, u32[]{:S(2)}) collective-permute-start(bf16[128,512]{1,0:T(8,128)(2,1)S(1)} %get-tuple-element.230), channel_id=1, source_target_pairs={{0,24},{1,25},{2,26},{3,27},{4,28},{5,29},{6,30},{7,31},{8,16},{9,... | collective-permute-start | bytes 393224 | tf_op jit(solution)/shard_map/ppermute | solution.py:879
  148.5 24.4 %collective-permute-start.21 = (bf16[1152,512]{1,0:T(8,128)(2,1)S(1)}, bf16[1152,512]{1,0:T(8,128)(2,1)S(1)}, u32[]{:S(2)}, u32[]{:S(2)}) collective-permute-start(bf16[1152,512]{1,0:T(8,128)(2,1)S(1)} %shard_map.247.refs_0_), channel_id=1, source_target_pairs={{0,4},{1,5},{2,3},{3,2},{4,0},{5,1},{6,7},{7,6},{8,12},{9,13},{10,... | collective-permute-start | bytes 3538952 | tf_op jit(solution)/shard_map/ppermute | solution.py:879
  151.6 6.7 %collective-permute-start.24 = (bf16[112,512]{1,0:T(8,128)(2,1)S(1)}, bf16[112,512]{1,0:T(8,128)(2,1)S(1)}, u32[]{:S(2)}, u32[]{:S(2)}) collective-permute-start(bf16[112,512]{1,0:T(8,128)(2,1)S(1)} %get-tuple-element.241.refs_0_), channel_id=1, source_target_pairs={{0,24},{1,25},{2,26},{3,27},{4,28},{5,29},{6,30},{7,31},{8,16},{9,... | collective-permute-start | bytes 344072 | tf_op jit(solution)/shard_map/ppermute | solution.py:879
  152.4 10.0 %collective-permute-start.23 = (bf16[112,512]{1,0:T(8,128)(2,1)S(1)}, bf16[112,512]{1,0:T(8,128)(2,1)S(1)}, u32[]{:S(2)}, u32[]{:S(2)}) collective-permute-start(bf16[112,512]{1,0:T(8,128)(2,1)S(1)} %get-tuple-element.241.refs_0_), channel_id=1, source_target_pairs={{0,16},{1,17},{2,18},{3,19},{4,20},{5,21},{6,22},{7,23},{8,24},{9,... | collective-permute-start | bytes 344072 | tf_op jit(solution)/shard_map/ppermute | solution.py:879
  157.1 6.0 %collective-permute-start.22 = (bf16[112,512]{1,0:T(8,128)(2,1)S(1)}, bf16[112,512]{1,0:T(8,128)(2,1)S(1)}, u32[]{:S(2)}, u32[]{:S(2)}) collective-permute-start(bf16[112,512]{1,0:T(8,128)(2,1)S(1)} %get-tuple-element.241.refs_0_), channel_id=1, source_target_pairs={{0,8},{1,9},{2,10},{3,11},{4,12},{5,13},{6,14},{7,15},{8,0},{9,1},... | collective-permute-start | bytes 344072 | tf_op jit(solution)/shard_map/ppermute | solution.py:879
  163.7 8.5 %collective-permute-start.25 = (bf16[448,512]{1,0:T(8,128)(2,1)S(1)}, bf16[448,512]{1,0:T(8,128)(2,1)S(1)}, u32[]{:S(2)}, u32[]{:S(2)}) collective-permute-start(bf16[448,512]{1,0:T(8,128)(2,1)S(1)} %shard_map.249.refs_0_), channel_id=1, source_target_pairs={{0,1},{1,0},{2,6},{3,7},{4,5},{5,4},{6,2},{7,3},{8,9},{9,8},{10,14... | collective-permute-start | bytes 1376264 | tf_op jit(solution)/shard_map/ppermute | solution.py:879
  172.8 2.9 %collective-permute-start.27 = (bf16[1152,512]{1,0:T(8,128)(2,1)S(1)}, bf16[1152,512]{1,0:T(8,128)(2,1)S(1)}, u32[]{:S(2)}, u32[]{:S(2)}) collective-permute-start(bf16[1152,512]{1,0:T(8,128)(2,1)S(1)} %shard_map.247.refs_0_), channel_id=1, source_target_pairs={{0,2},{1,3},{2,0},{3,1},{4,6},{5,7},{6,4},{7,5},{8,10},{9,11},{10,... | collective-permute-start | bytes 3538952 | tf_op jit(solution)/shard_map/ppermute | solution.py:879
  172.9 4.5 %collective-permute-start.28 = (bf16[1152,512]{1,0:T(8,128)(2,1)S(1)}, bf16[1152,512]{1,0:T(8,128)(2,1)S(1)}, u32[]{:S(2)}, u32[]{:S(2)}) collective-permute-start(bf16[1152,512]{1,0:T(8,128)(2,1)S(1)} %collective-permute-done.21.refs_2_), channel_id=1, source_target_pairs={{0,2},{1,3},{2,0},{3,1},{4,6},{5,7},{6,4},{7,5},{8,10},{9,11},{10,... | collective-permute-start | bytes 3538952 | tf_op jit(solution)/shard_map/ppermute | solution.py:879
  173.4 8.7 %collective-permute-start.29 = (bf16[896,512]{1,0:T(8,128)(2,1)S(1)}, bf16[896,512]{1,0:T(8,128)(2,1)S(1)}, u32[]{:S(2)}, u32[]{:S(2)}) collective-permute-start(bf16[896,512]{1,0:T(8,128)(2,1)S(1)} %shard_map.250.refs_0_), channel_id=1, source_target_pairs={{0,2},{1,3},{2,0},{3,1},{4,6},{5,7},{6,4},{7,5},{8,10},{9,11},{10,... | collective-permute-start | bytes 2752520 | tf_op jit(solution)/shard_map/ppermute | solution.py:879
  173.5 13.4 %collective-permute-start.26 = (bf16[896,512]{1,0:T(8,128)(2,1)S(1)}, bf16[896,512]{1,0:T(8,128)(2,1)S(1)}, u32[]{:S(2)}, u32[]{:S(2)}) collective-permute-start(bf16[896,512]{1,0:T(8,128)(2,1)S(1)} %shard_map.250.refs_0_), channel_id=1, source_target_pairs={{0,4},{1,5},{2,3},{3,2},{4,0},{5,1},{6,7},{7,6},{8,12},{9,13},{10,... | collective-permute-start | bytes 2752520 | tf_op jit(solution)/shard_map/ppermute | solution.py:879
  186.9 2.5 %collective-permute-start.30 = (bf16[896,512]{1,0:T(8,128)(2,1)S(1)}, bf16[896,512]{1,0:T(8,128)(2,1)S(1)}, u32[]{:S(2)}, u32[]{:S(2)}) collective-permute-start(bf16[896,512]{1,0:T(8,128)(2,1)S(1)} %collective-permute-done.26.refs_0_), channel_id=1, source_target_pairs={{0,2},{1,3},{2,0},{3,1},{4,6},{5,7},{6,4},{7,5},{8,10},{9,11},{10,... | collective-permute-start | bytes 2752520 | tf_op jit(solution)/shard_map/ppermute | solution.py:879
  188.0 4.0 %copy-start.27 = (bf16[8,256,512]{2,1,0:T(8,128)(2,1)}, bf16[8,256,512]{2,1,0:T(8,128)(2,1)S(1)}, u32[]{:S(2)}) copy-start(bf16[8,256,512]{2,1,0:T(8,128)(2,1)S(1)} %constant_dynamic-update-slice_fusion) | copy-start | bytes 6291460
  (13 other events, 36.1 us)
where the time goes:
time: 194 us; the launch traced here: 192 us
  Pallas kernels  101 us (52%)
  waiting for transfers between devices  48.7 us (25%)
  starting transfers between devices  36.1 us (19%)
  local copies, waits for them, and re-layouts  4.87 us (3%)
    pallas_call x25, Pallas kernels, call(): pl.pallas_call(kernel, out_shape=[jax.ShapeDtypeStruct(shape, kind) for s...  101 us
    ppermute x28, waiting for transfers between devices, permute(): return lax.ppermute(array, ('dp', 'mem'), pairs)  47.1 us
    ppermute x28, starting transfers between devices, permute(): return lax.ppermute(array, ('dp', 'mem'), pairs)  30.8 us
  transfers between devices with their start and end apart: 31, of which 17 were waited for; matrix products, arithmetic and copies ran while one was open for 1% of the time, Pallas kernels for 36%

commit v1 on v0

--- a/solution.py
+++ b/solution.py
@@ -789,7 +789,9 @@
     size = outs[0].shape[0]
     outs[0][...] = tree_sum([rows_of(ref, 0, size) for ref in ins]).astype(BF16)
     if ln:
-        outs[1][...] = tree_sum([rows_of(ref, size, LN_ROWS) for ref in ins])
+        norms = tree_sum([rows_of(ref, size, LN_ROWS) for ref in ins])
+        outs[1][...] = norms[:3]
+        outs[2][...] = norms[3:6]
 
 
 def join_kernel(stage, spot_ref, *refs):
@@ -895,19 +897,19 @@
         kernel = functools.partial(first_split_kernel, len(arrays) // 2, self.ln, self.sizes[0])
         return call(kernel, self.messages(0), [((self.rows, self.width), BF16)], 1, spot, *arrays, work=0.01)
 
-    def split(self, stage, spot, arrays):
+    def split(self, stage, spot, arrays, work=0.01):
         kernel = functools.partial(split_kernel, stage, self.ln, self.sizes[stage - 1])
-        return call(kernel, self.messages(stage), [], 1, spot, *arrays, work=0.01)
-
-    def total(self, arrays):
+        return call(kernel, self.messages(stage), [], 1, spot, *arrays, work=work)
+
+    def total(self, arrays, work=0.01):
         outs = [((self.chunk, self.width), BF16)]
         if self.ln:
-            outs.append(((LN_ROWS, self.width), F32))
-        return call(functools.partial(total_kernel, self.ln, self.sizes[2]), outs, [], 0, *arrays, work=0.01)
-
-    def join(self, stage, spot, arrays):
+            outs = outs + [((3, self.width), F32)] * 2
+        return call(functools.partial(total_kernel, self.ln, self.sizes[2]), outs, [], 0, *arrays, work=work)
+
+    def join(self, stage, spot, arrays, work=0.01):
         outs = [((self.after(stage), self.width), BF16)]
-        return call(functools.partial(join_kernel, stage), outs, [], 1, spot, *arrays, work=0.01)[0]
+        return call(functools.partial(join_kernel, stage), outs, [], 1, spot, *arrays, work=work)[0]
 
     def finish(self, spot, mine, others, offsets, pieces, outs, held=()):
         kernel = functools.partial(finish_kernel, offsets, self.sizes[0], self.twisted, pieces, len(held))
@@ -1253,18 +1255,20 @@
         work=30,
         vmem=16,
     )
-    parts_one, parts_two, grad_away, grad_target = lax.optimization_barrier(
-        (parts_one, parts_two, grad_away, grad_target)
-    )
+    parts_one, grad_away, grad_target = lax.optimization_barrier((parts_one, grad_away, grad_target))
+    spread_one = first_sum.spread(2, first_sum.total(parts_one)[0])
     backs_early = send_back(grad_away)
     parts_two = second_sum.swap(second_sum.split(1, spot, parts_two), 1)
-    spread_one = first_sum.spread(2, first_sum.total(parts_one)[0])
-    parts_two, spread_one, backs_early = lax.optimization_barrier((parts_two, spread_one, backs_early))
-    spread_one = first_sum.spread(1, first_sum.join(2, spot, spread_one))
-    parts_two = second_sum.swap(second_sum.split(2, spot, parts_two), 2)
-    parts_two, spread_one = lax.optimization_barrier((parts_two, spread_one))
-    spread_one = first_sum.spread(0, first_sum.join(1, spot, spread_one))
-    sum_two, norm_sums = second_sum.total(parts_two)
+    joined_one = first_sum.join(2, spot, spread_one, work=0.01)
+    spread_one = first_sum.spread(1, joined_one)
+    parts_two, joined_one = lax.optimization_barrier((parts_two, joined_one))
+    parts_two = second_sum.split(2, spot, parts_two, work=0.01)
+    spread_one, _ = lax.optimization_barrier((spread_one, parts_two))
+    parts_two = second_sum.swap(parts_two, 2)
+    joined_one = first_sum.join(1, spot, spread_one)
+    spread_one = first_sum.spread(0, joined_one)
+    parts_two, joined_one, backs_early = lax.optimization_barrier((parts_two, joined_one, backs_early))
+    sum_two, *norm_sums = second_sum.total(parts_two, work=8)
     spread_two = second_sum.spread(2, sum_two)
     spread_two = second_sum.spread(1, second_sum.join(2, spot, spread_two))
     joined_two = second_sum.join(1, spot, spread_two)
@@ -1328,8 +1332,7 @@
         grad_wo,
         grad_w_up,
         grad_w_down,
-        norm_sums[:3],
-        norm_sums[3:6],
+        *norm_sums,
     )
 
 

time: 194 us -> 197 us (1.015)
    ppermute x2, waiting for transfers between devices: 0.09 us -> 9.75 us  [send_back(): lax.ppermute(array, 'mem', [(k, (k - 1 - i) % groups) for k in range(grou...]
    ppermute x28, waiting for transfers between devices: 47.1 us -> 37.9 us  [permute(): return lax.ppermute(array, ('dp', 'mem'), pairs)]
    ppermute x28, starting transfers between devices: 30.8 us -> 33.7 us  [permute(): return lax.ppermute(array, ('dp', 'mem'), pairs)]
  transfers between devices with their start and end apart: 31 -> 31, of which waited for: 17 -> 15; matrix products, arithmetic and copies ran while one was open for 1% -> 1% of each run, Pallas kernels for 36% -> 36%
where the time goes in v1:
time: 197 us; the launch traced here: 194 us
  Pallas kernels  102 us (52%)
  waiting for transfers between devices  49.1 us (25%)
  starting transfers between devices  37.4 us (19%)
  local copies, waits for them, and re-layouts  4.3 us (2%)
    pallas_call x25, Pallas kernels, call(): pl.pallas_call(kernel, out_shape=[jax.ShapeDtypeStruct(shape, kind) for s...  102 us
    ppermute x28, waiting for transfers between devices, permute(): return lax.ppermute(array, ('dp', 'mem'), pairs)  37.9 us
    ppermute x28, starting transfers between devices, permute(): return lax.ppermute(array, ('dp', 'mem'), pairs)  33.7 us
    ppermute x2, waiting for transfers between devices, send_back(): lax.ppermute(array, 'mem', [(k, (k - 1 - i) % groups) for k in range(grou...  9.75 us
  transfers between devices with their start and end apart: 31, of which 15 were waited for; matrix products, arithmetic and copies ran while one was open for 1% of the time, Pallas kernels for 36%

profile of v1, /device:TPU:0, one launch (start us, length us, event | category | flops | bytes accessed | tf_op | source)
XLA Modules:
  0.0 194.1 jit_solution(12991406355971867791)
XLA Ops:
  0.7 1.3 constant_dynamic-slice_fusion
  2.0 3.0 %collective-permute-start = (bf16[4,256,512]{2,1,0:T(8,128)(2,1)S(1)}, bf16[4,256,512]{2,1,0:T(8,128)(2,1)S(1)}, u32[]{:S(2)}, u32[]{:S(2)}) collective-permute-start(bf16[4,256,512]{2,1,0:T(8,128)(2,1)S(1)} %constant_dynamic-slice_fusion), channel_id=1, source_target_pairs={{0,1},{1,0},{2,3},{3,2},{4,5},{5,4},{6,7},{7,6},{8,9},{9,8},{10,11... | collective-permute-start | bytes 3145736 | tf_op jit(solution)/shard_map/ppermute | solution.py:1057
  5.7 21.1 %shard_map.229 = (bf16[512,512]{1,0:T(8,128)(2,1)}, bf16[512,1536]{1,0:T(8,128)(2,1)}, f32[16,256]{1,0:T(8,128)}, bf16[512,512]{1,0:T(8,128)(2,1)}, f32[512,512]...) custom-call(s32[5]{0:T(128)} %stack.23.me_ref.refs_0_.spot_ref, ...), custom_call_target="tpu_custom_call" | custom-call | flops 500000000 | bytes 1500000 | tf_op jit(solution)/shard_map/pallas_call | solution.py:947
  26.7 1.4 collective-permute-done.refs_11_.refs_0_
  28.2 1.0 copy-done.4
  29.1 26.4 %shard_map.230 = (bf16[512,512]{1,0:T(8,128)(2,1)}, f32[16,256]{1,0:T(8,128)}, f32[16,256]{1,0:T(8,128)}, f32[512,512]{1,0:T(8,128)}, bf16[512,512]{1,0:T(8,128)...) custom-call(s32[5]{0:T(128)} %stack.23.me_ref.refs_0_.spot_ref, ...), custom_call_target="tpu_custom_call", output_to_operand_aliasing={{8}: (16, {})} | custom-call | flops 500000000 | bytes 1500000 | tf_op jit(solution)/shard_map/pallas_call | solution.py:947
  55.6 6.3 %shard_map.231 = (bf16[1,512,1024]{2,1,0:T(8,128)(2,1)}, bf16[512,256]{1,0:T(8,128)(2,1)}) custom-call(s32[5]{0:T(128)} %stack.23.me_ref.refs_0_.spot_ref, s32[2,4]{1,0:T(2,128)} %len_ref.15, s32[2,4]{1,0:T(2,128)} %src_ref.5, bf16[512,512]{1,0:T(8,128)(2,1)} %get-tuple-element.134.refs_4_.query_ref, f32[16,256]{1,0:T(8,128)} %get-tuple-element.142.norm_ref, ...), custom_call_target="tpu_custom_call" | custom-call | flops 10000000000 | bytes 30000000 | tf_op jit(solution)/shard_map/pallas_call | solution.py:947
  62.0 2.0 %shard_map.232 = (bf16[1152,512]{1,0:T(8,128)(2,1)S(1)}, bf16[1152,512]{1,0:T(8,128)(2,1)S(1)}) custom-call(s32[5]{0:T(128)S(1)} %copy-done.17, bf16[2304,512]{1,0:T(8,128)(2,1)S(1)} %copy-done.7, bf16[2304,512]{1,0:T(8,128)(2,1)S(1)} %collective-permute-done.1.refs_1_), custom_call_target="tpu_custom_call" | custom-call | flops 10000000 | bytes 30000 | tf_op jit(solution)/shard_map/pallas_call | solution.py:947
  64.0 1.8 collective-permute-start.2
  65.9 8.0 %shard_map.233 = (bf16[3,512,1024]{2,1,0:T(8,128)(2,1)S(1)}, bf16[512,256]{1,0:T(8,128)(2,1)S(1)}) custom-call(s32[5]{0:T(128)S(1)} %copy-done.17, s32[2,4]{1,0:T(2,128)S(1)} %copy-done.20, s32[2,4]{1,0:T(2,128)S(1)} %copy-done.23, bf16[512,512]{1,0:T(8,128)(2,1)S(1)} %copy-done.15, f32[16,256]{1,0:T(8,128)S(1)} %copy-done.25, f32[16,256]{1,0:T(8,128)S(1)} %copy-done.26, ...), custom_call_target="tpu_custom_call" | custom-call | flops 10000000000 | bytes 30000000 | tf_op jit(solution)/shard_map/pallas_call | solution.py:947
  74.1 2.9 %shard_map.234.wkv_grad_ref = bf16[2,512,512]{2,1,0:T(8,128)(2,1)S(1)} custom-call(s32[5]{0:T(128)S(1)} %copy-done.17, s32[2,4]{1,0:T(2,128)S(1)} %copy-done.20, bf16[1,512,1024]{2,1,0:T(8,128)(2,1)S(1)} %copy-done.2, bf16[3,512,1024]{2,1,0:T(8,128)(2,1)S(1)} %get-tuple-element.159.pair_grad_rest_ref, bf16[8,256,512]{2,1,0:T(8,128)(2,1)S(1)} %copy-done.1, ...), custom_call_target="tpu_custom_call" | custom-call | flops 1000000000 | bytes 3000000 | tf_op jit(solution)/shard_map/pallas_call | solution.py:947
  77.1 3.1 %shard_map.235 = (bf16[1040,512]{1,0:T(8,128)(2,1)S(1)}, bf16[1040,512]{1,0:T(8,128)(2,1)S(1)}, f32[512,512]{1,0:T(8,128)S(1)}, bf16[512,512]{1,0:T(8,128)(2,1)S(1)}) custom-call(s32[5]{0:T(128)S(1)} %copy-done.17, f32[512,512]{1,0:T(8,128)S(1)} %copy-done.6, bf16[512,256]{1,0:T(8,128)(2,1)S(1)} %copy-done.16, ...), custom_call_target="tpu_custom_call" | custom-call | flops 100000000 | bytes 300000 | tf_op jit(solution)/shard_map/pallas_call | solution.py:947
  80.5 0.8 shard_map.236
  81.4 1.6 collective-permute-start.3
  83.0 2.1 %shard_map.237 = bf16[4,128,512]{2,1,0:T(8,128)(2,1)S(1)} custom-call(s32[5]{0:T(128)S(1)} %copy-done.17, s32[2,4]{1,0:T(2,128)S(1)} %copy-done.20, bf16[1,512,1024]{2,1,0:T(8,128)(2,1)S(1)} %copy-done.2, bf16[3,512,1024]{2,1,0:T(8,128)(2,1)S(1)} %get-tuple-element.159.pair_grad_rest_ref, bf16[512,1024]{1,0:T(8,128)(2,1)S(1)} %copy-done), custom_call_target="tpu_custom_call" | custom-call | flops 10000000 | bytes 30000 | tf_op jit(solution)/shard_map/pallas_call | solution.py:947
  85.6 6.5 %shard_map.238 = (bf16[512,1536]{1,0:T(8,128)(2,1)S(1)}, bf16[384,512]{1,0:T(8,128)(2,1)S(1)}, bf16[384,512]{1,0:T(8,128)(2,1)S(1)}, bf16[384,512]{1,0:T(8,128)(2,1)S(1)}, bf16[384,512]{1,0:T(8,128)(2,1)S(1)}) custom-call(s32[5]{0:T(128)S(1)} %copy-done.17, s32[2,4]{1,0:T(2,128)S(1)} %copy-done.20, bf16[512,1536]{1,0:T(8,128)(2,1)S(1)} %copy-done.11, ...), custom_call_target="tpu_custom_call" | custom-call | flops 100000000 | bytes 300000 | tf_op jit(solution)/shard_map/pallas_call | solution.py:947
  92.1 3.0 %collective-permute-done.3.refs_1_ = bf16[576,512]{1,0:T(8,128)(2,1)S(1)} collective-permute-done((bf16[576,512]{1,0:T(8,128)(2,1)S(1)}, bf16[576,512]{1,0:T(8,128)(2,1)S(1)}, u32[]{:S(2)}, u32[]{:S(2)}) %collective-permute-start.3) | collective-permute-done | bytes 589856 | tf_op jit(solution)/shard_map/ppermute | solution.py:881
  96.4 1.7 collective-permute-start.5
  98.1 2.6 %collective-permute-start.6 = (bf16[144,512]{1,0:T(8,128)(2,1)S(1)}, bf16[144,512]{1,0:T(8,128)(2,1)S(1)}, u32[]{:S(2)}, u32[]{:S(2)}) collective-permute-start(bf16[144,512]{1,0:T(8,128)(2,1)S(1)} %get-tuple-element.188), channel_id=1, source_target_pairs={{0,16},{1,17},{2,18},{3,19},{4,20},{5,21},{6,22},{7,23},{8,24},{9,... | collective-permute-start | bytes 442376 | tf_op jit(solution)/shard_map/ppermute | solution.py:881
  100.9 1.6 shard_map.240
  102.6 2.2 %collective-permute-start.11 = (bf16[912,512]{1,0:T(8,128)(2,1)S(1)}, bf16[912,512]{1,0:T(8,128)(2,1)S(1)}, u32[]{:S(2)}, u32[]{:S(2)}) collective-permute-start(bf16[912,512]{1,0:T(8,128)(2,1)S(1)} %get-tuple-element.208), channel_id=1, source_target_pairs={{0,4},{1,5},{2,3},{3,2},{4,0},{5,1},{6,7},{7,6},{8,12},{9,13},{10,... | collective-permute-start | bytes 2801672 | tf_op jit(solution)/shard_map/ppermute | solution.py:881
  104.8 2.7 %shard_map.242 = bf16[512,512]{1,0:T(8,128)(2,1)} custom-call(s32[5]{0:T(128)S(1)} %copy-done.17, s32[2,4]{1,0:T(2,128)S(1)} %copy-done.20, bf16[512,1536]{1,0:T(8,128)(2,1)S(1)} %get-tuple-element.203.grad_triple_ref, bf16[512,1536]{1,0:T(8,128)(2,1)S(1)} %copy-done.10, f32[512,512]{1,0:T(8,128)S(1)} %get-tuple-element.204.grad_hidden_ref), custom_call_target="tpu_custom_call" | custom-call | flops 30000001024 | bytes 90000000 | tf_op jit(solution)/shard_map/pallas_call | solution.py:947
  107.5 3.1 %shard_map.241 = (bf16[4,256,512]{2,1,0:T(8,128)(2,1)S(1)}, bf16[4,128,512]{2,1,0:T(8,128)(2,1)S(1)}) custom-call(s32[5]{0:T(128)S(1)} %copy-done.17, s32[2,4]{1,0:T(2,128)S(1)} %copy-done.20, bf16[1,512,1024]{2,1,0:T(8,128)(2,1)S(1)} %copy-done.2, bf16[3,512,1024]{2,1,0:T(8,128)(2,1)S(1)} %get-tuple-element.159.pair_grad_rest_ref, bf16[512,1024]{1,0:T(8,128)(2,1)S(1)} %copy-done), custom_call_target="tpu_custom_call" | custom-call | flops 10000000 | bytes 30000 | tf_op jit(solution)/shard_map/pallas_call | solution.py:947
  110.7 1.4 collective-permute-done.6.refs_2_
  112.2 2.4 %collective-permute-start.15 = (bf16[144,512]{1,0:T(8,128)(2,1)S(1)}, bf16[144,512]{1,0:T(8,128)(2,1)S(1)}, u32[]{:S(2)}, u32[]{:S(2)}) collective-permute-start(bf16[144,512]{1,0:T(8,128)(2,1)S(1)} %shard_map.244.refs_0_), channel_id=1, source_target_pairs={{0,24},{1,25},{2,26},{3,27},{4,28},{5,29},{6,30},{7,31},{8,16},{9,... | collective-permute-start | bytes 442376 | tf_op jit(solution)/shard_map/ppermute | solution.py:881
  114.6 1.6 collective-permute-start.14
  117.4 1.9 collective-permute-start.12
  119.3 1.3 collective-permute-done.15.refs_3_
  120.6 6.3 %collective-permute-done.14.refs_2_ = bf16[144,512]{1,0:T(8,128)(2,1)S(1)} collective-permute-done((bf16[144,512]{1,0:T(8,128)(2,1)S(1)}, bf16[144,512]{1,0:T(8,128)(2,1)S(1)}, u32[]{:S(2)}, u32[]{:S(2)}) %collective-permute-start.14) | collective-permute-done | bytes 147488 | tf_op jit(solution)/shard_map/ppermute | solution.py:881
  127.6 2.0 %collective-permute-start.19 = (bf16[576,512]{1,0:T(8,128)(2,1)S(1)}, bf16[576,512]{1,0:T(8,128)(2,1)S(1)}, u32[]{:S(2)}, u32[]{:S(2)}) collective-permute-start(bf16[576,512]{1,0:T(8,128)(2,1)S(1)} %shard_map.245.refs_0_), channel_id=1, source_target_pairs={{0,1},{1,0},{2,6},{3,7},{4,5},{5,4},{6,2},{7,3},{8,9},{9,8},{10,14... | collective-permute-start | bytes 1769480 | tf_op jit(solution)/shard_map/ppermute | solution.py:881
  130.6 3.4 %collective-permute-start.17 = (bf16[128,512]{1,0:T(8,128)(2,1)S(1)}, bf16[128,512]{1,0:T(8,128)(2,1)S(1)}, u32[]{:S(2)}, u32[]{:S(2)}) collective-permute-start(bf16[128,512]{1,0:T(8,128)(2,1)S(1)} %get-tuple-element.219), channel_id=1, source_target_pairs={{0,16},{1,17},{2,18},{3,19},{4,20},{5,21},{6,22},{7,23},{8,24},{9,... | collective-permute-start | bytes 393224 | tf_op jit(solution)/shard_map/ppermute | solution.py:881
  134.0 0.8 collective-permute-start.18
  134.8 9.1 %collective-permute-done.19.refs_1_ = bf16[576,512]{1,0:T(8,128)(2,1)S(1)} collective-permute-done((bf16[576,512]{1,0:T(8,128)(2,1)S(1)}, bf16[576,512]{1,0:T(8,128)(2,1)S(1)}, u32[]{:S(2)}, u32[]{:S(2)}) %collective-permute-start.19) | collective-permute-done | bytes 589856 | tf_op jit(solution)/shard_map/ppermute | solution.py:881
  144.5 1.0 collective-permute-start.21
  145.4 9.6 %collective-permute-done.20 = bf16[4,128,512]{2,1,0:T(8,128)(2,1)S(1)} collective-permute-done((bf16[4,128,512]{2,1,0:T(8,128)(2,1)S(1)}, bf16[4,128,512]{2,1,0:T(8,128)(2,1)S(1)}, u32[]{:S(2)}, u32[]{:S(2)}) %collective-permute-start.20) | collective-permute-done | bytes 524320 | tf_op jit(solution)/shard_map/ppermute | solution.py:1194
  155.9 3.0 %collective-permute-start.24 = (bf16[112,512]{1,0:T(8,128)(2,1)S(1)}, bf16[112,512]{1,0:T(8,128)(2,1)S(1)}, u32[]{:S(2)}, u32[]{:S(2)}) collective-permute-start(bf16[112,512]{1,0:T(8,128)(2,1)S(1)} %get-tuple-element.230.refs_0_), channel_id=1, source_target_pairs={{0,24},{1,25},{2,26},{3,27},{4,28},{5,29},{6,30},{7,31},{8,16},{9,... | collective-permute-start | bytes 344072 | tf_op jit(solution)/shard_map/ppermute | solution.py:881
  158.9 1.4 collective-permute-start.22
  160.3 2.2 %collective-permute-done.24.refs_3_ = bf16[112,512]{1,0:T(8,128)(2,1)S(1)} collective-permute-done((bf16[112,512]{1,0:T(8,128)(2,1)S(1)}, bf16[112,512]{1,0:T(8,128)(2,1)S(1)}, u32[]{:S(2)}, u32[]{:S(2)}) %collective-permute-start.24) | collective-permute-done | bytes 114720 | tf_op jit(solution)/shard_map/ppermute | solution.py:881
  162.5 2.5 %collective-permute-done.23.refs_2_ = bf16[112,512]{1,0:T(8,128)(2,1)S(1)} collective-permute-done((bf16[112,512]{1,0:T(8,128)(2,1)S(1)}, bf16[112,512]{1,0:T(8,128)(2,1)S(1)}, u32[]{:S(2)}, u32[]{:S(2)}) %collective-permute-start.23) | collective-permute-done | bytes 114720 | tf_op jit(solution)/shard_map/ppermute | solution.py:881
  165.5 2.0 %collective-permute-start.25 = (bf16[448,512]{1,0:T(8,128)(2,1)S(1)}, bf16[448,512]{1,0:T(8,128)(2,1)S(1)}, u32[]{:S(2)}, u32[]{:S(2)}) collective-permute-start(bf16[448,512]{1,0:T(8,128)(2,1)S(1)} %shard_map.249.refs_0_), channel_id=1, source_target_pairs={{0,1},{1,0},{2,6},{3,7},{4,5},{5,4},{6,2},{7,3},{8,9},{9,8},{10,14... | collective-permute-start | bytes 1376264 | tf_op jit(solution)/shard_map/ppermute | solution.py:881
  167.5 6.5 %collective-permute-done.25.refs_1_ = bf16[448,512]{1,0:T(8,128)(2,1)S(1)} collective-permute-done((bf16[448,512]{1,0:T(8,128)(2,1)S(1)}, bf16[448,512]{1,0:T(8,128)(2,1)S(1)}, u32[]{:S(2)}, u32[]{:S(2)}) %collective-permute-start.25) | collective-permute-done | bytes 458784 | tf_op jit(solution)/shard_map/ppermute | solution.py:881
  175.3 1.9 collective-permute-start.26
  177.6 1.7 collective-permute-done.28.refs_3_
  179.3 4.7 %shard_map.251 = (f32[2048,512]{1,0:T(8,128)}, f32[512,2048]{1,0:T(8,128)}, f32[512,512]{1,0:T(8,128)}) custom-call(s32[5]{0:T(128)S(1)} %copy-done.17, bf16[1152,512]{1,0:T(8,128)(2,1)S(1)} %shard_map.247.refs_0_, bf16[1152,512]{1,0:T(8,128)(2,1)S(1)} %collective-permute-done.27.refs_1_, bf16[1152,512]{1,0:T(8,128)(2,1)S(1)} %collective-permute-done.21.refs_2_, ...), custom_call_target="tpu_custom_call" | custom-call | flops 1000000000 | bytes 3000000 | tf_op jit(solution)/shard_map/pallas_call | solution.py:947
  184.0 2.6 %shard_map.252 = (f32[512,512]{1,0:T(8,128)}, f32[512,1024]{1,0:T(8,128)}, f32[512,1536]{1,0:T(8,128)}, f32[512,512]{1,0:T(8,128)}) custom-call(s32[5]{0:T(128)S(1)} %copy-done.17, bf16[896,512]{1,0:T(8,128)(2,1)S(1)} %shard_map.250.refs_0_, bf16[896,512]{1,0:T(8,128)(2,1)S(1)} %collective-permute-done.29.refs_1_), custom_call_target="tpu_custom_call" | custom-call | flops 1000000000 | bytes 3000000 | tf_op jit(solution)/shard_map/pallas_call | solution.py:947
  186.6 2.1 %collective-permute-done.26.refs_0_ = bf16[896,512]{1,0:T(8,128)(2,1)S(1)} collective-permute-done((bf16[896,512]{1,0:T(8,128)(2,1)S(1)}, bf16[896,512]{1,0:T(8,128)(2,1)S(1)}, u32[]{:S(2)}, u32[]{:S(2)}) %collective-permute-start.26) | collective-permute-done | bytes 917536 | tf_op jit(solution)/shard_map/ppermute | solution.py:881
  189.9 1.3 collective-permute-done.30.refs_1_
  191.2 2.6 %shard_map.253 = (f32[512,512]{1,0:T(8,128)}, f32[512,1024]{1,0:T(8,128)}, f32[512,1536]{1,0:T(8,128)}, f32[512,512]{1,0:T(8,128)}) custom-call(s32[5]{0:T(128)S(1)} %copy-done.17, bf16[896,512]{1,0:T(8,128)(2,1)S(1)} %collective-permute-done.26.refs_0_, ...), custom_call_target="tpu_custom_call", output_to_operand_aliasing={{0}: (3, {}), {1}: (4, {}), {2}: (5, {}), {3}: (6, {})} | custom-call | flops 1000000000 | bytes 3000000 | tf_op jit(solution)/shard_map/pallas_call | solution.py:947
  (105 shorter events, 10.9 us)
Async XLA Ops:
  2.0 26.2 %collective-permute-start = (bf16[4,256,512]{2,1,0:T(8,128)(2,1)S(1)}, bf16[4,256,512]{2,1,0:T(8,128)(2,1)S(1)}, u32[]{:S(2)}, u32[]{:S(2)}) collective-permute-start(bf16[4,256,512]{2,1,0:T(8,128)(2,1)S(1)} %constant_dynamic-slice_fusion), channel_id=1, source_target_pairs={{0,1},{1,0},{2,3},{3,2},{4,5},{5,4},{6,7},{7,6},{8,9},{9,8},{10,11... | collective-permute-start | bytes 3145736 | tf_op jit(solution)/shard_map/ppermute | solution.py:1057
  55.5 6.5 %collective-permute-start.1 = (bf16[2304,512]{1,0:T(8,128)(2,1)}, bf16[2304,512]{1,0:T(8,128)(2,1)S(1)}, u32[]{:S(2)}, u32[]{:S(2)}) collective-permute-start(bf16[2304,512]{1,0:T(8,128)(2,1)} %get-tuple-element.141), channel_id=1, source_target_pairs={{0,2},{1,3},{2,0},{3,1},{4,6},{5,7},{6,4},{7,5},{8,10},{9,11},{10,... | collective-permute-start | bytes 7077896 | tf_op jit(solution)/shard_map/ppermute | solution.py:881
  55.6 6.4 %copy-start.7 = (bf16[2304,512]{1,0:T(8,128)(2,1)S(1)}, bf16[2304,512]{1,0:T(8,128)(2,1)}, u32[]{:S(2)}) copy-start(bf16[2304,512]{1,0:T(8,128)(2,1)} %get-tuple-element.140.refs_0_) | copy-start | bytes 7077892
  55.6 6.4 %copy-start.17 = (s32[5]{0:T(128)S(1)}, s32[5]{0:T(128)}, u32[]{:S(2)}) copy-start(s32[5]{0:T(128)} %stack.23.me_ref.refs_0_.spot_ref) | copy-start | bytes 64
  55.6 10.2 %copy-start.24 = (bf16[512,512]{1,0:T(8,128)(2,1)S(1)}, bf16[512,512]{1,0:T(8,128)(2,1)}, u32[]{:S(2)}) copy-start(bf16[512,512]{1,0:T(8,128)(2,1)} %get-tuple-element.144.grad_attn_ref) | copy-start | bytes 1572868
  55.6 10.2 %copy-start.25 = (f32[16,256]{1,0:T(8,128)S(1)}, f32[16,256]{1,0:T(8,128)}, u32[]{:S(2)}) copy-start(f32[16,256]{1,0:T(8,128)} %get-tuple-element.142.norm_ref) | copy-start | bytes 49156
  55.6 10.2 %copy-start.26 = (f32[16,256]{1,0:T(8,128)S(1)}, f32[16,256]{1,0:T(8,128)}, u32[]{:S(2)}) copy-start(f32[16,256]{1,0:T(8,128)} %get-tuple-element.143.along_ref) | copy-start | bytes 49156
  62.0 3.8 %copy-start.3 = (bf16[4,512,1024]{2,1,0:T(8,128)(2,1)S(1)}, bf16[4,512,1024]{2,1,0:T(8,128)(2,1)}, u32[]{:S(2)}) copy-start(bf16[4,512,1024]{2,1,0:T(8,128)(2,1)} %get-tuple-element.153.pair_hbm) | copy-start | bytes 12582916
  62.0 3.8 %copy-start.15 = (bf16[512,512]{1,0:T(8,128)(2,1)S(1)}, bf16[512,512]{1,0:T(8,128)(2,1)}, u32[]{:S(2)}) copy-start(bf16[512,512]{1,0:T(8,128)(2,1)} %get-tuple-element.134.refs_4_.query_ref) | copy-start | bytes 1572868
  62.0 3.8 %copy-start.20 = (s32[2,4]{1,0:T(2,128)S(1)}, s32[2,4]{1,0:T(2,128)}, u32[]{:S(2)}) copy-start(s32[2,4]{1,0:T(2,128)} %len_ref.15) | copy-start | bytes 100
  62.0 3.8 %copy-start.23 = (s32[2,4]{1,0:T(2,128)S(1)}, s32[2,4]{1,0:T(2,128)}, u32[]{:S(2)}) copy-start(s32[2,4]{1,0:T(2,128)} %src_ref.5) | copy-start | bytes 100
  64.0 9.9 %copy-start.1 = (bf16[8,256,512]{2,1,0:T(8,128)(2,1)S(1)}, bf16[8,256,512]{2,1,0:T(8,128)(2,1)}, u32[]{:S(2)}) copy-start(bf16[8,256,512]{2,1,0:T(8,128)(2,1)} %memory_ref.3) | copy-start | bytes 6291460
  64.0 9.9 %copy-start.2 = (bf16[1,512,1024]{2,1,0:T(8,128)(2,1)S(1)}, bf16[1,512,1024]{2,1,0:T(8,128)(2,1)}, u32[]{:S(2)}) copy-start(bf16[1,512,1024]{2,1,0:T(8,128)(2,1)} %get-tuple-element.200.pair_grad_long_ref) | copy-start | bytes 3145732
  64.0 9.9 %copy-start.5 = (bf16[4,256,512]{2,1,0:T(8,128)(2,1)S(1)}, bf16[4,256,512]{2,1,0:T(8,128)(2,1)}, u32[]{:S(2)}) copy-start(bf16[4,256,512]{2,1,0:T(8,128)(2,1)} %copy-done.4) | copy-start | bytes 3145732
  64.0 16.5 %collective-permute-start.2 = (bf16[1152,512]{1,0:T(8,128)(2,1)S(1)}, bf16[1152,512]{1,0:T(8,128)(2,1)S(1)}, u32[]{:S(2)}, u32[]{:S(2)}) collective-permute-start(bf16[1152,512]{1,0:T(8,128)(2,1)S(1)} %get-tuple-element.151), channel_id=1, source_target_pairs={{0,4},{1,5},{2,3},{3,2},{4,0},{5,1},{6,7},{7,6},{8,12},{9,13},{10,... | collective-permute-start | bytes 3538952 | tf_op jit(solution)/shard_map/ppermute | solution.py:881
  80.2 12.0 %collective-permute-start.4 = (bf16[1040,512]{1,0:T(8,128)(2,1)S(1)}, bf16[1040,512]{1,0:T(8,128)(2,1)S(1)}, u32[]{:S(2)}, u32[]{:S(2)}) collective-permute-start(bf16[1040,512]{1,0:T(8,128)(2,1)S(1)} %get-tuple-element.178), channel_id=1, source_target_pairs={{0,2},{1,3},{2,0},{3,1},{4,6},{5,7},{6,4},{7,5},{8,10},{9,11},{10,... | collective-permute-start | bytes 3194888 | tf_op jit(solution)/shard_map/ppermute | solution.py:881
  81.3 4.3 %copy-start.11 = (bf16[512,1536]{1,0:T(8,128)(2,1)S(1)}, bf16[512,1536]{1,0:T(8,128)(2,1)}, u32[]{:S(2)}) copy-start(bf16[512,1536]{1,0:T(8,128)(2,1)} %get-tuple-element.168.qkv_ref) | copy-start | bytes 4718596
  81.4 4.2 %copy-start.13 = (bf16[512,512]{1,0:T(8,128)(2,1)S(1)}, bf16[512,512]{1,0:T(8,128)(2,1)}, u32[]{:S(2)}) copy-start(bf16[512,512]{1,0:T(8,128)(2,1)} %get-tuple-element.173.sorted_ref) | copy-start | bytes 1572868
  81.4 4.2 %copy-start.21 = (f32[16,256]{1,0:T(8,128)S(1)}, f32[16,256]{1,0:T(8,128)}, u32[]{:S(2)}) copy-start(f32[16,256]{1,0:T(8,128)} %get-tuple-element.169.norm_ref) | copy-start | bytes 49156
  81.4 13.8 %collective-permute-start.3 = (bf16[576,512]{1,0:T(8,128)(2,1)S(1)}, bf16[576,512]{1,0:T(8,128)(2,1)S(1)}, u32[]{:S(2)}, u32[]{:S(2)}) collective-permute-start(bf16[576,512]{1,0:T(8,128)(2,1)S(1)} %get-tuple-element.167), channel_id=1, source_target_pairs={{0,1},{1,0},{2,6},{3,7},{4,5},{5,4},{6,2},{7,3},{8,9},{9,8},{10,14... | collective-permute-start | bytes 1769480 | tf_op jit(solution)/shard_map/ppermute | solution.py:881
  85.1 17.5 %collective-permute-start.10 = (bf16[4,128,512]{2,1,0:T(8,128)(2,1)S(1)}, bf16[4,128,512]{2,1,0:T(8,128)(2,1)S(1)}, u32[]{:S(2)}, u32[]{:S(2)}) collective-permute-start(bf16[4,128,512]{2,1,0:T(8,128)(2,1)S(1)} %shard_map.237), channel_id=1, source_target_pairs={{0,1},{1,0},{2,3},{3,2},{4,5},{5,4},{6,7},{7,6},{8,9},{9,8},{10,11... | collective-permute-start | bytes 1572872 | tf_op jit(solution)/shard_map/ppermute | solution.py:1194
  95.2 5.5 %collective-permute-start.8 = (bf16[384,512]{1,0:T(8,128)(2,1)S(1)}, bf16[384,512]{1,0:T(8,128)(2,1)S(1)}, u32[]{:S(2)}, u32[]{:S(2)}) collective-permute-start(bf16[384,512]{1,0:T(8,128)(2,1)S(1)} %get-tuple-element.193), channel_id=1, source_target_pairs={{0,2},{1,3},{2,0},{3,1},{4,6},{5,7},{6,4},{7,5},{8,10},{9,11},{10,... | collective-permute-start | bytes 1179656 | tf_op jit(solution)/shard_map/ppermute | solution.py:881
  95.2 5.7 %collective-permute-start.9 = (bf16[384,512]{1,0:T(8,128)(2,1)S(1)}, bf16[384,512]{1,0:T(8,128)(2,1)S(1)}, u32[]{:S(2)}, u32[]{:S(2)}) collective-permute-start(bf16[384,512]{1,0:T(8,128)(2,1)S(1)} %get-tuple-element.195), channel_id=1, source_target_pairs={{0,2},{1,3},{2,0},{3,1},{4,6},{5,7},{6,4},{7,5},{8,10},{9,11},{10,... | collective-permute-start | bytes 1179656 | tf_op jit(solution)/shard_map/ppermute | solution.py:881
  96.4 8.4 %copy-start.10 = (bf16[512,1536]{1,0:T(8,128)(2,1)S(1)}, bf16[512,1536]{1,0:T(8,128)(2,1)}, u32[]{:S(2)}) copy-start(bf16[512,1536]{1,0:T(8,128)(2,1)} %w_qkv_ref.3) | copy-start | bytes 4718596
  96.4 14.3 %collective-permute-start.5 = (bf16[144,512]{1,0:T(8,128)(2,1)S(1)}, bf16[144,512]{1,0:T(8,128)(2,1)S(1)}, u32[]{:S(2)}, u32[]{:S(2)}) collective-permute-start(bf16[144,512]{1,0:T(8,128)(2,1)S(1)} %get-tuple-element.187), channel_id=1, source_target_pairs={{0,8},{1,9},{2,10},{3,11},{4,12},{5,13},{6,14},{7,15},{8,0},{9,1},... | collective-permute-start | bytes 442376 | tf_op jit(solution)/shard_map/ppermute | solution.py:881
  98.1 14.0 %collective-permute-start.6 = (bf16[144,512]{1,0:T(8,128)(2,1)S(1)}, bf16[144,512]{1,0:T(8,128)(2,1)S(1)}, u32[]{:S(2)}, u32[]{:S(2)}) collective-permute-start(bf16[144,512]{1,0:T(8,128)(2,1)S(1)} %get-tuple-element.188), channel_id=1, source_target_pairs={{0,16},{1,17},{2,18},{3,19},{4,20},{5,21},{6,22},{7,23},{8,24},{9,... | collective-permute-start | bytes 442376 | tf_op jit(solution)/shard_map/ppermute | solution.py:881
  100.7 11.4 %collective-permute-start.7 = (bf16[144,512]{1,0:T(8,128)(2,1)S(1)}, bf16[144,512]{1,0:T(8,128)(2,1)S(1)}, u32[]{:S(2)}, u32[]{:S(2)}) collective-permute-start(bf16[144,512]{1,0:T(8,128)(2,1)S(1)} %get-tuple-element.189), channel_id=1, source_target_pairs={{0,24},{1,25},{2,26},{3,27},{4,28},{5,29},{6,30},{7,31},{8,16},{9,... | collective-permute-start | bytes 442376 | tf_op jit(solution)/shard_map/ppermute | solution.py:881
  102.6 14.1 %collective-permute-start.11 = (bf16[912,512]{1,0:T(8,128)(2,1)S(1)}, bf16[912,512]{1,0:T(8,128)(2,1)S(1)}, u32[]{:S(2)}, u32[]{:S(2)}) collective-permute-start(bf16[912,512]{1,0:T(8,128)(2,1)S(1)} %get-tuple-element.208), channel_id=1, source_target_pairs={{0,4},{1,5},{2,3},{3,2},{4,0},{5,1},{6,7},{7,6},{8,12},{9,13},{10,... | collective-permute-start | bytes 2801672 | tf_op jit(solution)/shard_map/ppermute | solution.py:881
  112.2 8.4 %collective-permute-start.15 = (bf16[144,512]{1,0:T(8,128)(2,1)S(1)}, bf16[144,512]{1,0:T(8,128)(2,1)S(1)}, u32[]{:S(2)}, u32[]{:S(2)}) collective-permute-start(bf16[144,512]{1,0:T(8,128)(2,1)S(1)} %shard_map.244.refs_0_), channel_id=1, source_target_pairs={{0,24},{1,25},{2,26},{3,27},{4,28},{5,29},{6,30},{7,31},{8,16},{9,... | collective-permute-start | bytes 442376 | tf_op jit(solution)/shard_map/ppermute | solution.py:881
  114.6 12.4 %collective-permute-start.14 = (bf16[144,512]{1,0:T(8,128)(2,1)S(1)}, bf16[144,512]{1,0:T(8,128)(2,1)S(1)}, u32[]{:S(2)}, u32[]{:S(2)}) collective-permute-start(bf16[144,512]{1,0:T(8,128)(2,1)S(1)} %shard_map.244.refs_0_), channel_id=1, source_target_pairs={{0,16},{1,17},{2,18},{3,19},{4,20},{5,21},{6,22},{7,23},{8,24},{9,... | collective-permute-start | bytes 442376 | tf_op jit(solution)/shard_map/ppermute | solution.py:881
  116.2 10.8 %collective-permute-start.13 = (bf16[144,512]{1,0:T(8,128)(2,1)S(1)}, bf16[144,512]{1,0:T(8,128)(2,1)S(1)}, u32[]{:S(2)}, u32[]{:S(2)}) collective-permute-start(bf16[144,512]{1,0:T(8,128)(2,1)S(1)} %shard_map.244.refs_0_), channel_id=1, source_target_pairs={{0,8},{1,9},{2,10},{3,11},{4,12},{5,13},{6,14},{7,15},{8,0},{9,1},... | collective-permute-start | bytes 442376 | tf_op jit(solution)/shard_map/ppermute | solution.py:881
  117.4 12.3 %collective-permute-start.12 = (bf16[464,512]{1,0:T(8,128)(2,1)S(1)}, bf16[464,512]{1,0:T(8,128)(2,1)S(1)}, u32[]{:S(2)}, u32[]{:S(2)}) collective-permute-start(bf16[464,512]{1,0:T(8,128)(2,1)S(1)} %get-tuple-element.210), channel_id=1, source_target_pairs={{0,1},{1,0},{2,6},{3,7},{4,5},{5,4},{6,2},{7,3},{8,9},{9,8},{10,14... | collective-permute-start | bytes 1425416 | tf_op jit(solution)/shard_map/ppermute | solution.py:881
  127.6 16.3 %collective-permute-start.19 = (bf16[576,512]{1,0:T(8,128)(2,1)S(1)}, bf16[576,512]{1,0:T(8,128)(2,1)S(1)}, u32[]{:S(2)}, u32[]{:S(2)}) collective-permute-start(bf16[576,512]{1,0:T(8,128)(2,1)S(1)} %shard_map.245.refs_0_), channel_id=1, source_target_pairs={{0,1},{1,0},{2,6},{3,7},{4,5},{5,4},{6,2},{7,3},{8,9},{9,8},{10,14... | collective-permute-start | bytes 1769480 | tf_op jit(solution)/shard_map/ppermute | solution.py:881
  129.5 25.5 %collective-permute-start.20 = (bf16[4,128,512]{2,1,0:T(8,128)(2,1)S(1)}, bf16[4,128,512]{2,1,0:T(8,128)(2,1)S(1)}, u32[]{:S(2)}, u32[]{:S(2)}) collective-permute-start(bf16[4,128,512]{2,1,0:T(8,128)(2,1)S(1)} %get-tuple-element.223), channel_id=1, source_target_pairs={{0,1},{1,0},{2,3},{3,2},{4,5},{5,4},{6,7},{7,6},{8,9},{9,8},{10,11... | collective-permute-start | bytes 1572872 | tf_op jit(solution)/shard_map/ppermute | solution.py:1194
  130.3 24.7 %collective-permute-start.16 = (bf16[128,512]{1,0:T(8,128)(2,1)S(1)}, bf16[128,512]{1,0:T(8,128)(2,1)S(1)}, u32[]{:S(2)}, u32[]{:S(2)}) collective-permute-start(bf16[128,512]{1,0:T(8,128)(2,1)S(1)} %get-tuple-element.218), channel_id=1, source_target_pairs={{0,8},{1,9},{2,10},{3,11},{4,12},{5,13},{6,14},{7,15},{8,0},{9,1},... | collective-permute-start | bytes 393224 | tf_op jit(solution)/shard_map/ppermute | solution.py:881
  130.6 24.5 %collective-permute-start.17 = (bf16[128,512]{1,0:T(8,128)(2,1)S(1)}, bf16[128,512]{1,0:T(8,128)(2,1)S(1)}, u32[]{:S(2)}, u32[]{:S(2)}) collective-permute-start(bf16[128,512]{1,0:T(8,128)(2,1)S(1)} %get-tuple-element.219), channel_id=1, source_target_pairs={{0,16},{1,17},{2,18},{3,19},{4,20},{5,21},{6,22},{7,23},{8,24},{9,... | collective-permute-start | bytes 393224 | tf_op jit(solution)/shard_map/ppermute | solution.py:881
  134.0 21.1 %collective-permute-start.18 = (bf16[128,512]{1,0:T(8,128)(2,1)S(1)}, bf16[128,512]{1,0:T(8,128)(2,1)S(1)}, u32[]{:S(2)}, u32[]{:S(2)}) collective-permute-start(bf16[128,512]{1,0:T(8,128)(2,1)S(1)} %get-tuple-element.220), channel_id=1, source_target_pairs={{0,24},{1,25},{2,26},{3,27},{4,28},{5,29},{6,30},{7,31},{8,16},{9,... | collective-permute-start | bytes 393224 | tf_op jit(solution)/shard_map/ppermute | solution.py:881
  144.5 30.2 %collective-permute-start.21 = (bf16[1152,512]{1,0:T(8,128)(2,1)S(1)}, bf16[1152,512]{1,0:T(8,128)(2,1)S(1)}, u32[]{:S(2)}, u32[]{:S(2)}) collective-permute-start(bf16[1152,512]{1,0:T(8,128)(2,1)S(1)} %shard_map.247.refs_0_), channel_id=1, source_target_pairs={{0,4},{1,5},{2,3},{3,2},{4,0},{5,1},{6,7},{7,6},{8,12},{9,13},{10,... | collective-permute-start | bytes 3538952 | tf_op jit(solution)/shard_map/ppermute | solution.py:881
  155.9 6.6 %collective-permute-start.24 = (bf16[112,512]{1,0:T(8,128)(2,1)S(1)}, bf16[112,512]{1,0:T(8,128)(2,1)S(1)}, u32[]{:S(2)}, u32[]{:S(2)}) collective-permute-start(bf16[112,512]{1,0:T(8,128)(2,1)S(1)} %get-tuple-element.230.refs_0_), channel_id=1, source_target_pairs={{0,24},{1,25},{2,26},{3,27},{4,28},{5,29},{6,30},{7,31},{8,16},{9,... | collective-permute-start | bytes 344072 | tf_op jit(solution)/shard_map/ppermute | solution.py:881
  158.9 6.0 %collective-permute-start.23 = (bf16[112,512]{1,0:T(8,128)(2,1)S(1)}, bf16[112,512]{1,0:T(8,128)(2,1)S(1)}, u32[]{:S(2)}, u32[]{:S(2)}) collective-permute-start(bf16[112,512]{1,0:T(8,128)(2,1)S(1)} %get-tuple-element.230.refs_0_), channel_id=1, source_target_pairs={{0,16},{1,17},{2,18},{3,19},{4,20},{5,21},{6,22},{7,23},{8,24},{9,... | collective-permute-start | bytes 344072 | tf_op jit(solution)/shard_map/ppermute | solution.py:881
  158.9 6.0 %collective-permute-start.22 = (bf16[112,512]{1,0:T(8,128)(2,1)S(1)}, bf16[112,512]{1,0:T(8,128)(2,1)S(1)}, u32[]{:S(2)}, u32[]{:S(2)}) collective-permute-start(bf16[112,512]{1,0:T(8,128)(2,1)S(1)} %get-tuple-element.230.refs_0_), channel_id=1, source_target_pairs={{0,8},{1,9},{2,10},{3,11},{4,12},{5,13},{6,14},{7,15},{8,0},{9,1},... | collective-permute-start | bytes 344072 | tf_op jit(solution)/shard_map/ppermute | solution.py:881
  165.5 8.5 %collective-permute-start.25 = (bf16[448,512]{1,0:T(8,128)(2,1)S(1)}, bf16[448,512]{1,0:T(8,128)(2,1)S(1)}, u32[]{:S(2)}, u32[]{:S(2)}) collective-permute-start(bf16[448,512]{1,0:T(8,128)(2,1)S(1)} %shard_map.249.refs_0_), channel_id=1, source_target_pairs={{0,1},{1,0},{2,6},{3,7},{4,5},{5,4},{6,2},{7,3},{8,9},{9,8},{10,14... | collective-permute-start | bytes 1376264 | tf_op jit(solution)/shard_map/ppermute | solution.py:881
  174.7 2.9 %collective-permute-start.27 = (bf16[1152,512]{1,0:T(8,128)(2,1)S(1)}, bf16[1152,512]{1,0:T(8,128)(2,1)S(1)}, u32[]{:S(2)}, u32[]{:S(2)}) collective-permute-start(bf16[1152,512]{1,0:T(8,128)(2,1)S(1)} %shard_map.247.refs_0_), channel_id=1, source_target_pairs={{0,2},{1,3},{2,0},{3,1},{4,6},{5,7},{6,4},{7,5},{8,10},{9,11},{10,... | collective-permute-start | bytes 3538952 | tf_op jit(solution)/shard_map/ppermute | solution.py:881
  174.8 4.5 %collective-permute-start.28 = (bf16[1152,512]{1,0:T(8,128)(2,1)S(1)}, bf16[1152,512]{1,0:T(8,128)(2,1)S(1)}, u32[]{:S(2)}, u32[]{:S(2)}) collective-permute-start(bf16[1152,512]{1,0:T(8,128)(2,1)S(1)} %collective-permute-done.21.refs_2_), channel_id=1, source_target_pairs={{0,2},{1,3},{2,0},{3,1},{4,6},{5,7},{6,4},{7,5},{8,10},{9,11},{10,... | collective-permute-start | bytes 3538952 | tf_op jit(solution)/shard_map/ppermute | solution.py:881
  175.3 8.7 %collective-permute-start.29 = (bf16[896,512]{1,0:T(8,128)(2,1)S(1)}, bf16[896,512]{1,0:T(8,128)(2,1)S(1)}, u32[]{:S(2)}, u32[]{:S(2)}) collective-permute-start(bf16[896,512]{1,0:T(8,128)(2,1)S(1)} %shard_map.250.refs_0_), channel_id=1, source_target_pairs={{0,2},{1,3},{2,0},{3,1},{4,6},{5,7},{6,4},{7,5},{8,10},{9,11},{10,... | collective-permute-start | bytes 2752520 | tf_op jit(solution)/shard_map/ppermute | solution.py:881
  175.3 13.4 %collective-permute-start.26 = (bf16[896,512]{1,0:T(8,128)(2,1)S(1)}, bf16[896,512]{1,0:T(8,128)(2,1)S(1)}, u32[]{:S(2)}, u32[]{:S(2)}) collective-permute-start(bf16[896,512]{1,0:T(8,128)(2,1)S(1)} %shard_map.250.refs_0_), channel_id=1, source_target_pairs={{0,4},{1,5},{2,3},{3,2},{4,0},{5,1},{6,7},{7,6},{8,12},{9,13},{10,... | collective-permute-start | bytes 2752520 | tf_op jit(solution)/shard_map/ppermute | solution.py:881
  188.7 2.5 %collective-permute-start.30 = (bf16[896,512]{1,0:T(8,128)(2,1)S(1)}, bf16[896,512]{1,0:T(8,128)(2,1)S(1)}, u32[]{:S(2)}, u32[]{:S(2)}) collective-permute-start(bf16[896,512]{1,0:T(8,128)(2,1)S(1)} %collective-permute-done.26.refs_0_), channel_id=1, source_target_pairs={{0,2},{1,3},{2,0},{3,1},{4,6},{5,7},{6,4},{7,5},{8,10},{9,11},{10,... | collective-permute-start | bytes 2752520 | tf_op jit(solution)/shard_map/ppermute | solution.py:881
  189.9 4.0 %copy-start.27 = (bf16[8,256,512]{2,1,0:T(8,128)(2,1)}, bf16[8,256,512]{2,1,0:T(8,128)(2,1)S(1)}, u32[]{:S(2)}) copy-start(bf16[8,256,512]{2,1,0:T(8,128)(2,1)S(1)} %constant_dynamic-update-slice_fusion) | copy-start | bytes 6291460
  (13 other events, 32.9 us)

commit v2 on v1

--- a/solution.py
+++ b/solution.py
@@ -1267,10 +1267,11 @@
     parts_two = second_sum.swap(parts_two, 2)
     joined_one = first_sum.join(1, spot, spread_one)
     spread_one = first_sum.spread(0, joined_one)
-    parts_two, joined_one, backs_early = lax.optimization_barrier((parts_two, joined_one, backs_early))
-    sum_two, *norm_sums = second_sum.total(parts_two, work=8)
+    parts_two, joined_one = lax.optimization_barrier((parts_two, joined_one))
+    sum_two, *norm_sums = second_sum.total(parts_two, work=0.01)
     spread_two = second_sum.spread(2, sum_two)
-    spread_two = second_sum.spread(1, second_sum.join(2, spot, spread_two))
+    spread_two, backs_early = lax.optimization_barrier((spread_two, backs_early))
+    spread_two = second_sum.spread(1, second_sum.join(2, spot, spread_two, work=8))
     joined_two = second_sum.join(1, spot, spread_two)
     spread_one, joined_two = lax.optimization_barrier((spread_one, joined_two))
     other_one = [first_sum.core_swap(array) for array in spread_one]

time: 197 us -> 192 us (0.975)
  starting transfers between devices: 37.4 us -> 34.7 us
    ppermute x2, waiting for transfers between devices: 9.75 us -> 0.12 us  [send_back(): lax.ppermute(array, 'mem', [(k, (k - 1 - i) % groups) for k in range(grou...]
    ppermute x28, waiting for transfers between devices: 37.9 us -> 45.7 us  [permute(): return lax.ppermute(array, ('dp', 'mem'), pairs)]
    ppermute x28, starting transfers between devices: 33.7 us -> 31 us  [permute(): return lax.ppermute(array, ('dp', 'mem'), pairs)]
  transfers between devices with their start and end apart: 31 -> 31, of which waited for: 15 -> 16; matrix products, arithmetic and copies ran while one was open for 1% -> 1% of each run, Pallas kernels for 36% -> 37%
where the time goes in v2:
time: 192 us; the launch traced here: 189 us
  Pallas kernels  102 us (53%)
  waiting for transfers between devices  47.2 us (25%)
  starting transfers between devices  34.7 us (18%)
  local copies, waits for them, and re-layouts  4.22 us (2%)
    pallas_call x25, Pallas kernels, call(): pl.pallas_call(kernel, out_shape=[jax.ShapeDtypeStruct(shape, kind) for s...  102 us
    ppermute x28, waiting for transfers between devices, permute(): return lax.ppermute(array, ('dp', 'mem'), pairs)  45.7 us
    ppermute x28, starting transfers between devices, permute(): return lax.ppermute(array, ('dp', 'mem'), pairs)  31 us
  transfers between devices with their start and end apart: 31, of which 16 were waited for; matrix products, arithmetic and copies ran while one was open for 1% of the time, Pallas kernels for 37%

profile of v2, /device:TPU:0, one launch (start us, length us, event | category | flops | bytes accessed | tf_op | source)
XLA Modules:
  0.0 189.4 jit_solution(5619391329111963339)
XLA Ops:
  0.7 1.3 constant_dynamic-slice_fusion
  2.0 3.0 %collective-permute-start = (bf16[4,256,512]{2,1,0:T(8,128)(2,1)S(1)}, bf16[4,256,512]{2,1,0:T(8,128)(2,1)S(1)}, u32[]{:S(2)}, u32[]{:S(2)}) collective-permute-start(bf16[4,256,512]{2,1,0:T(8,128)(2,1)S(1)} %constant_dynamic-slice_fusion), channel_id=1, source_target_pairs={{0,1},{1,0},{2,3},{3,2},{4,5},{5,4},{6,7},{7,6},{8,9},{9,8},{10,11... | collective-permute-start | bytes 3145736 | tf_op jit(solution)/shard_map/ppermute | solution.py:1057
  5.7 21.1 %shard_map.229 = (bf16[512,512]{1,0:T(8,128)(2,1)}, bf16[512,1536]{1,0:T(8,128)(2,1)}, f32[16,256]{1,0:T(8,128)}, bf16[512,512]{1,0:T(8,128)(2,1)}, f32[512,512]...) custom-call(s32[5]{0:T(128)} %stack.23.me_ref.refs_0_.spot_ref, ...), custom_call_target="tpu_custom_call" | custom-call | flops 500000000 | bytes 1500000 | tf_op jit(solution)/shard_map/pallas_call | solution.py:947
  26.7 1.4 collective-permute-done.refs_11_.refs_0_
  28.2 1.0 copy-done.4
  29.1 26.4 %shard_map.230 = (bf16[512,512]{1,0:T(8,128)(2,1)}, f32[16,256]{1,0:T(8,128)}, f32[16,256]{1,0:T(8,128)}, f32[512,512]{1,0:T(8,128)}, bf16[512,512]{1,0:T(8,128)...) custom-call(s32[5]{0:T(128)} %stack.23.me_ref.refs_0_.spot_ref, ...), custom_call_target="tpu_custom_call", output_to_operand_aliasing={{8}: (16, {})} | custom-call | flops 500000000 | bytes 1500000 | tf_op jit(solution)/shard_map/pallas_call | solution.py:947
  55.6 6.3 %shard_map.231 = (bf16[1,512,1024]{2,1,0:T(8,128)(2,1)}, bf16[512,256]{1,0:T(8,128)(2,1)}) custom-call(s32[5]{0:T(128)} %stack.23.me_ref.refs_0_.spot_ref, s32[2,4]{1,0:T(2,128)} %len_ref.15, s32[2,4]{1,0:T(2,128)} %src_ref.5, bf16[512,512]{1,0:T(8,128)(2,1)} %get-tuple-element.138.refs_4_.query_ref, f32[16,256]{1,0:T(8,128)} %get-tuple-element.146.norm_ref, ...), custom_call_target="tpu_custom_call" | custom-call | flops 10000000000 | bytes 30000000 | tf_op jit(solution)/shard_map/pallas_call | solution.py:947
  62.0 2.0 %shard_map.232 = (bf16[1152,512]{1,0:T(8,128)(2,1)S(1)}, bf16[1152,512]{1,0:T(8,128)(2,1)S(1)}) custom-call(s32[5]{0:T(128)S(1)} %copy-done.17, bf16[2304,512]{1,0:T(8,128)(2,1)S(1)} %copy-done.7, bf16[2304,512]{1,0:T(8,128)(2,1)S(1)} %collective-permute-done.1.refs_1_), custom_call_target="tpu_custom_call" | custom-call | flops 10000000 | bytes 30000 | tf_op jit(solution)/shard_map/pallas_call | solution.py:947
  64.0 1.8 collective-permute-start.2
  65.9 8.1 %shard_map.233 = (bf16[3,512,1024]{2,1,0:T(8,128)(2,1)S(1)}, bf16[512,256]{1,0:T(8,128)(2,1)S(1)}) custom-call(s32[5]{0:T(128)S(1)} %copy-done.17, s32[2,4]{1,0:T(2,128)S(1)} %copy-done.20, s32[2,4]{1,0:T(2,128)S(1)} %copy-done.23, bf16[512,512]{1,0:T(8,128)(2,1)S(1)} %copy-done.15, f32[16,256]{1,0:T(8,128)S(1)} %copy-done.25, f32[16,256]{1,0:T(8,128)S(1)} %copy-done.26, ...), custom_call_target="tpu_custom_call" | custom-call | flops 10000000000 | bytes 30000000 | tf_op jit(solution)/shard_map/pallas_call | solution.py:947
  74.1 2.9 %shard_map.234.wkv_grad_ref = bf16[2,512,512]{2,1,0:T(8,128)(2,1)S(1)} custom-call(s32[5]{0:T(128)S(1)} %copy-done.17, s32[2,4]{1,0:T(2,128)S(1)} %copy-done.20, bf16[1,512,1024]{2,1,0:T(8,128)(2,1)S(1)} %copy-done.2, bf16[3,512,1024]{2,1,0:T(8,128)(2,1)S(1)} %get-tuple-element.163.pair_grad_rest_ref, bf16[8,256,512]{2,1,0:T(8,128)(2,1)S(1)} %copy-done.1, ...), custom_call_target="tpu_custom_call" | custom-call | flops 1000000000 | bytes 3000000 | tf_op jit(solution)/shard_map/pallas_call | solution.py:947
  77.1 3.1 %shard_map.235 = (bf16[1040,512]{1,0:T(8,128)(2,1)S(1)}, bf16[1040,512]{1,0:T(8,128)(2,1)S(1)}, f32[512,512]{1,0:T(8,128)S(1)}, bf16[512,512]{1,0:T(8,128)(2,1)S(1)}) custom-call(s32[5]{0:T(128)S(1)} %copy-done.17, f32[512,512]{1,0:T(8,128)S(1)} %copy-done.6, bf16[512,256]{1,0:T(8,128)(2,1)S(1)} %copy-done.16, ...), custom_call_target="tpu_custom_call" | custom-call | flops 100000000 | bytes 300000 | tf_op jit(solution)/shard_map/pallas_call | solution.py:947
  81.3 1.7 collective-permute-start.3
  83.0 2.1 %shard_map.237 = bf16[4,128,512]{2,1,0:T(8,128)(2,1)S(1)} custom-call(s32[5]{0:T(128)S(1)} %copy-done.17, s32[2,4]{1,0:T(2,128)S(1)} %copy-done.20, bf16[1,512,1024]{2,1,0:T(8,128)(2,1)S(1)} %copy-done.2, bf16[3,512,1024]{2,1,0:T(8,128)(2,1)S(1)} %get-tuple-element.163.pair_grad_rest_ref, bf16[512,1024]{1,0:T(8,128)(2,1)S(1)} %copy-done), custom_call_target="tpu_custom_call" | custom-call | flops 10000000 | bytes 30000 | tf_op jit(solution)/shard_map/pallas_call | solution.py:947
  85.6 6.5 %shard_map.238 = (bf16[512,1536]{1,0:T(8,128)(2,1)S(1)}, bf16[384,512]{1,0:T(8,128)(2,1)S(1)}, bf16[384,512]{1,0:T(8,128)(2,1)S(1)}, bf16[384,512]{1,0:T(8,128)(2,1)S(1)}, bf16[384,512]{1,0:T(8,128)(2,1)S(1)}) custom-call(s32[5]{0:T(128)S(1)} %copy-done.17, s32[2,4]{1,0:T(2,128)S(1)} %copy-done.20, bf16[512,1536]{1,0:T(8,128)(2,1)S(1)} %copy-done.11, ...), custom_call_target="tpu_custom_call" | custom-call | flops 100000000 | bytes 300000 | tf_op jit(solution)/shard_map/pallas_call | solution.py:947
  92.1 3.0 %collective-permute-done.3.refs_1_ = bf16[576,512]{1,0:T(8,128)(2,1)S(1)} collective-permute-done((bf16[576,512]{1,0:T(8,128)(2,1)S(1)}, bf16[576,512]{1,0:T(8,128)(2,1)S(1)}, u32[]{:S(2)}, u32[]{:S(2)}) %collective-permute-start.3) | collective-permute-done | bytes 589856 | tf_op jit(solution)/shard_map/ppermute | solution.py:881
  96.4 1.7 collective-permute-start.5
  98.1 2.6 %collective-permute-start.6 = (bf16[144,512]{1,0:T(8,128)(2,1)S(1)}, bf16[144,512]{1,0:T(8,128)(2,1)S(1)}, u32[]{:S(2)}, u32[]{:S(2)}) collective-permute-start(bf16[144,512]{1,0:T(8,128)(2,1)S(1)} %get-tuple-element.192), channel_id=1, source_target_pairs={{0,16},{1,17},{2,18},{3,19},{4,20},{5,21},{6,22},{7,23},{8,24},{9,... | collective-permute-start | bytes 442376 | tf_op jit(solution)/shard_map/ppermute | solution.py:881
  100.8 1.6 shard_map.240
  102.5 2.3 %collective-permute-start.11 = (bf16[912,512]{1,0:T(8,128)(2,1)S(1)}, bf16[912,512]{1,0:T(8,128)(2,1)S(1)}, u32[]{:S(2)}, u32[]{:S(2)}) collective-permute-start(bf16[912,512]{1,0:T(8,128)(2,1)S(1)} %get-tuple-element.212), channel_id=1, source_target_pairs={{0,4},{1,5},{2,3},{3,2},{4,0},{5,1},{6,7},{7,6},{8,12},{9,13},{10,... | collective-permute-start | bytes 2801672 | tf_op jit(solution)/shard_map/ppermute | solution.py:881
  104.8 2.7 %shard_map.242 = bf16[512,512]{1,0:T(8,128)(2,1)} custom-call(s32[5]{0:T(128)S(1)} %copy-done.17, s32[2,4]{1,0:T(2,128)S(1)} %copy-done.20, bf16[512,1536]{1,0:T(8,128)(2,1)S(1)} %get-tuple-element.207.grad_triple_ref, bf16[512,1536]{1,0:T(8,128)(2,1)S(1)} %copy-done.10, f32[512,512]{1,0:T(8,128)S(1)} %get-tuple-element.208.grad_hidden_ref), custom_call_target="tpu_custom_call" | custom-call | flops 30000001024 | bytes 90000000 | tf_op jit(solution)/shard_map/pallas_call | solution.py:947
  107.5 3.1 %shard_map.241 = (bf16[4,256,512]{2,1,0:T(8,128)(2,1)S(1)}, bf16[4,128,512]{2,1,0:T(8,128)(2,1)S(1)}) custom-call(s32[5]{0:T(128)S(1)} %copy-done.17, s32[2,4]{1,0:T(2,128)S(1)} %copy-done.20, bf16[1,512,1024]{2,1,0:T(8,128)(2,1)S(1)} %copy-done.2, bf16[3,512,1024]{2,1,0:T(8,128)(2,1)S(1)} %get-tuple-element.163.pair_grad_rest_ref, bf16[512,1024]{1,0:T(8,128)(2,1)S(1)} %copy-done), custom_call_target="tpu_custom_call" | custom-call | flops 10000000 | bytes 30000 | tf_op jit(solution)/shard_map/pallas_call | solution.py:947
  110.6 1.4 collective-permute-done.6.refs_2_
  112.1 2.5 %collective-permute-start.15 = (bf16[144,512]{1,0:T(8,128)(2,1)S(1)}, bf16[144,512]{1,0:T(8,128)(2,1)S(1)}, u32[]{:S(2)}, u32[]{:S(2)}) collective-permute-start(bf16[144,512]{1,0:T(8,128)(2,1)S(1)} %shard_map.244.refs_0_), channel_id=1, source_target_pairs={{0,24},{1,25},{2,26},{3,27},{4,28},{5,29},{6,30},{7,31},{8,16},{9,... | collective-permute-start | bytes 442376 | tf_op jit(solution)/shard_map/ppermute | solution.py:881
  114.6 1.6 collective-permute-start.14
  117.4 2.0 %collective-permute-start.12 = (bf16[464,512]{1,0:T(8,128)(2,1)S(1)}, bf16[464,512]{1,0:T(8,128)(2,1)S(1)}, u32[]{:S(2)}, u32[]{:S(2)}) collective-permute-start(bf16[464,512]{1,0:T(8,128)(2,1)S(1)} %get-tuple-element.214), channel_id=1, source_target_pairs={{0,1},{1,0},{2,6},{3,7},{4,5},{5,4},{6,2},{7,3},{8,9},{9,8},{10,14... | collective-permute-start | bytes 1425416 | tf_op jit(solution)/shard_map/ppermute | solution.py:881
  119.3 1.2 collective-permute-done.15.refs_3_
  120.5 6.5 %collective-permute-done.14.refs_2_ = bf16[144,512]{1,0:T(8,128)(2,1)S(1)} collective-permute-done((bf16[144,512]{1,0:T(8,128)(2,1)S(1)}, bf16[144,512]{1,0:T(8,128)(2,1)S(1)}, u32[]{:S(2)}, u32[]{:S(2)}) %collective-permute-start.14) | collective-permute-done | bytes 147488 | tf_op jit(solution)/shard_map/ppermute | solution.py:881
  127.6 1.9 %collective-permute-start.19 = (bf16[576,512]{1,0:T(8,128)(2,1)S(1)}, bf16[576,512]{1,0:T(8,128)(2,1)S(1)}, u32[]{:S(2)}, u32[]{:S(2)}) collective-permute-start(bf16[576,512]{1,0:T(8,128)(2,1)S(1)} %shard_map.245.refs_0_), channel_id=1, source_target_pairs={{0,1},{1,0},{2,6},{3,7},{4,5},{5,4},{6,2},{7,3},{8,9},{9,8},{10,14... | collective-permute-start | bytes 1769480 | tf_op jit(solution)/shard_map/ppermute | solution.py:881
  130.6 3.4 %collective-permute-start.17 = (bf16[128,512]{1,0:T(8,128)(2,1)S(1)}, bf16[128,512]{1,0:T(8,128)(2,1)S(1)}, u32[]{:S(2)}, u32[]{:S(2)}) collective-permute-start(bf16[128,512]{1,0:T(8,128)(2,1)S(1)} %get-tuple-element.223), channel_id=1, source_target_pairs={{0,16},{1,17},{2,18},{3,19},{4,20},{5,21},{6,22},{7,23},{8,24},{9,... | collective-permute-start | bytes 393224 | tf_op jit(solution)/shard_map/ppermute | solution.py:881
  134.0 0.8 collective-permute-start.18
  134.8 7.3 %collective-permute-done.19.refs_1_ = bf16[576,512]{1,0:T(8,128)(2,1)S(1)} collective-permute-done((bf16[576,512]{1,0:T(8,128)(2,1)S(1)}, bf16[576,512]{1,0:T(8,128)(2,1)S(1)}, u32[]{:S(2)}, u32[]{:S(2)}) %collective-permute-start.19) | collective-permute-done | bytes 589856 | tf_op jit(solution)/shard_map/ppermute | solution.py:881
  142.8 1.2 collective-permute-done.17.refs_2_
  144.6 2.8 %collective-permute-start.22 = (bf16[112,512]{1,0:T(8,128)(2,1)S(1)}, bf16[112,512]{1,0:T(8,128)(2,1)S(1)}, u32[]{:S(2)}, u32[]{:S(2)}) collective-permute-start(bf16[112,512]{1,0:T(8,128)(2,1)S(1)} %get-tuple-element.235.refs_0_), channel_id=1, source_target_pairs={{0,24},{1,25},{2,26},{3,27},{4,28},{5,29},{6,30},{7,31},{8,16},{9,... | collective-permute-start | bytes 344072 | tf_op jit(solution)/shard_map/ppermute | solution.py:881
  147.4 0.8 collective-permute-start.21
  149.0 0.9 collective-permute-start.24
  149.9 2.6 %collective-permute-done.22.refs_3_ = bf16[112,512]{1,0:T(8,128)(2,1)S(1)} collective-permute-done((bf16[112,512]{1,0:T(8,128)(2,1)S(1)}, bf16[112,512]{1,0:T(8,128)(2,1)S(1)}, u32[]{:S(2)}, u32[]{:S(2)}) %collective-permute-start.22) | collective-permute-done | bytes 114720 | tf_op jit(solution)/shard_map/ppermute | solution.py:881
  152.5 4.1 %collective-permute-done.21.refs_2_ = bf16[112,512]{1,0:T(8,128)(2,1)S(1)} collective-permute-done((bf16[112,512]{1,0:T(8,128)(2,1)S(1)}, bf16[112,512]{1,0:T(8,128)(2,1)S(1)}, u32[]{:S(2)}, u32[]{:S(2)}) %collective-permute-start.21) | collective-permute-done | bytes 114720 | tf_op jit(solution)/shard_map/ppermute | solution.py:881
  157.6 9.3 %collective-permute-done.25.refs_1_ = bf16[448,512]{1,0:T(8,128)(2,1)S(1)} collective-permute-done((bf16[448,512]{1,0:T(8,128)(2,1)S(1)}, bf16[448,512]{1,0:T(8,128)(2,1)S(1)}, u32[]{:S(2)}, u32[]{:S(2)}) %collective-permute-start.25) | collective-permute-done | bytes 458784 | tf_op jit(solution)/shard_map/ppermute | solution.py:881
  167.5 2.6 %collective-permute-done.24.refs_2_ = bf16[1152,512]{1,0:T(8,128)(2,1)S(1)} collective-permute-done((bf16[1152,512]{1,0:T(8,128)(2,1)S(1)}, bf16[1152,512]{1,0:T(8,128)(2,1)S(1)}, u32[]{:S(2)}, u32[]{:S(2)}) %collective-permute-start.24) | collective-permute-done | bytes 1179680 | tf_op jit(solution)/shard_map/ppermute | solution.py:881
  170.6 0.9 collective-permute-start.26
  171.6 1.4 collective-permute-done.27.refs_1_
  173.0 1.7 collective-permute-done.28.refs_3_
  174.7 4.7 %shard_map.251 = (f32[2048,512]{1,0:T(8,128)}, f32[512,2048]{1,0:T(8,128)}, f32[512,512]{1,0:T(8,128)}) custom-call(s32[5]{0:T(128)S(1)} %copy-done.17, bf16[1152,512]{1,0:T(8,128)(2,1)S(1)} %shard_map.247.refs_0_, bf16[1152,512]{1,0:T(8,128)(2,1)S(1)} %collective-permute-done.27.refs_1_, bf16[1152,512]{1,0:T(8,128)(2,1)S(1)} %collective-permute-done.24.refs_2_, ...), custom_call_target="tpu_custom_call" | custom-call | flops 1000000000 | bytes 3000000 | tf_op jit(solution)/shard_map/pallas_call | solution.py:947
  179.3 2.6 %shard_map.252 = (f32[512,512]{1,0:T(8,128)}, f32[512,1024]{1,0:T(8,128)}, f32[512,1536]{1,0:T(8,128)}, f32[512,512]{1,0:T(8,128)}) custom-call(s32[5]{0:T(128)S(1)} %copy-done.17, bf16[896,512]{1,0:T(8,128)(2,1)S(1)} %shard_map.250.refs_0_, bf16[896,512]{1,0:T(8,128)(2,1)S(1)} %collective-permute-done.29.refs_1_), custom_call_target="tpu_custom_call" | custom-call | flops 1000000000 | bytes 3000000 | tf_op jit(solution)/shard_map/pallas_call | solution.py:947
  182.0 2.1 %collective-permute-done.26.refs_0_ = bf16[896,512]{1,0:T(8,128)(2,1)S(1)} collective-permute-done((bf16[896,512]{1,0:T(8,128)(2,1)S(1)}, bf16[896,512]{1,0:T(8,128)(2,1)S(1)}, u32[]{:S(2)}, u32[]{:S(2)}) %collective-permute-start.26) | collective-permute-done | bytes 917536 | tf_op jit(solution)/shard_map/ppermute | solution.py:881
  185.2 1.3 collective-permute-done.30.refs_1_
  186.5 2.6 %shard_map.253 = (f32[512,512]{1,0:T(8,128)}, f32[512,1024]{1,0:T(8,128)}, f32[512,1536]{1,0:T(8,128)}, f32[512,512]{1,0:T(8,128)}) custom-call(s32[5]{0:T(128)S(1)} %copy-done.17, bf16[896,512]{1,0:T(8,128)(2,1)S(1)} %collective-permute-done.26.refs_0_, ...), custom_call_target="tpu_custom_call", output_to_operand_aliasing={{0}: (3, {}), {1}: (4, {}), {2}: (5, {}), {3}: (6, {})} | custom-call | flops 1000000000 | bytes 3000000 | tf_op jit(solution)/shard_map/pallas_call | solution.py:947
  (105 shorter events, 12.1 us)
Async XLA Ops:
  2.0 26.2 %collective-permute-start = (bf16[4,256,512]{2,1,0:T(8,128)(2,1)S(1)}, bf16[4,256,512]{2,1,0:T(8,128)(2,1)S(1)}, u32[]{:S(2)}, u32[]{:S(2)}) collective-permute-start(bf16[4,256,512]{2,1,0:T(8,128)(2,1)S(1)} %constant_dynamic-slice_fusion), channel_id=1, source_target_pairs={{0,1},{1,0},{2,3},{3,2},{4,5},{5,4},{6,7},{7,6},{8,9},{9,8},{10,11... | collective-permute-start | bytes 3145736 | tf_op jit(solution)/shard_map/ppermute | solution.py:1057
  55.5 6.5 %collective-permute-start.1 = (bf16[2304,512]{1,0:T(8,128)(2,1)}, bf16[2304,512]{1,0:T(8,128)(2,1)S(1)}, u32[]{:S(2)}, u32[]{:S(2)}) collective-permute-start(bf16[2304,512]{1,0:T(8,128)(2,1)} %get-tuple-element.145), channel_id=1, source_target_pairs={{0,2},{1,3},{2,0},{3,1},{4,6},{5,7},{6,4},{7,5},{8,10},{9,11},{10,... | collective-permute-start | bytes 7077896 | tf_op jit(solution)/shard_map/ppermute | solution.py:881
  55.6 6.4 %copy-start.7 = (bf16[2304,512]{1,0:T(8,128)(2,1)S(1)}, bf16[2304,512]{1,0:T(8,128)(2,1)}, u32[]{:S(2)}) copy-start(bf16[2304,512]{1,0:T(8,128)(2,1)} %get-tuple-element.144.refs_0_) | copy-start | bytes 7077892
  55.6 6.4 %copy-start.17 = (s32[5]{0:T(128)S(1)}, s32[5]{0:T(128)}, u32[]{:S(2)}) copy-start(s32[5]{0:T(128)} %stack.23.me_ref.refs_0_.spot_ref) | copy-start | bytes 64
  55.6 10.2 %copy-start.24 = (bf16[512,512]{1,0:T(8,128)(2,1)S(1)}, bf16[512,512]{1,0:T(8,128)(2,1)}, u32[]{:S(2)}) copy-start(bf16[512,512]{1,0:T(8,128)(2,1)} %get-tuple-element.148.grad_attn_ref) | copy-start | bytes 1572868
  55.6 10.2 %copy-start.25 = (f32[16,256]{1,0:T(8,128)S(1)}, f32[16,256]{1,0:T(8,128)}, u32[]{:S(2)}) copy-start(f32[16,256]{1,0:T(8,128)} %get-tuple-element.146.norm_ref) | copy-start | bytes 49156
  55.6 10.2 %copy-start.26 = (f32[16,256]{1,0:T(8,128)S(1)}, f32[16,256]{1,0:T(8,128)}, u32[]{:S(2)}) copy-start(f32[16,256]{1,0:T(8,128)} %get-tuple-element.147.along_ref) | copy-start | bytes 49156
  62.0 3.8 %copy-start.3 = (bf16[4,512,1024]{2,1,0:T(8,128)(2,1)S(1)}, bf16[4,512,1024]{2,1,0:T(8,128)(2,1)}, u32[]{:S(2)}) copy-start(bf16[4,512,1024]{2,1,0:T(8,128)(2,1)} %get-tuple-element.157.pair_hbm) | copy-start | bytes 12582916
  62.0 3.8 %copy-start.15 = (bf16[512,512]{1,0:T(8,128)(2,1)S(1)}, bf16[512,512]{1,0:T(8,128)(2,1)}, u32[]{:S(2)}) copy-start(bf16[512,512]{1,0:T(8,128)(2,1)} %get-tuple-element.138.refs_4_.query_ref) | copy-start | bytes 1572868
  62.0 3.8 %copy-start.20 = (s32[2,4]{1,0:T(2,128)S(1)}, s32[2,4]{1,0:T(2,128)}, u32[]{:S(2)}) copy-start(s32[2,4]{1,0:T(2,128)} %len_ref.15) | copy-start | bytes 100
  64.0 9.9 %copy-start.1 = (bf16[8,256,512]{2,1,0:T(8,128)(2,1)S(1)}, bf16[8,256,512]{2,1,0:T(8,128)(2,1)}, u32[]{:S(2)}) copy-start(bf16[8,256,512]{2,1,0:T(8,128)(2,1)} %memory_ref.3) | copy-start | bytes 6291460
  64.0 9.9 %copy-start.2 = (bf16[1,512,1024]{2,1,0:T(8,128)(2,1)S(1)}, bf16[1,512,1024]{2,1,0:T(8,128)(2,1)}, u32[]{:S(2)}) copy-start(bf16[1,512,1024]{2,1,0:T(8,128)(2,1)} %get-tuple-element.204.pair_grad_long_ref) | copy-start | bytes 3145732
  64.0 9.9 %copy-start.5 = (bf16[4,256,512]{2,1,0:T(8,128)(2,1)S(1)}, bf16[4,256,512]{2,1,0:T(8,128)(2,1)}, u32[]{:S(2)}) copy-start(bf16[4,256,512]{2,1,0:T(8,128)(2,1)} %copy-done.4) | copy-start | bytes 3145732
  64.0 16.4 %collective-permute-start.2 = (bf16[1152,512]{1,0:T(8,128)(2,1)S(1)}, bf16[1152,512]{1,0:T(8,128)(2,1)S(1)}, u32[]{:S(2)}, u32[]{:S(2)}) collective-permute-start(bf16[1152,512]{1,0:T(8,128)(2,1)S(1)} %get-tuple-element.155), channel_id=1, source_target_pairs={{0,4},{1,5},{2,3},{3,2},{4,0},{5,1},{6,7},{7,6},{8,12},{9,13},{10,... | collective-permute-start | bytes 3538952 | tf_op jit(solution)/shard_map/ppermute | solution.py:881
  80.2 11.9 %collective-permute-start.4 = (bf16[1040,512]{1,0:T(8,128)(2,1)S(1)}, bf16[1040,512]{1,0:T(8,128)(2,1)S(1)}, u32[]{:S(2)}, u32[]{:S(2)}) collective-permute-start(bf16[1040,512]{1,0:T(8,128)(2,1)S(1)} %get-tuple-element.182), channel_id=1, source_target_pairs={{0,2},{1,3},{2,0},{3,1},{4,6},{5,7},{6,4},{7,5},{8,10},{9,11},{10,... | collective-permute-start | bytes 3194888 | tf_op jit(solution)/shard_map/ppermute | solution.py:881
  81.3 4.3 %copy-start.11 = (bf16[512,1536]{1,0:T(8,128)(2,1)S(1)}, bf16[512,1536]{1,0:T(8,128)(2,1)}, u32[]{:S(2)}) copy-start(bf16[512,1536]{1,0:T(8,128)(2,1)} %get-tuple-element.172.qkv_ref) | copy-start | bytes 4718596
  81.3 4.3 %copy-start.13 = (bf16[512,512]{1,0:T(8,128)(2,1)S(1)}, bf16[512,512]{1,0:T(8,128)(2,1)}, u32[]{:S(2)}) copy-start(bf16[512,512]{1,0:T(8,128)(2,1)} %get-tuple-element.177.sorted_ref) | copy-start | bytes 1572868
  81.3 4.3 %copy-start.21 = (f32[16,256]{1,0:T(8,128)S(1)}, f32[16,256]{1,0:T(8,128)}, u32[]{:S(2)}) copy-start(f32[16,256]{1,0:T(8,128)} %get-tuple-element.173.norm_ref) | copy-start | bytes 49156
  81.3 13.8 %collective-permute-start.3 = (bf16[576,512]{1,0:T(8,128)(2,1)S(1)}, bf16[576,512]{1,0:T(8,128)(2,1)S(1)}, u32[]{:S(2)}, u32[]{:S(2)}) collective-permute-start(bf16[576,512]{1,0:T(8,128)(2,1)S(1)} %get-tuple-element.171), channel_id=1, source_target_pairs={{0,1},{1,0},{2,6},{3,7},{4,5},{5,4},{6,2},{7,3},{8,9},{9,8},{10,14... | collective-permute-start | bytes 1769480 | tf_op jit(solution)/shard_map/ppermute | solution.py:881
  85.1 17.5 %collective-permute-start.10 = (bf16[4,128,512]{2,1,0:T(8,128)(2,1)S(1)}, bf16[4,128,512]{2,1,0:T(8,128)(2,1)S(1)}, u32[]{:S(2)}, u32[]{:S(2)}) collective-permute-start(bf16[4,128,512]{2,1,0:T(8,128)(2,1)S(1)} %shard_map.237), channel_id=1, source_target_pairs={{0,1},{1,0},{2,3},{3,2},{4,5},{5,4},{6,7},{7,6},{8,9},{9,8},{10,11... | collective-permute-start | bytes 1572872 | tf_op jit(solution)/shard_map/ppermute | solution.py:1194
  95.1 5.5 %collective-permute-start.8 = (bf16[384,512]{1,0:T(8,128)(2,1)S(1)}, bf16[384,512]{1,0:T(8,128)(2,1)S(1)}, u32[]{:S(2)}, u32[]{:S(2)}) collective-permute-start(bf16[384,512]{1,0:T(8,128)(2,1)S(1)} %get-tuple-element.197), channel_id=1, source_target_pairs={{0,2},{1,3},{2,0},{3,1},{4,6},{5,7},{6,4},{7,5},{8,10},{9,11},{10,... | collective-permute-start | bytes 1179656 | tf_op jit(solution)/shard_map/ppermute | solution.py:881
  95.2 5.7 %collective-permute-start.9 = (bf16[384,512]{1,0:T(8,128)(2,1)S(1)}, bf16[384,512]{1,0:T(8,128)(2,1)S(1)}, u32[]{:S(2)}, u32[]{:S(2)}) collective-permute-start(bf16[384,512]{1,0:T(8,128)(2,1)S(1)} %get-tuple-element.199), channel_id=1, source_target_pairs={{0,2},{1,3},{2,0},{3,1},{4,6},{5,7},{6,4},{7,5},{8,10},{9,11},{10,... | collective-permute-start | bytes 1179656 | tf_op jit(solution)/shard_map/ppermute | solution.py:881
  96.3 8.4 %copy-start.10 = (bf16[512,1536]{1,0:T(8,128)(2,1)S(1)}, bf16[512,1536]{1,0:T(8,128)(2,1)}, u32[]{:S(2)}) copy-start(bf16[512,1536]{1,0:T(8,128)(2,1)} %w_qkv_ref.3) | copy-start | bytes 4718596
  96.4 14.3 %collective-permute-start.5 = (bf16[144,512]{1,0:T(8,128)(2,1)S(1)}, bf16[144,512]{1,0:T(8,128)(2,1)S(1)}, u32[]{:S(2)}, u32[]{:S(2)}) collective-permute-start(bf16[144,512]{1,0:T(8,128)(2,1)S(1)} %get-tuple-element.191), channel_id=1, source_target_pairs={{0,8},{1,9},{2,10},{3,11},{4,12},{5,13},{6,14},{7,15},{8,0},{9,1},... | collective-permute-start | bytes 442376 | tf_op jit(solution)/shard_map/ppermute | solution.py:881
  98.1 14.0 %collective-permute-start.6 = (bf16[144,512]{1,0:T(8,128)(2,1)S(1)}, bf16[144,512]{1,0:T(8,128)(2,1)S(1)}, u32[]{:S(2)}, u32[]{:S(2)}) collective-permute-start(bf16[144,512]{1,0:T(8,128)(2,1)S(1)} %get-tuple-element.192), channel_id=1, source_target_pairs={{0,16},{1,17},{2,18},{3,19},{4,20},{5,21},{6,22},{7,23},{8,24},{9,... | collective-permute-start | bytes 442376 | tf_op jit(solution)/shard_map/ppermute | solution.py:881
  100.7 11.4 %collective-permute-start.7 = (bf16[144,512]{1,0:T(8,128)(2,1)S(1)}, bf16[144,512]{1,0:T(8,128)(2,1)S(1)}, u32[]{:S(2)}, u32[]{:S(2)}) collective-permute-start(bf16[144,512]{1,0:T(8,128)(2,1)S(1)} %get-tuple-element.193), channel_id=1, source_target_pairs={{0,24},{1,25},{2,26},{3,27},{4,28},{5,29},{6,30},{7,31},{8,16},{9,... | collective-permute-start | bytes 442376 | tf_op jit(solution)/shard_map/ppermute | solution.py:881
  102.5 14.1 %collective-permute-start.11 = (bf16[912,512]{1,0:T(8,128)(2,1)S(1)}, bf16[912,512]{1,0:T(8,128)(2,1)S(1)}, u32[]{:S(2)}, u32[]{:S(2)}) collective-permute-start(bf16[912,512]{1,0:T(8,128)(2,1)S(1)} %get-tuple-element.212), channel_id=1, source_target_pairs={{0,4},{1,5},{2,3},{3,2},{4,0},{5,1},{6,7},{7,6},{8,12},{9,13},{10,... | collective-permute-start | bytes 2801672 | tf_op jit(solution)/shard_map/ppermute | solution.py:881
  112.1 8.4 %collective-permute-start.15 = (bf16[144,512]{1,0:T(8,128)(2,1)S(1)}, bf16[144,512]{1,0:T(8,128)(2,1)S(1)}, u32[]{:S(2)}, u32[]{:S(2)}) collective-permute-start(bf16[144,512]{1,0:T(8,128)(2,1)S(1)} %shard_map.244.refs_0_), channel_id=1, source_target_pairs={{0,24},{1,25},{2,26},{3,27},{4,28},{5,29},{6,30},{7,31},{8,16},{9,... | collective-permute-start | bytes 442376 | tf_op jit(solution)/shard_map/ppermute | solution.py:881
  114.6 12.4 %collective-permute-start.14 = (bf16[144,512]{1,0:T(8,128)(2,1)S(1)}, bf16[144,512]{1,0:T(8,128)(2,1)S(1)}, u32[]{:S(2)}, u32[]{:S(2)}) collective-permute-start(bf16[144,512]{1,0:T(8,128)(2,1)S(1)} %shard_map.244.refs_0_), channel_id=1, source_target_pairs={{0,16},{1,17},{2,18},{3,19},{4,20},{5,21},{6,22},{7,23},{8,24},{9,... | collective-permute-start | bytes 442376 | tf_op jit(solution)/shard_map/ppermute | solution.py:881
  116.2 10.9 %collective-permute-start.13 = (bf16[144,512]{1,0:T(8,128)(2,1)S(1)}, bf16[144,512]{1,0:T(8,128)(2,1)S(1)}, u32[]{:S(2)}, u32[]{:S(2)}) collective-permute-start(bf16[144,512]{1,0:T(8,128)(2,1)S(1)} %shard_map.244.refs_0_), channel_id=1, source_target_pairs={{0,8},{1,9},{2,10},{3,11},{4,12},{5,13},{6,14},{7,15},{8,0},{9,1},... | collective-permute-start | bytes 442376 | tf_op jit(solution)/shard_map/ppermute | solution.py:881
  117.4 12.3 %collective-permute-start.12 = (bf16[464,512]{1,0:T(8,128)(2,1)S(1)}, bf16[464,512]{1,0:T(8,128)(2,1)S(1)}, u32[]{:S(2)}, u32[]{:S(2)}) collective-permute-start(bf16[464,512]{1,0:T(8,128)(2,1)S(1)} %get-tuple-element.214), channel_id=1, source_target_pairs={{0,1},{1,0},{2,6},{3,7},{4,5},{5,4},{6,2},{7,3},{8,9},{9,8},{10,14... | collective-permute-start | bytes 1425416 | tf_op jit(solution)/shard_map/ppermute | solution.py:881
  127.6 14.5 %collective-permute-start.19 = (bf16[576,512]{1,0:T(8,128)(2,1)S(1)}, bf16[576,512]{1,0:T(8,128)(2,1)S(1)}, u32[]{:S(2)}, u32[]{:S(2)}) collective-permute-start(bf16[576,512]{1,0:T(8,128)(2,1)S(1)} %shard_map.245.refs_0_), channel_id=1, source_target_pairs={{0,1},{1,0},{2,6},{3,7},{4,5},{5,4},{6,2},{7,3},{8,9},{9,8},{10,14... | collective-permute-start | bytes 1769480 | tf_op jit(solution)/shard_map/ppermute | solution.py:881
  129.5 20.4 %collective-permute-start.23 = (bf16[4,128,512]{2,1,0:T(8,128)(2,1)S(1)}, bf16[4,128,512]{2,1,0:T(8,128)(2,1)S(1)}, u32[]{:S(2)}, u32[]{:S(2)}) collective-permute-start(bf16[4,128,512]{2,1,0:T(8,128)(2,1)S(1)} %get-tuple-element.232), channel_id=1, source_target_pairs={{0,1},{1,0},{2,3},{3,2},{4,5},{5,4},{6,7},{7,6},{8,9},{9,8},{10,11... | collective-permute-start | bytes 1572872 | tf_op jit(solution)/shard_map/ppermute | solution.py:1194
  130.4 12.4 %collective-permute-start.16 = (bf16[128,512]{1,0:T(8,128)(2,1)S(1)}, bf16[128,512]{1,0:T(8,128)(2,1)S(1)}, u32[]{:S(2)}, u32[]{:S(2)}) collective-permute-start(bf16[128,512]{1,0:T(8,128)(2,1)S(1)} %get-tuple-element.222), channel_id=1, source_target_pairs={{0,8},{1,9},{2,10},{3,11},{4,12},{5,13},{6,14},{7,15},{8,0},{9,1},... | collective-permute-start | bytes 393224 | tf_op jit(solution)/shard_map/ppermute | solution.py:881
  130.6 13.4 %collective-permute-start.17 = (bf16[128,512]{1,0:T(8,128)(2,1)S(1)}, bf16[128,512]{1,0:T(8,128)(2,1)S(1)}, u32[]{:S(2)}, u32[]{:S(2)}) collective-permute-start(bf16[128,512]{1,0:T(8,128)(2,1)S(1)} %get-tuple-element.223), channel_id=1, source_target_pairs={{0,16},{1,17},{2,18},{3,19},{4,20},{5,21},{6,22},{7,23},{8,24},{9,... | collective-permute-start | bytes 393224 | tf_op jit(solution)/shard_map/ppermute | solution.py:881
  134.0 10.0 %collective-permute-start.18 = (bf16[128,512]{1,0:T(8,128)(2,1)S(1)}, bf16[128,512]{1,0:T(8,128)(2,1)S(1)}, u32[]{:S(2)}, u32[]{:S(2)}) collective-permute-start(bf16[128,512]{1,0:T(8,128)(2,1)S(1)} %get-tuple-element.224), channel_id=1, source_target_pairs={{0,24},{1,25},{2,26},{3,27},{4,28},{5,29},{6,30},{7,31},{8,16},{9,... | collective-permute-start | bytes 393224 | tf_op jit(solution)/shard_map/ppermute | solution.py:881
  144.6 7.9 %collective-permute-start.22 = (bf16[112,512]{1,0:T(8,128)(2,1)S(1)}, bf16[112,512]{1,0:T(8,128)(2,1)S(1)}, u32[]{:S(2)}, u32[]{:S(2)}) collective-permute-start(bf16[112,512]{1,0:T(8,128)(2,1)S(1)} %get-tuple-element.235.refs_0_), channel_id=1, source_target_pairs={{0,24},{1,25},{2,26},{3,27},{4,28},{5,29},{6,30},{7,31},{8,16},{9,... | collective-permute-start | bytes 344072 | tf_op jit(solution)/shard_map/ppermute | solution.py:881
  147.4 9.2 %collective-permute-start.21 = (bf16[112,512]{1,0:T(8,128)(2,1)S(1)}, bf16[112,512]{1,0:T(8,128)(2,1)S(1)}, u32[]{:S(2)}, u32[]{:S(2)}) collective-permute-start(bf16[112,512]{1,0:T(8,128)(2,1)S(1)} %get-tuple-element.235.refs_0_), channel_id=1, source_target_pairs={{0,16},{1,17},{2,18},{3,19},{4,20},{5,21},{6,22},{7,23},{8,24},{9,... | collective-permute-start | bytes 344072 | tf_op jit(solution)/shard_map/ppermute | solution.py:881
  148.3 8.3 %collective-permute-start.20 = (bf16[112,512]{1,0:T(8,128)(2,1)S(1)}, bf16[112,512]{1,0:T(8,128)(2,1)S(1)}, u32[]{:S(2)}, u32[]{:S(2)}) collective-permute-start(bf16[112,512]{1,0:T(8,128)(2,1)S(1)} %get-tuple-element.235.refs_0_), channel_id=1, source_target_pairs={{0,8},{1,9},{2,10},{3,11},{4,12},{5,13},{6,14},{7,15},{8,0},{9,1},... | collective-permute-start | bytes 344072 | tf_op jit(solution)/shard_map/ppermute | solution.py:881
  149.0 21.1 %collective-permute-start.24 = (bf16[1152,512]{1,0:T(8,128)(2,1)S(1)}, bf16[1152,512]{1,0:T(8,128)(2,1)S(1)}, u32[]{:S(2)}, u32[]{:S(2)}) collective-permute-start(bf16[1152,512]{1,0:T(8,128)(2,1)S(1)} %shard_map.247.refs_0_), channel_id=1, source_target_pairs={{0,4},{1,5},{2,3},{3,2},{4,0},{5,1},{6,7},{7,6},{8,12},{9,13},{10,... | collective-permute-start | bytes 3538952 | tf_op jit(solution)/shard_map/ppermute | solution.py:881
  149.9 7.2 %copy-start.28 = (bf16[4,128,512]{2,1,0:T(8,128)(2,1)}, bf16[4,128,512]{2,1,0:T(8,128)(2,1)S(1)}, u32[]{:S(2)}) copy-start(bf16[4,128,512]{2,1,0:T(8,128)(2,1)S(1)} %collective-permute-done.23) | copy-start | bytes 1572868
  157.2 9.7 %collective-permute-start.25 = (bf16[448,512]{1,0:T(8,128)(2,1)S(1)}, bf16[448,512]{1,0:T(8,128)(2,1)S(1)}, u32[]{:S(2)}, u32[]{:S(2)}) collective-permute-start(bf16[448,512]{1,0:T(8,128)(2,1)S(1)} %shard_map.249.refs_0_), channel_id=1, source_target_pairs={{0,1},{1,0},{2,6},{3,7},{4,5},{5,4},{6,2},{7,3},{8,9},{9,8},{10,14... | collective-permute-start | bytes 1376264 | tf_op jit(solution)/shard_map/ppermute | solution.py:881
  170.1 2.8 %collective-permute-start.27 = (bf16[1152,512]{1,0:T(8,128)(2,1)S(1)}, bf16[1152,512]{1,0:T(8,128)(2,1)S(1)}, u32[]{:S(2)}, u32[]{:S(2)}) collective-permute-start(bf16[1152,512]{1,0:T(8,128)(2,1)S(1)} %shard_map.247.refs_0_), channel_id=1, source_target_pairs={{0,2},{1,3},{2,0},{3,1},{4,6},{5,7},{6,4},{7,5},{8,10},{9,11},{10,... | collective-permute-start | bytes 3538952 | tf_op jit(solution)/shard_map/ppermute | solution.py:881
  170.1 4.5 %collective-permute-start.28 = (bf16[1152,512]{1,0:T(8,128)(2,1)S(1)}, bf16[1152,512]{1,0:T(8,128)(2,1)S(1)}, u32[]{:S(2)}, u32[]{:S(2)}) collective-permute-start(bf16[1152,512]{1,0:T(8,128)(2,1)S(1)} %collective-permute-done.24.refs_2_), channel_id=1, source_target_pairs={{0,2},{1,3},{2,0},{3,1},{4,6},{5,7},{6,4},{7,5},{8,10},{9,11},{10,... | collective-permute-start | bytes 3538952 | tf_op jit(solution)/shard_map/ppermute | solution.py:881
  170.6 8.7 %collective-permute-start.29 = (bf16[896,512]{1,0:T(8,128)(2,1)S(1)}, bf16[896,512]{1,0:T(8,128)(2,1)S(1)}, u32[]{:S(2)}, u32[]{:S(2)}) collective-permute-start(bf16[896,512]{1,0:T(8,128)(2,1)S(1)} %shard_map.250.refs_0_), channel_id=1, source_target_pairs={{0,2},{1,3},{2,0},{3,1},{4,6},{5,7},{6,4},{7,5},{8,10},{9,11},{10,... | collective-permute-start | bytes 2752520 | tf_op jit(solution)/shard_map/ppermute | solution.py:881
  170.6 13.4 %collective-permute-start.26 = (bf16[896,512]{1,0:T(8,128)(2,1)S(1)}, bf16[896,512]{1,0:T(8,128)(2,1)S(1)}, u32[]{:S(2)}, u32[]{:S(2)}) collective-permute-start(bf16[896,512]{1,0:T(8,128)(2,1)S(1)} %shard_map.250.refs_0_), channel_id=1, source_target_pairs={{0,4},{1,5},{2,3},{3,2},{4,0},{5,1},{6,7},{7,6},{8,12},{9,13},{10,... | collective-permute-start | bytes 2752520 | tf_op jit(solution)/shard_map/ppermute | solution.py:881
  184.0 2.5 %collective-permute-start.30 = (bf16[896,512]{1,0:T(8,128)(2,1)S(1)}, bf16[896,512]{1,0:T(8,128)(2,1)S(1)}, u32[]{:S(2)}, u32[]{:S(2)}) collective-permute-start(bf16[896,512]{1,0:T(8,128)(2,1)S(1)} %collective-permute-done.26.refs_0_), channel_id=1, source_target_pairs={{0,2},{1,3},{2,0},{3,1},{4,6},{5,7},{6,4},{7,5},{8,10},{9,11},{10,... | collective-permute-start | bytes 2752520 | tf_op jit(solution)/shard_map/ppermute | solution.py:881
  185.2 4.0 %copy-start.27 = (bf16[8,256,512]{2,1,0:T(8,128)(2,1)}, bf16[8,256,512]{2,1,0:T(8,128)(2,1)S(1)}, u32[]{:S(2)}) copy-start(bf16[8,256,512]{2,1,0:T(8,128)(2,1)S(1)} %constant_dynamic-update-slice_fusion) | copy-start | bytes 6291460
  (13 other events, 35.9 us)

commit v3 on v2

--- a/solution.py
+++ b/solution.py
@@ -1271,7 +1271,7 @@
     sum_two, *norm_sums = second_sum.total(parts_two, work=0.01)
     spread_two = second_sum.spread(2, sum_two)
     spread_two, backs_early = lax.optimization_barrier((spread_two, backs_early))
-    spread_two = second_sum.spread(1, second_sum.join(2, spot, spread_two, work=8))
+    spread_two = second_sum.spread(1, second_sum.join(2, spot, spread_two, work=6.3))
     joined_two = second_sum.join(1, spot, spread_two)
     spread_one, joined_two = lax.optimization_barrier((spread_one, joined_two))
     other_one = [first_sum.core_swap(array) for array in spread_one]

time: 192 us -> 189 us (0.984)
  waiting for transfers between devices: 47.2 us -> 43.4 us
    ppermute x28, waiting for transfers between devices: 45.7 us -> 37.3 us  [permute(): return lax.ppermute(array, ('dp', 'mem'), pairs)]
    ppermute x2, waiting for transfers between devices: 0.12 us -> 4.65 us  [send_back(): lax.ppermute(array, 'mem', [(k, (k - 1 - i) % groups) for k in range(grou...]
  transfers between devices with their start and end apart: 31 -> 31, of which waited for: 16 -> 14; matrix products, arithmetic and copies ran while one was open for 1% -> 1% of each run, Pallas kernels for 37% -> 38%
where the time goes in v3:
time: 189 us; the launch traced here: 186 us
  Pallas kernels  102 us (54%)
  waiting for transfers between devices  43.4 us (23%)
  starting transfers between devices  34.7 us (18%)
  local copies, waits for them, and re-layouts  4.22 us (2%)
    pallas_call x25, Pallas kernels, call(): pl.pallas_call(kernel, out_shape=[jax.ShapeDtypeStruct(shape, kind) for s...  102 us
    ppermute x28, waiting for transfers between devices, permute(): return lax.ppermute(array, ('dp', 'mem'), pairs)  37.3 us
    ppermute x28, starting transfers between devices, permute(): return lax.ppermute(array, ('dp', 'mem'), pairs)  31 us
    ppermute x2, waiting for transfers between devices, send_back(): lax.ppermute(array, 'mem', [(k, (k - 1 - i) % groups) for k in range(grou...  4.65 us
  transfers between devices with their start and end apart: 31, of which 14 were waited for; matrix products, arithmetic and copies ran while one was open for 1% of the time, Pallas kernels for 38%

profile of v3, /device:TPU:0, one launch (start us, length us, event | category | flops | bytes accessed | tf_op | source)
XLA Modules:
  0.0 185.5 jit_solution(16527956627103979134)
XLA Ops:
  0.7 1.3 constant_dynamic-slice_fusion
  2.0 3.0 %collective-permute-start = (bf16[4,256,512]{2,1,0:T(8,128)(2,1)S(1)}, bf16[4,256,512]{2,1,0:T(8,128)(2,1)S(1)}, u32[]{:S(2)}, u32[]{:S(2)}) collective-permute-start(bf16[4,256,512]{2,1,0:T(8,128)(2,1)S(1)} %constant_dynamic-slice_fusion), channel_id=1, source_target_pairs={{0,1},{1,0},{2,3},{3,2},{4,5},{5,4},{6,7},{7,6},{8,9},{9,8},{10,11... | collective-permute-start | bytes 3145736 | tf_op jit(solution)/shard_map/ppermute | solution.py:1057
  5.7 21.1 %shard_map.229 = (bf16[512,512]{1,0:T(8,128)(2,1)}, bf16[512,1536]{1,0:T(8,128)(2,1)}, f32[16,256]{1,0:T(8,128)}, bf16[512,512]{1,0:T(8,128)(2,1)}, f32[512,512]...) custom-call(s32[5]{0:T(128)} %stack.23.me_ref.refs_0_.spot_ref, ...), custom_call_target="tpu_custom_call" | custom-call | flops 500000000 | bytes 1500000 | tf_op jit(solution)/shard_map/pallas_call | solution.py:947
  26.7 1.4 collective-permute-done.refs_11_.refs_0_
  28.2 1.0 copy-done.4
  29.1 26.4 %shard_map.230 = (bf16[512,512]{1,0:T(8,128)(2,1)}, f32[16,256]{1,0:T(8,128)}, f32[16,256]{1,0:T(8,128)}, f32[512,512]{1,0:T(8,128)}, bf16[512,512]{1,0:T(8,128)...) custom-call(s32[5]{0:T(128)} %stack.23.me_ref.refs_0_.spot_ref, ...), custom_call_target="tpu_custom_call", output_to_operand_aliasing={{8}: (16, {})} | custom-call | flops 500000000 | bytes 1500000 | tf_op jit(solution)/shard_map/pallas_call | solution.py:947
  55.6 6.3 %shard_map.231 = (bf16[1,512,1024]{2,1,0:T(8,128)(2,1)}, bf16[512,256]{1,0:T(8,128)(2,1)}) custom-call(s32[5]{0:T(128)} %stack.23.me_ref.refs_0_.spot_ref, s32[2,4]{1,0:T(2,128)} %len_ref.15, s32[2,4]{1,0:T(2,128)} %src_ref.5, bf16[512,512]{1,0:T(8,128)(2,1)} %get-tuple-element.138.refs_4_.query_ref, f32[16,256]{1,0:T(8,128)} %get-tuple-element.146.norm_ref, ...), custom_call_target="tpu_custom_call" | custom-call | flops 10000000000 | bytes 30000000 | tf_op jit(solution)/shard_map/pallas_call | solution.py:947
  62.0 2.0 %shard_map.232 = (bf16[1152,512]{1,0:T(8,128)(2,1)S(1)}, bf16[1152,512]{1,0:T(8,128)(2,1)S(1)}) custom-call(s32[5]{0:T(128)S(1)} %copy-done.17, bf16[2304,512]{1,0:T(8,128)(2,1)S(1)} %copy-done.7, bf16[2304,512]{1,0:T(8,128)(2,1)S(1)} %collective-permute-done.1.refs_1_), custom_call_target="tpu_custom_call" | custom-call | flops 10000000 | bytes 30000 | tf_op jit(solution)/shard_map/pallas_call | solution.py:947
  64.0 1.8 collective-permute-start.2
  65.9 8.1 %shard_map.233 = (bf16[3,512,1024]{2,1,0:T(8,128)(2,1)S(1)}, bf16[512,256]{1,0:T(8,128)(2,1)S(1)}) custom-call(s32[5]{0:T(128)S(1)} %copy-done.17, s32[2,4]{1,0:T(2,128)S(1)} %copy-done.20, s32[2,4]{1,0:T(2,128)S(1)} %copy-done.23, bf16[512,512]{1,0:T(8,128)(2,1)S(1)} %copy-done.15, f32[16,256]{1,0:T(8,128)S(1)} %copy-done.25, f32[16,256]{1,0:T(8,128)S(1)} %copy-done.26, ...), custom_call_target="tpu_custom_call" | custom-call | flops 10000000000 | bytes 30000000 | tf_op jit(solution)/shard_map/pallas_call | solution.py:947
  74.1 2.9 %shard_map.234.wkv_grad_ref = bf16[2,512,512]{2,1,0:T(8,128)(2,1)S(1)} custom-call(s32[5]{0:T(128)S(1)} %copy-done.17, s32[2,4]{1,0:T(2,128)S(1)} %copy-done.20, bf16[1,512,1024]{2,1,0:T(8,128)(2,1)S(1)} %copy-done.2, bf16[3,512,1024]{2,1,0:T(8,128)(2,1)S(1)} %get-tuple-element.163.pair_grad_rest_ref, bf16[8,256,512]{2,1,0:T(8,128)(2,1)S(1)} %copy-done.1, ...), custom_call_target="tpu_custom_call" | custom-call | flops 1000000000 | bytes 3000000 | tf_op jit(solution)/shard_map/pallas_call | solution.py:947
  77.1 3.1 %shard_map.235 = (bf16[1040,512]{1,0:T(8,128)(2,1)S(1)}, bf16[1040,512]{1,0:T(8,128)(2,1)S(1)}, f32[512,512]{1,0:T(8,128)S(1)}, bf16[512,512]{1,0:T(8,128)(2,1)S(1)}) custom-call(s32[5]{0:T(128)S(1)} %copy-done.17, f32[512,512]{1,0:T(8,128)S(1)} %copy-done.6, bf16[512,256]{1,0:T(8,128)(2,1)S(1)} %copy-done.16, ...), custom_call_target="tpu_custom_call" | custom-call | flops 100000000 | bytes 300000 | tf_op jit(solution)/shard_map/pallas_call | solution.py:947
  80.5 0.8 shard_map.236
  81.3 1.7 collective-permute-start.3
  83.0 2.1 %shard_map.237 = bf16[4,128,512]{2,1,0:T(8,128)(2,1)S(1)} custom-call(s32[5]{0:T(128)S(1)} %copy-done.17, s32[2,4]{1,0:T(2,128)S(1)} %copy-done.20, bf16[1,512,1024]{2,1,0:T(8,128)(2,1)S(1)} %copy-done.2, bf16[3,512,1024]{2,1,0:T(8,128)(2,1)S(1)} %get-tuple-element.163.pair_grad_rest_ref, bf16[512,1024]{1,0:T(8,128)(2,1)S(1)} %copy-done), custom_call_target="tpu_custom_call" | custom-call | flops 10000000 | bytes 30000 | tf_op jit(solution)/shard_map/pallas_call | solution.py:947
  85.6 6.5 %shard_map.238 = (bf16[512,1536]{1,0:T(8,128)(2,1)S(1)}, bf16[384,512]{1,0:T(8,128)(2,1)S(1)}, bf16[384,512]{1,0:T(8,128)(2,1)S(1)}, bf16[384,512]{1,0:T(8,128)(2,1)S(1)}, bf16[384,512]{1,0:T(8,128)(2,1)S(1)}) custom-call(s32[5]{0:T(128)S(1)} %copy-done.17, s32[2,4]{1,0:T(2,128)S(1)} %copy-done.20, bf16[512,1536]{1,0:T(8,128)(2,1)S(1)} %copy-done.11, ...), custom_call_target="tpu_custom_call" | custom-call | flops 100000000 | bytes 300000 | tf_op jit(solution)/shard_map/pallas_call | solution.py:947
  92.1 3.0 %collective-permute-done.3.refs_1_ = bf16[576,512]{1,0:T(8,128)(2,1)S(1)} collective-permute-done((bf16[576,512]{1,0:T(8,128)(2,1)S(1)}, bf16[576,512]{1,0:T(8,128)(2,1)S(1)}, u32[]{:S(2)}, u32[]{:S(2)}) %collective-permute-start.3) | collective-permute-done | bytes 589856 | tf_op jit(solution)/shard_map/ppermute | solution.py:881
  96.3 1.8 collective-permute-start.5
  98.1 2.6 %collective-permute-start.6 = (bf16[144,512]{1,0:T(8,128)(2,1)S(1)}, bf16[144,512]{1,0:T(8,128)(2,1)S(1)}, u32[]{:S(2)}, u32[]{:S(2)}) collective-permute-start(bf16[144,512]{1,0:T(8,128)(2,1)S(1)} %get-tuple-element.192), channel_id=1, source_target_pairs={{0,16},{1,17},{2,18},{3,19},{4,20},{5,21},{6,22},{7,23},{8,24},{9,... | collective-permute-start | bytes 442376 | tf_op jit(solution)/shard_map/ppermute | solution.py:881
  100.8 1.6 shard_map.240
  102.5 2.3 %collective-permute-start.11 = (bf16[912,512]{1,0:T(8,128)(2,1)S(1)}, bf16[912,512]{1,0:T(8,128)(2,1)S(1)}, u32[]{:S(2)}, u32[]{:S(2)}) collective-permute-start(bf16[912,512]{1,0:T(8,128)(2,1)S(1)} %get-tuple-element.212), channel_id=1, source_target_pairs={{0,4},{1,5},{2,3},{3,2},{4,0},{5,1},{6,7},{7,6},{8,12},{9,13},{10,... | collective-permute-start | bytes 2801672 | tf_op jit(solution)/shard_map/ppermute | solution.py:881
  104.8 2.7 %shard_map.242 = bf16[512,512]{1,0:T(8,128)(2,1)} custom-call(s32[5]{0:T(128)S(1)} %copy-done.17, s32[2,4]{1,0:T(2,128)S(1)} %copy-done.20, bf16[512,1536]{1,0:T(8,128)(2,1)S(1)} %get-tuple-element.207.grad_triple_ref, bf16[512,1536]{1,0:T(8,128)(2,1)S(1)} %copy-done.10, f32[512,512]{1,0:T(8,128)S(1)} %get-tuple-element.208.grad_hidden_ref), custom_call_target="tpu_custom_call" | custom-call | flops 30000001024 | bytes 90000000 | tf_op jit(solution)/shard_map/pallas_call | solution.py:947
  107.5 3.1 %shard_map.241 = (bf16[4,256,512]{2,1,0:T(8,128)(2,1)S(1)}, bf16[4,128,512]{2,1,0:T(8,128)(2,1)S(1)}) custom-call(s32[5]{0:T(128)S(1)} %copy-done.17, s32[2,4]{1,0:T(2,128)S(1)} %copy-done.20, bf16[1,512,1024]{2,1,0:T(8,128)(2,1)S(1)} %copy-done.2, bf16[3,512,1024]{2,1,0:T(8,128)(2,1)S(1)} %get-tuple-element.163.pair_grad_rest_ref, bf16[512,1024]{1,0:T(8,128)(2,1)S(1)} %copy-done), custom_call_target="tpu_custom_call" | custom-call | flops 10000000 | bytes 30000 | tf_op jit(solution)/shard_map/pallas_call | solution.py:947
  110.6 1.5 collective-permute-done.6.refs_2_
  112.2 2.4 %collective-permute-start.15 = (bf16[144,512]{1,0:T(8,128)(2,1)S(1)}, bf16[144,512]{1,0:T(8,128)(2,1)S(1)}, u32[]{:S(2)}, u32[]{:S(2)}) collective-permute-start(bf16[144,512]{1,0:T(8,128)(2,1)S(1)} %shard_map.244.refs_0_), channel_id=1, source_target_pairs={{0,24},{1,25},{2,26},{3,27},{4,28},{5,29},{6,30},{7,31},{8,16},{9,... | collective-permute-start | bytes 442376 | tf_op jit(solution)/shard_map/ppermute | solution.py:881
  114.6 1.6 collective-permute-start.14
  116.7 0.8 shard_map.243
  117.4 1.9 %collective-permute-start.12 = (bf16[464,512]{1,0:T(8,128)(2,1)S(1)}, bf16[464,512]{1,0:T(8,128)(2,1)S(1)}, u32[]{:S(2)}, u32[]{:S(2)}) collective-permute-start(bf16[464,512]{1,0:T(8,128)(2,1)S(1)} %get-tuple-element.214), channel_id=1, source_target_pairs={{0,1},{1,0},{2,6},{3,7},{4,5},{5,4},{6,2},{7,3},{8,9},{9,8},{10,14... | collective-permute-start | bytes 1425416 | tf_op jit(solution)/shard_map/ppermute | solution.py:881
  119.3 1.2 collective-permute-done.15.refs_3_
  120.6 6.5 %collective-permute-done.14.refs_2_ = bf16[144,512]{1,0:T(8,128)(2,1)S(1)} collective-permute-done((bf16[144,512]{1,0:T(8,128)(2,1)S(1)}, bf16[144,512]{1,0:T(8,128)(2,1)S(1)}, u32[]{:S(2)}, u32[]{:S(2)}) %collective-permute-start.14) | collective-permute-done | bytes 147488 | tf_op jit(solution)/shard_map/ppermute | solution.py:881
  127.6 1.9 %collective-permute-start.19 = (bf16[576,512]{1,0:T(8,128)(2,1)S(1)}, bf16[576,512]{1,0:T(8,128)(2,1)S(1)}, u32[]{:S(2)}, u32[]{:S(2)}) collective-permute-start(bf16[576,512]{1,0:T(8,128)(2,1)S(1)} %shard_map.245.refs_0_), channel_id=1, source_target_pairs={{0,1},{1,0},{2,6},{3,7},{4,5},{5,4},{6,2},{7,3},{8,9},{9,8},{10,14... | collective-permute-start | bytes 1769480 | tf_op jit(solution)/shard_map/ppermute | solution.py:881
  130.6 3.4 %collective-permute-start.17 = (bf16[128,512]{1,0:T(8,128)(2,1)S(1)}, bf16[128,512]{1,0:T(8,128)(2,1)S(1)}, u32[]{:S(2)}, u32[]{:S(2)}) collective-permute-start(bf16[128,512]{1,0:T(8,128)(2,1)S(1)} %get-tuple-element.223), channel_id=1, source_target_pairs={{0,16},{1,17},{2,18},{3,19},{4,20},{5,21},{6,22},{7,23},{8,24},{9,... | collective-permute-start | bytes 393224 | tf_op jit(solution)/shard_map/ppermute | solution.py:881
  134.0 0.8 collective-permute-start.18
  134.8 9.1 %collective-permute-done.19.refs_1_ = bf16[576,512]{1,0:T(8,128)(2,1)S(1)} collective-permute-done((bf16[576,512]{1,0:T(8,128)(2,1)S(1)}, bf16[576,512]{1,0:T(8,128)(2,1)S(1)}, u32[]{:S(2)}, u32[]{:S(2)}) %collective-permute-start.19) | collective-permute-done | bytes 589856 | tf_op jit(solution)/shard_map/ppermute | solution.py:881
  144.5 0.9 collective-permute-start.24
  146.1 4.0 %collective-permute-start.22 = (bf16[112,512]{1,0:T(8,128)(2,1)S(1)}, bf16[112,512]{1,0:T(8,128)(2,1)S(1)}, u32[]{:S(2)}, u32[]{:S(2)}) collective-permute-start(bf16[112,512]{1,0:T(8,128)(2,1)S(1)} %get-tuple-element.235.refs_0_), channel_id=1, source_target_pairs={{0,24},{1,25},{2,26},{3,27},{4,28},{5,29},{6,30},{7,31},{8,16},{9,... | collective-permute-start | bytes 344072 | tf_op jit(solution)/shard_map/ppermute | solution.py:881
  150.6 4.5 %collective-permute-done.23 = bf16[4,128,512]{2,1,0:T(8,128)(2,1)S(1)} collective-permute-done((bf16[4,128,512]{2,1,0:T(8,128)(2,1)S(1)}, bf16[4,128,512]{2,1,0:T(8,128)(2,1)S(1)}, u32[]{:S(2)}, u32[]{:S(2)}) %collective-permute-start.23) | collective-permute-done | bytes 524320 | tf_op jit(solution)/shard_map/ppermute | solution.py:1194
  155.1 1.2 collective-permute-done.21.refs_2_
  157.0 0.9 collective-permute-start.25
  157.8 7.7 %collective-permute-done.25.refs_1_ = bf16[448,512]{1,0:T(8,128)(2,1)S(1)} collective-permute-done((bf16[448,512]{1,0:T(8,128)(2,1)S(1)}, bf16[448,512]{1,0:T(8,128)(2,1)S(1)}, u32[]{:S(2)}, u32[]{:S(2)}) %collective-permute-start.25) | collective-permute-done | bytes 458784 | tf_op jit(solution)/shard_map/ppermute | solution.py:881
  167.1 2.0 %collective-permute-done.27.refs_1_ = bf16[1152,512]{1,0:T(8,128)(2,1)S(1)} collective-permute-done((bf16[1152,512]{1,0:T(8,128)(2,1)S(1)}, bf16[1152,512]{1,0:T(8,128)(2,1)S(1)}, u32[]{:S(2)}, u32[]{:S(2)}) %collective-permute-start.27) | collective-permute-done | bytes 1179680 | tf_op jit(solution)/shard_map/ppermute | solution.py:881
  169.1 1.7 collective-permute-done.28.refs_3_
  170.7 4.7 %shard_map.251 = (f32[2048,512]{1,0:T(8,128)}, f32[512,2048]{1,0:T(8,128)}, f32[512,512]{1,0:T(8,128)}) custom-call(s32[5]{0:T(128)S(1)} %copy-done.17, bf16[1152,512]{1,0:T(8,128)(2,1)S(1)} %shard_map.247.refs_0_, bf16[1152,512]{1,0:T(8,128)(2,1)S(1)} %collective-permute-done.27.refs_1_, bf16[1152,512]{1,0:T(8,128)(2,1)S(1)} %collective-permute-done.24.refs_2_, ...), custom_call_target="tpu_custom_call" | custom-call | flops 1000000000 | bytes 3000000 | tf_op jit(solution)/shard_map/pallas_call | solution.py:947
  175.4 2.6 %shard_map.252 = (f32[512,512]{1,0:T(8,128)}, f32[512,1024]{1,0:T(8,128)}, f32[512,1536]{1,0:T(8,128)}, f32[512,512]{1,0:T(8,128)}) custom-call(s32[5]{0:T(128)S(1)} %copy-done.17, bf16[896,512]{1,0:T(8,128)(2,1)S(1)} %shard_map.250.refs_0_, bf16[896,512]{1,0:T(8,128)(2,1)S(1)} %collective-permute-done.29.refs_1_), custom_call_target="tpu_custom_call" | custom-call | flops 1000000000 | bytes 3000000 | tf_op jit(solution)/shard_map/pallas_call | solution.py:947
  178.0 2.1 %collective-permute-done.26.refs_0_ = bf16[896,512]{1,0:T(8,128)(2,1)S(1)} collective-permute-done((bf16[896,512]{1,0:T(8,128)(2,1)S(1)}, bf16[896,512]{1,0:T(8,128)(2,1)S(1)}, u32[]{:S(2)}, u32[]{:S(2)}) %collective-permute-start.26) | collective-permute-done | bytes 917536 | tf_op jit(solution)/shard_map/ppermute | solution.py:881
  180.5 0.7 copy-done.29
  181.3 1.3 collective-permute-done.30.refs_1_
  182.7 2.6 %shard_map.253 = (f32[512,512]{1,0:T(8,128)}, f32[512,1024]{1,0:T(8,128)}, f32[512,1536]{1,0:T(8,128)}, f32[512,512]{1,0:T(8,128)}) custom-call(s32[5]{0:T(128)S(1)} %copy-done.17, bf16[896,512]{1,0:T(8,128)(2,1)S(1)} %collective-permute-done.26.refs_0_, ...), custom_call_target="tpu_custom_call", output_to_operand_aliasing={{0}: (3, {}), {1}: (4, {}), {2}: (5, {}), {3}: (6, {})} | custom-call | flops 1000000000 | bytes 3000000 | tf_op jit(solution)/shard_map/pallas_call | solution.py:947
  (105 shorter events, 9.6 us)
Async XLA Ops:
  2.0 26.2 %collective-permute-start = (bf16[4,256,512]{2,1,0:T(8,128)(2,1)S(1)}, bf16[4,256,512]{2,1,0:T(8,128)(2,1)S(1)}, u32[]{:S(2)}, u32[]{:S(2)}) collective-permute-start(bf16[4,256,512]{2,1,0:T(8,128)(2,1)S(1)} %constant_dynamic-slice_fusion), channel_id=1, source_target_pairs={{0,1},{1,0},{2,3},{3,2},{4,5},{5,4},{6,7},{7,6},{8,9},{9,8},{10,11... | collective-permute-start | bytes 3145736 | tf_op jit(solution)/shard_map/ppermute | solution.py:1057
  55.5 6.5 %collective-permute-start.1 = (bf16[2304,512]{1,0:T(8,128)(2,1)}, bf16[2304,512]{1,0:T(8,128)(2,1)S(1)}, u32[]{:S(2)}, u32[]{:S(2)}) collective-permute-start(bf16[2304,512]{1,0:T(8,128)(2,1)} %get-tuple-element.145), channel_id=1, source_target_pairs={{0,2},{1,3},{2,0},{3,1},{4,6},{5,7},{6,4},{7,5},{8,10},{9,11},{10,... | collective-permute-start | bytes 7077896 | tf_op jit(solution)/shard_map/ppermute | solution.py:881
  55.6 6.4 %copy-start.7 = (bf16[2304,512]{1,0:T(8,128)(2,1)S(1)}, bf16[2304,512]{1,0:T(8,128)(2,1)}, u32[]{:S(2)}) copy-start(bf16[2304,512]{1,0:T(8,128)(2,1)} %get-tuple-element.144.refs_0_) | copy-start | bytes 7077892
  55.6 6.4 %copy-start.17 = (s32[5]{0:T(128)S(1)}, s32[5]{0:T(128)}, u32[]{:S(2)}) copy-start(s32[5]{0:T(128)} %stack.23.me_ref.refs_0_.spot_ref) | copy-start | bytes 64
  55.6 10.2 %copy-start.24 = (bf16[512,512]{1,0:T(8,128)(2,1)S(1)}, bf16[512,512]{1,0:T(8,128)(2,1)}, u32[]{:S(2)}) copy-start(bf16[512,512]{1,0:T(8,128)(2,1)} %get-tuple-element.148.grad_attn_ref) | copy-start | bytes 1572868
  55.6 10.2 %copy-start.25 = (f32[16,256]{1,0:T(8,128)S(1)}, f32[16,256]{1,0:T(8,128)}, u32[]{:S(2)}) copy-start(f32[16,256]{1,0:T(8,128)} %get-tuple-element.146.norm_ref) | copy-start | bytes 49156
  55.6 10.2 %copy-start.26 = (f32[16,256]{1,0:T(8,128)S(1)}, f32[16,256]{1,0:T(8,128)}, u32[]{:S(2)}) copy-start(f32[16,256]{1,0:T(8,128)} %get-tuple-element.147.along_ref) | copy-start | bytes 49156
  62.0 3.8 %copy-start.3 = (bf16[4,512,1024]{2,1,0:T(8,128)(2,1)S(1)}, bf16[4,512,1024]{2,1,0:T(8,128)(2,1)}, u32[]{:S(2)}) copy-start(bf16[4,512,1024]{2,1,0:T(8,128)(2,1)} %get-tuple-element.157.pair_hbm) | copy-start | bytes 12582916
  62.0 3.8 %copy-start.15 = (bf16[512,512]{1,0:T(8,128)(2,1)S(1)}, bf16[512,512]{1,0:T(8,128)(2,1)}, u32[]{:S(2)}) copy-start(bf16[512,512]{1,0:T(8,128)(2,1)} %get-tuple-element.138.refs_4_.query_ref) | copy-start | bytes 1572868
  62.0 3.8 %copy-start.20 = (s32[2,4]{1,0:T(2,128)S(1)}, s32[2,4]{1,0:T(2,128)}, u32[]{:S(2)}) copy-start(s32[2,4]{1,0:T(2,128)} %len_ref.15) | copy-start | bytes 100
  62.0 3.8 %copy-start.23 = (s32[2,4]{1,0:T(2,128)S(1)}, s32[2,4]{1,0:T(2,128)}, u32[]{:S(2)}) copy-start(s32[2,4]{1,0:T(2,128)} %src_ref.5) | copy-start | bytes 100
  64.0 9.9 %copy-start.1 = (bf16[8,256,512]{2,1,0:T(8,128)(2,1)S(1)}, bf16[8,256,512]{2,1,0:T(8,128)(2,1)}, u32[]{:S(2)}) copy-start(bf16[8,256,512]{2,1,0:T(8,128)(2,1)} %memory_ref.3) | copy-start | bytes 6291460
  64.0 9.9 %copy-start.2 = (bf16[1,512,1024]{2,1,0:T(8,128)(2,1)S(1)}, bf16[1,512,1024]{2,1,0:T(8,128)(2,1)}, u32[]{:S(2)}) copy-start(bf16[1,512,1024]{2,1,0:T(8,128)(2,1)} %get-tuple-element.204.pair_grad_long_ref) | copy-start | bytes 3145732
  64.0 9.9 %copy-start.5 = (bf16[4,256,512]{2,1,0:T(8,128)(2,1)S(1)}, bf16[4,256,512]{2,1,0:T(8,128)(2,1)}, u32[]{:S(2)}) copy-start(bf16[4,256,512]{2,1,0:T(8,128)(2,1)} %copy-done.4) | copy-start | bytes 3145732
  64.0 16.4 %collective-permute-start.2 = (bf16[1152,512]{1,0:T(8,128)(2,1)S(1)}, bf16[1152,512]{1,0:T(8,128)(2,1)S(1)}, u32[]{:S(2)}, u32[]{:S(2)}) collective-permute-start(bf16[1152,512]{1,0:T(8,128)(2,1)S(1)} %get-tuple-element.155), channel_id=1, source_target_pairs={{0,4},{1,5},{2,3},{3,2},{4,0},{5,1},{6,7},{7,6},{8,12},{9,13},{10,... | collective-permute-start | bytes 3538952 | tf_op jit(solution)/shard_map/ppermute | solution.py:881
  80.2 11.9 %collective-permute-start.4 = (bf16[1040,512]{1,0:T(8,128)(2,1)S(1)}, bf16[1040,512]{1,0:T(8,128)(2,1)S(1)}, u32[]{:S(2)}, u32[]{:S(2)}) collective-permute-start(bf16[1040,512]{1,0:T(8,128)(2,1)S(1)} %get-tuple-element.182), channel_id=1, source_target_pairs={{0,2},{1,3},{2,0},{3,1},{4,6},{5,7},{6,4},{7,5},{8,10},{9,11},{10,... | collective-permute-start | bytes 3194888 | tf_op jit(solution)/shard_map/ppermute | solution.py:881
  81.3 4.3 %copy-start.11 = (bf16[512,1536]{1,0:T(8,128)(2,1)S(1)}, bf16[512,1536]{1,0:T(8,128)(2,1)}, u32[]{:S(2)}) copy-start(bf16[512,1536]{1,0:T(8,128)(2,1)} %get-tuple-element.172.qkv_ref) | copy-start | bytes 4718596
  81.3 4.3 %copy-start.13 = (bf16[512,512]{1,0:T(8,128)(2,1)S(1)}, bf16[512,512]{1,0:T(8,128)(2,1)}, u32[]{:S(2)}) copy-start(bf16[512,512]{1,0:T(8,128)(2,1)} %get-tuple-element.177.sorted_ref) | copy-start | bytes 1572868
  81.3 4.3 %copy-start.21 = (f32[16,256]{1,0:T(8,128)S(1)}, f32[16,256]{1,0:T(8,128)}, u32[]{:S(2)}) copy-start(f32[16,256]{1,0:T(8,128)} %get-tuple-element.173.norm_ref) | copy-start | bytes 49156
  81.3 13.8 %collective-permute-start.3 = (bf16[576,512]{1,0:T(8,128)(2,1)S(1)}, bf16[576,512]{1,0:T(8,128)(2,1)S(1)}, u32[]{:S(2)}, u32[]{:S(2)}) collective-permute-start(bf16[576,512]{1,0:T(8,128)(2,1)S(1)} %get-tuple-element.171), channel_id=1, source_target_pairs={{0,1},{1,0},{2,6},{3,7},{4,5},{5,4},{6,2},{7,3},{8,9},{9,8},{10,14... | collective-permute-start | bytes 1769480 | tf_op jit(solution)/shard_map/ppermute | solution.py:881
  85.1 17.5 %collective-permute-start.10 = (bf16[4,128,512]{2,1,0:T(8,128)(2,1)S(1)}, bf16[4,128,512]{2,1,0:T(8,128)(2,1)S(1)}, u32[]{:S(2)}, u32[]{:S(2)}) collective-permute-start(bf16[4,128,512]{2,1,0:T(8,128)(2,1)S(1)} %shard_map.237), channel_id=1, source_target_pairs={{0,1},{1,0},{2,3},{3,2},{4,5},{5,4},{6,7},{7,6},{8,9},{9,8},{10,11... | collective-permute-start | bytes 1572872 | tf_op jit(solution)/shard_map/ppermute | solution.py:1194
  95.1 5.6 %collective-permute-start.8 = (bf16[384,512]{1,0:T(8,128)(2,1)S(1)}, bf16[384,512]{1,0:T(8,128)(2,1)S(1)}, u32[]{:S(2)}, u32[]{:S(2)}) collective-permute-start(bf16[384,512]{1,0:T(8,128)(2,1)S(1)} %get-tuple-element.197), channel_id=1, source_target_pairs={{0,2},{1,3},{2,0},{3,1},{4,6},{5,7},{6,4},{7,5},{8,10},{9,11},{10,... | collective-permute-start | bytes 1179656 | tf_op jit(solution)/shard_map/ppermute | solution.py:881
  95.1 5.7 %collective-permute-start.9 = (bf16[384,512]{1,0:T(8,128)(2,1)S(1)}, bf16[384,512]{1,0:T(8,128)(2,1)S(1)}, u32[]{:S(2)}, u32[]{:S(2)}) collective-permute-start(bf16[384,512]{1,0:T(8,128)(2,1)S(1)} %get-tuple-element.199), channel_id=1, source_target_pairs={{0,2},{1,3},{2,0},{3,1},{4,6},{5,7},{6,4},{7,5},{8,10},{9,11},{10,... | collective-permute-start | bytes 1179656 | tf_op jit(solution)/shard_map/ppermute | solution.py:881
  96.3 8.5 %copy-start.10 = (bf16[512,1536]{1,0:T(8,128)(2,1)S(1)}, bf16[512,1536]{1,0:T(8,128)(2,1)}, u32[]{:S(2)}) copy-start(bf16[512,1536]{1,0:T(8,128)(2,1)} %w_qkv_ref.3) | copy-start | bytes 4718596
  96.3 14.3 %collective-permute-start.5 = (bf16[144,512]{1,0:T(8,128)(2,1)S(1)}, bf16[144,512]{1,0:T(8,128)(2,1)S(1)}, u32[]{:S(2)}, u32[]{:S(2)}) collective-permute-start(bf16[144,512]{1,0:T(8,128)(2,1)S(1)} %get-tuple-element.191), channel_id=1, source_target_pairs={{0,8},{1,9},{2,10},{3,11},{4,12},{5,13},{6,14},{7,15},{8,0},{9,1},... | collective-permute-start | bytes 442376 | tf_op jit(solution)/shard_map/ppermute | solution.py:881
  98.1 14.0 %collective-permute-start.6 = (bf16[144,512]{1,0:T(8,128)(2,1)S(1)}, bf16[144,512]{1,0:T(8,128)(2,1)S(1)}, u32[]{:S(2)}, u32[]{:S(2)}) collective-permute-start(bf16[144,512]{1,0:T(8,128)(2,1)S(1)} %get-tuple-element.192), channel_id=1, source_target_pairs={{0,16},{1,17},{2,18},{3,19},{4,20},{5,21},{6,22},{7,23},{8,24},{9,... | collective-permute-start | bytes 442376 | tf_op jit(solution)/shard_map/ppermute | solution.py:881
  100.7 11.4 %collective-permute-start.7 = (bf16[144,512]{1,0:T(8,128)(2,1)S(1)}, bf16[144,512]{1,0:T(8,128)(2,1)S(1)}, u32[]{:S(2)}, u32[]{:S(2)}) collective-permute-start(bf16[144,512]{1,0:T(8,128)(2,1)S(1)} %get-tuple-element.193), channel_id=1, source_target_pairs={{0,24},{1,25},{2,26},{3,27},{4,28},{5,29},{6,30},{7,31},{8,16},{9,... | collective-permute-start | bytes 442376 | tf_op jit(solution)/shard_map/ppermute | solution.py:881
  102.5 14.1 %collective-permute-start.11 = (bf16[912,512]{1,0:T(8,128)(2,1)S(1)}, bf16[912,512]{1,0:T(8,128)(2,1)S(1)}, u32[]{:S(2)}, u32[]{:S(2)}) collective-permute-start(bf16[912,512]{1,0:T(8,128)(2,1)S(1)} %get-tuple-element.212), channel_id=1, source_target_pairs={{0,4},{1,5},{2,3},{3,2},{4,0},{5,1},{6,7},{7,6},{8,12},{9,13},{10,... | collective-permute-start | bytes 2801672 | tf_op jit(solution)/shard_map/ppermute | solution.py:881
  112.2 8.4 %collective-permute-start.15 = (bf16[144,512]{1,0:T(8,128)(2,1)S(1)}, bf16[144,512]{1,0:T(8,128)(2,1)S(1)}, u32[]{:S(2)}, u32[]{:S(2)}) collective-permute-start(bf16[144,512]{1,0:T(8,128)(2,1)S(1)} %shard_map.244.refs_0_), channel_id=1, source_target_pairs={{0,24},{1,25},{2,26},{3,27},{4,28},{5,29},{6,30},{7,31},{8,16},{9,... | collective-permute-start | bytes 442376 | tf_op jit(solution)/shard_map/ppermute | solution.py:881
  114.6 12.4 %collective-permute-start.14 = (bf16[144,512]{1,0:T(8,128)(2,1)S(1)}, bf16[144,512]{1,0:T(8,128)(2,1)S(1)}, u32[]{:S(2)}, u32[]{:S(2)}) collective-permute-start(bf16[144,512]{1,0:T(8,128)(2,1)S(1)} %shard_map.244.refs_0_), channel_id=1, source_target_pairs={{0,16},{1,17},{2,18},{3,19},{4,20},{5,21},{6,22},{7,23},{8,24},{9,... | collective-permute-start | bytes 442376 | tf_op jit(solution)/shard_map/ppermute | solution.py:881
  116.2 10.8 %collective-permute-start.13 = (bf16[144,512]{1,0:T(8,128)(2,1)S(1)}, bf16[144,512]{1,0:T(8,128)(2,1)S(1)}, u32[]{:S(2)}, u32[]{:S(2)}) collective-permute-start(bf16[144,512]{1,0:T(8,128)(2,1)S(1)} %shard_map.244.refs_0_), channel_id=1, source_target_pairs={{0,8},{1,9},{2,10},{3,11},{4,12},{5,13},{6,14},{7,15},{8,0},{9,1},... | collective-permute-start | bytes 442376 | tf_op jit(solution)/shard_map/ppermute | solution.py:881
  117.4 12.3 %collective-permute-start.12 = (bf16[464,512]{1,0:T(8,128)(2,1)S(1)}, bf16[464,512]{1,0:T(8,128)(2,1)S(1)}, u32[]{:S(2)}, u32[]{:S(2)}) collective-permute-start(bf16[464,512]{1,0:T(8,128)(2,1)S(1)} %get-tuple-element.214), channel_id=1, source_target_pairs={{0,1},{1,0},{2,6},{3,7},{4,5},{5,4},{6,2},{7,3},{8,9},{9,8},{10,14... | collective-permute-start | bytes 1425416 | tf_op jit(solution)/shard_map/ppermute | solution.py:881
  127.6 16.3 %collective-permute-start.19 = (bf16[576,512]{1,0:T(8,128)(2,1)S(1)}, bf16[576,512]{1,0:T(8,128)(2,1)S(1)}, u32[]{:S(2)}, u32[]{:S(2)}) collective-permute-start(bf16[576,512]{1,0:T(8,128)(2,1)S(1)} %shard_map.245.refs_0_), channel_id=1, source_target_pairs={{0,1},{1,0},{2,6},{3,7},{4,5},{5,4},{6,2},{7,3},{8,9},{9,8},{10,14... | collective-permute-start | bytes 1769480 | tf_op jit(solution)/shard_map/ppermute | solution.py:881
  129.5 25.6 %collective-permute-start.23 = (bf16[4,128,512]{2,1,0:T(8,128)(2,1)S(1)}, bf16[4,128,512]{2,1,0:T(8,128)(2,1)S(1)}, u32[]{:S(2)}, u32[]{:S(2)}) collective-permute-start(bf16[4,128,512]{2,1,0:T(8,128)(2,1)S(1)} %get-tuple-element.232), channel_id=1, source_target_pairs={{0,1},{1,0},{2,3},{3,2},{4,5},{5,4},{6,7},{7,6},{8,9},{9,8},{10,11... | collective-permute-start | bytes 1572872 | tf_op jit(solution)/shard_map/ppermute | solution.py:1194
  130.4 15.0 %collective-permute-start.16 = (bf16[128,512]{1,0:T(8,128)(2,1)S(1)}, bf16[128,512]{1,0:T(8,128)(2,1)S(1)}, u32[]{:S(2)}, u32[]{:S(2)}) collective-permute-start(bf16[128,512]{1,0:T(8,128)(2,1)S(1)} %get-tuple-element.222), channel_id=1, source_target_pairs={{0,8},{1,9},{2,10},{3,11},{4,12},{5,13},{6,14},{7,15},{8,0},{9,1},... | collective-permute-start | bytes 393224 | tf_op jit(solution)/shard_map/ppermute | solution.py:881
  130.6 14.8 %collective-permute-start.17 = (bf16[128,512]{1,0:T(8,128)(2,1)S(1)}, bf16[128,512]{1,0:T(8,128)(2,1)S(1)}, u32[]{:S(2)}, u32[]{:S(2)}) collective-permute-start(bf16[128,512]{1,0:T(8,128)(2,1)S(1)} %get-tuple-element.223), channel_id=1, source_target_pairs={{0,16},{1,17},{2,18},{3,19},{4,20},{5,21},{6,22},{7,23},{8,24},{9,... | collective-permute-start | bytes 393224 | tf_op jit(solution)/shard_map/ppermute | solution.py:881
  134.0 11.5 %collective-permute-start.18 = (bf16[128,512]{1,0:T(8,128)(2,1)S(1)}, bf16[128,512]{1,0:T(8,128)(2,1)S(1)}, u32[]{:S(2)}, u32[]{:S(2)}) collective-permute-start(bf16[128,512]{1,0:T(8,128)(2,1)S(1)} %get-tuple-element.224), channel_id=1, source_target_pairs={{0,24},{1,25},{2,26},{3,27},{4,28},{5,29},{6,30},{7,31},{8,16},{9,... | collective-permute-start | bytes 393224 | tf_op jit(solution)/shard_map/ppermute | solution.py:881
  144.5 21.6 %collective-permute-start.24 = (bf16[1152,512]{1,0:T(8,128)(2,1)S(1)}, bf16[1152,512]{1,0:T(8,128)(2,1)S(1)}, u32[]{:S(2)}, u32[]{:S(2)}) collective-permute-start(bf16[1152,512]{1,0:T(8,128)(2,1)S(1)} %shard_map.247.refs_0_), channel_id=1, source_target_pairs={{0,4},{1,5},{2,3},{3,2},{4,0},{5,1},{6,7},{7,6},{8,12},{9,13},{10,... | collective-permute-start | bytes 3538952 | tf_op jit(solution)/shard_map/ppermute | solution.py:881
  146.1 9.1 %collective-permute-start.22 = (bf16[112,512]{1,0:T(8,128)(2,1)S(1)}, bf16[112,512]{1,0:T(8,128)(2,1)S(1)}, u32[]{:S(2)}, u32[]{:S(2)}) collective-permute-start(bf16[112,512]{1,0:T(8,128)(2,1)S(1)} %get-tuple-element.235.refs_0_), channel_id=1, source_target_pairs={{0,24},{1,25},{2,26},{3,27},{4,28},{5,29},{6,30},{7,31},{8,16},{9,... | collective-permute-start | bytes 344072 | tf_op jit(solution)/shard_map/ppermute | solution.py:881
  150.1 6.3 %collective-permute-start.21 = (bf16[112,512]{1,0:T(8,128)(2,1)S(1)}, bf16[112,512]{1,0:T(8,128)(2,1)S(1)}, u32[]{:S(2)}, u32[]{:S(2)}) collective-permute-start(bf16[112,512]{1,0:T(8,128)(2,1)S(1)} %get-tuple-element.235.refs_0_), channel_id=1, source_target_pairs={{0,16},{1,17},{2,18},{3,19},{4,20},{5,21},{6,22},{7,23},{8,24},{9,... | collective-permute-start | bytes 344072 | tf_op jit(solution)/shard_map/ppermute | solution.py:881
  150.1 6.3 %collective-permute-start.20 = (bf16[112,512]{1,0:T(8,128)(2,1)S(1)}, bf16[112,512]{1,0:T(8,128)(2,1)S(1)}, u32[]{:S(2)}, u32[]{:S(2)}) collective-permute-start(bf16[112,512]{1,0:T(8,128)(2,1)S(1)} %get-tuple-element.235.refs_0_), channel_id=1, source_target_pairs={{0,8},{1,9},{2,10},{3,11},{4,12},{5,13},{6,14},{7,15},{8,0},{9,1},... | collective-permute-start | bytes 344072 | tf_op jit(solution)/shard_map/ppermute | solution.py:881
  157.0 8.5 %collective-permute-start.25 = (bf16[448,512]{1,0:T(8,128)(2,1)S(1)}, bf16[448,512]{1,0:T(8,128)(2,1)S(1)}, u32[]{:S(2)}, u32[]{:S(2)}) collective-permute-start(bf16[448,512]{1,0:T(8,128)(2,1)S(1)} %shard_map.249.refs_0_), channel_id=1, source_target_pairs={{0,1},{1,0},{2,6},{3,7},{4,5},{5,4},{6,2},{7,3},{8,9},{9,8},{10,14... | collective-permute-start | bytes 1376264 | tf_op jit(solution)/shard_map/ppermute | solution.py:881
  166.1 2.9 %collective-permute-start.27 = (bf16[1152,512]{1,0:T(8,128)(2,1)S(1)}, bf16[1152,512]{1,0:T(8,128)(2,1)S(1)}, u32[]{:S(2)}, u32[]{:S(2)}) collective-permute-start(bf16[1152,512]{1,0:T(8,128)(2,1)S(1)} %shard_map.247.refs_0_), channel_id=1, source_target_pairs={{0,2},{1,3},{2,0},{3,1},{4,6},{5,7},{6,4},{7,5},{8,10},{9,11},{10,... | collective-permute-start | bytes 3538952 | tf_op jit(solution)/shard_map/ppermute | solution.py:881
  166.2 4.5 %collective-permute-start.28 = (bf16[1152,512]{1,0:T(8,128)(2,1)S(1)}, bf16[1152,512]{1,0:T(8,128)(2,1)S(1)}, u32[]{:S(2)}, u32[]{:S(2)}) collective-permute-start(bf16[1152,512]{1,0:T(8,128)(2,1)S(1)} %collective-permute-done.24.refs_2_), channel_id=1, source_target_pairs={{0,2},{1,3},{2,0},{3,1},{4,6},{5,7},{6,4},{7,5},{8,10},{9,11},{10,... | collective-permute-start | bytes 3538952 | tf_op jit(solution)/shard_map/ppermute | solution.py:881
  166.7 8.7 %collective-permute-start.29 = (bf16[896,512]{1,0:T(8,128)(2,1)S(1)}, bf16[896,512]{1,0:T(8,128)(2,1)S(1)}, u32[]{:S(2)}, u32[]{:S(2)}) collective-permute-start(bf16[896,512]{1,0:T(8,128)(2,1)S(1)} %shard_map.250.refs_0_), channel_id=1, source_target_pairs={{0,2},{1,3},{2,0},{3,1},{4,6},{5,7},{6,4},{7,5},{8,10},{9,11},{10,... | collective-permute-start | bytes 2752520 | tf_op jit(solution)/shard_map/ppermute | solution.py:881
  166.8 13.4 %collective-permute-start.26 = (bf16[896,512]{1,0:T(8,128)(2,1)S(1)}, bf16[896,512]{1,0:T(8,128)(2,1)S(1)}, u32[]{:S(2)}, u32[]{:S(2)}) collective-permute-start(bf16[896,512]{1,0:T(8,128)(2,1)S(1)} %shard_map.250.refs_0_), channel_id=1, source_target_pairs={{0,4},{1,5},{2,3},{3,2},{4,0},{5,1},{6,7},{7,6},{8,12},{9,13},{10,... | collective-permute-start | bytes 2752520 | tf_op jit(solution)/shard_map/ppermute | solution.py:881
  180.2 2.5 %collective-permute-start.30 = (bf16[896,512]{1,0:T(8,128)(2,1)S(1)}, bf16[896,512]{1,0:T(8,128)(2,1)S(1)}, u32[]{:S(2)}, u32[]{:S(2)}) collective-permute-start(bf16[896,512]{1,0:T(8,128)(2,1)S(1)} %collective-permute-done.26.refs_0_), channel_id=1, source_target_pairs={{0,2},{1,3},{2,0},{3,1},{4,6},{5,7},{6,4},{7,5},{8,10},{9,11},{10,... | collective-permute-start | bytes 2752520 | tf_op jit(solution)/shard_map/ppermute | solution.py:881
  181.3 4.0 %copy-start.27 = (bf16[8,256,512]{2,1,0:T(8,128)(2,1)}, bf16[8,256,512]{2,1,0:T(8,128)(2,1)S(1)}, u32[]{:S(2)}) copy-start(bf16[8,256,512]{2,1,0:T(8,128)(2,1)S(1)} %constant_dynamic-update-slice_fusion) | copy-start | bytes 6291460
  (13 other events, 33.9 us)
